TPU v7x, 512 devices: a whole 4x8x8 slice. The times are simulated.
512 devices in a mesh: row: 16 (over y, core), col: 32 (over z, x).
Axes of the slice: x: 4, y: 8, z: 8, core: 2. Of those that a mesh axis runs over, the one named last changes fastest.
Arguments:
- matrix: float32 [4, 16, 256, 2, 32, 256], P(None, 'row', None, None, 'col'), may hold values from -1.1 to 65.1, as said below
- precision: int32 [4, 16, 2, 32], P(None, 'row', None, 'col'), may hold values from 0 to 2, as said below
- first_col: int32 [1], replicated, may hold values from 0 to 46
Outputs:
- factored: float32 [4, 16, 256, 2, 32, 256], P(None, 'row', None, None, 'col')
Inputs may be any that keep to these rules, and one draw needn't show every extreme that they name: `precision`: 2 marks a float32 tile, 1 a bfloat16 tile, 0 a dropped tile. Every diagonal tile is 2 and every tile above the diagonal is 0; down each tile column from the diagonal the values never rise. `matrix`: diagonal tiles are symmetric and positive definite; tiles above the diagonal are not read.
All inputs are finite; a program needn't handle non-finite values.
Results may differ from a plain program's by a relative error of at most 0.0003.
Values sent between devices are 32-bit elements; how exact they have to be, the bound alone decides.
No kernel may reach another device: no remote copies, remote signals or barrier semaphores. Data moves between devices by JAX's collectives and lax.ppermute only.
A program may use at most 64 MiB of HBM per device.

v0:
```python
import jax
import jax.numpy as jnp
from jax import lax
from jax.sharding import PartitionSpec as P


def spread(value, axis, source):
    kept = jnp.where(lax.axis_index(axis) == source, value, 0).astype(value.dtype)
    return lax.psum(kept, axis)


def to_bfloat(values):
    narrow = lax.optimization_barrier(values.astype(jnp.bfloat16))
    return narrow.astype(jnp.float32)


def by_level(values, levels):
    shaped = levels.reshape(levels.shape + (1, 1))
    return jnp.where(shaped == 2, values, jnp.where(shaped == 1, to_bfloat(values), 0.0))


def solve_rows(factor, panel_in):
    pick_count = panel_in.shape[0]
    tile_width = panel_in.shape[1]
    stacked = panel_in.reshape(pick_count * tile_width, tile_width)
    solved = jax.scipy.linalg.solve_triangular(factor, stacked.T, lower=True)
    return solved.T.reshape(pick_count, tile_width, tile_width)


def per_device(matrix, precision, first_col):
    row_count = lax.axis_size("row")
    col_count = lax.axis_size("col")
    row_at = lax.axis_index("row")
    col_at = lax.axis_index("col")
    rtiles = matrix.shape[0]
    tile_width = matrix.shape[2]
    ctiles = matrix.shape[3]
    levels = precision.reshape(rtiles, ctiles)
    blocks = by_level(
        matrix.reshape(rtiles, tile_width, ctiles, tile_width).transpose(0, 2, 1, 3), levels
    )
    row_ids = jnp.arange(rtiles, dtype=jnp.int32) * row_count + row_at
    col_ids = jnp.arange(ctiles, dtype=jnp.int32) * col_count + col_at
    pick_rows = col_ids // row_count
    identity = jnp.eye(tile_width, dtype=jnp.float32)
    contract = (((1,), (1,)), ((), ()))
    zero_at = jnp.zeros((), jnp.int32)

    def factor_panel(blocks, column):
        local_row = column // row_count
        local_col = column // col_count
        owner_row = column % row_count
        owner_col = column % col_count
        in_column = col_at == owner_col
        own_tile = lax.dynamic_slice(
            blocks, (local_row, local_col, zero_at, zero_at), (1, 1, tile_width, tile_width)
        )[0, 0]
        panel_in = lax.dynamic_slice(
            blocks, (zero_at, local_col, zero_at, zero_at), (rtiles, 1, tile_width, tile_width)
        )[:, 0]
        column_levels = lax.dynamic_slice(levels, (zero_at, local_col), (rtiles, 1))[:, 0]
        below_mask = (row_ids > column).reshape(rtiles, 1, 1)
        received = spread(own_tile, "row", owner_row)
        factor = jnp.linalg.cholesky(jnp.where(in_column, received, identity))
        local_lower = jnp.where(
            below_mask, by_level(solve_rows(factor, panel_in), column_levels), 0.0
        )
        lower_rows = spread(local_lower, "col", owner_col)
        on_diag = (row_ids == column).reshape(rtiles, 1, 1)
        new_column = jnp.where(below_mask, lower_rows, jnp.where(on_diag, factor, panel_in))
        placed = lax.dynamic_update_slice(
            blocks, new_column[:, None], (zero_at, local_col, zero_at, zero_at)
        )
        blocks = jnp.where(in_column, placed, blocks)
        picked = jnp.take(lower_rows, pick_rows, axis=0)
        lower_cols = spread(picked, "row", col_at % row_count)
        return (blocks, lower_rows, lower_cols)

    def update(blocks, lower_rows, lower_cols, column, picks):
        pick_count = picks.shape[0]
        rows_flat = jnp.repeat(jnp.arange(rtiles, dtype=jnp.int32), pick_count)
        cols_flat = jnp.tile(picks, rtiles)

        def keep_tile(one_block, left_tile, right_tile):
            return one_block

        def narrow(one_block, left_tile, right_tile):
            product = lax.dot_general(
                left_tile.astype(jnp.bfloat16),
                right_tile.astype(jnp.bfloat16),
                contract,
                preferred_element_type=jnp.float32,
            )
            return to_bfloat(one_block - product)

        def precise(one_block, left_tile, right_tile):
            product = lax.dot_general(
                left_tile,
                right_tile,
                contract,
                precision=lax.Precision.HIGHEST,
                preferred_element_type=jnp.float32,
            )
            return one_block - product

        def one_tile(pair_item):
            row_pos, col_pos = pair_item
            active = (row_ids[row_pos] >= col_ids[col_pos]) & (col_ids[col_pos] > column)
            branch_at = jnp.where(active, levels[row_pos, col_pos], 0)
            return lax.switch(
                branch_at,
                (keep_tile, narrow, precise),
                blocks[row_pos, col_pos],
                lower_rows[row_pos],
                lower_cols[col_pos],
            )

        results = lax.map(one_tile, (rows_flat, cols_flat))
        return blocks.at[rows_flat, cols_flat].set(results)

    start_col = first_col[0]
    all_cols = jnp.arange(ctiles, dtype=jnp.int32)
    blocks, lower_rows, lower_cols = factor_panel(blocks, start_col)
    blocks = update(blocks, lower_rows, lower_cols, start_col, all_cols)
    blocks, next_rows, next_cols = factor_panel(blocks, start_col + 1)
    blocks = update(blocks, next_rows, next_cols, start_col + 1, all_cols)
    return blocks.transpose(0, 2, 1, 3).reshape(matrix.shape)


def solution(mesh):
    in_specs = (P(None, "row", None, None, "col", None), P(None, "row", None, "col"), P())
    out_specs = P(None, "row", None, None, "col", None)
    return jax.shard_map(
        per_device, mesh=mesh, in_specs=in_specs, out_specs=out_specs, check_vma=False
    )
```

profile of v0, /device:TPU:1, one launch (start us, length us, event | category | flops | bytes accessed | tf_op | source)
XLA Modules:
  0.0 1155.8 jit_solution(14233637071442762164)
XLA Ops:
  8.1 4.6 copy.21
  18.6 117.0 %all-reduce.8.cloned.1.call-done = f32[256,256]{0,1:T(8,128)} async-done(((f32[256,256]{0,1:T(8,128)}), f32[256,256]{0,1:T(8,128)}) %all-reduce.8.cloned.1.call-update) | async-done | bytes 262160 | tf_op jit(solution)/shard_map/psum | solution.py:9
  135.9 11.7 %cholesky.130 = f32[128,128]{1,0:T(8,128)S(1)} custom-call(f32[128,128]{1,0:T(8,128)S(1)} %cholesky.194), custom_call_target="Cholesky" | custom-call | tf_op jit(solution)/shard_map/jit(cholesky)/cholesky | solution.py:64
  147.6 9.8 custom-call.17
  157.9 11.7 %cholesky.147 = f32[128,128]{1,0:T(8,128)S(1)} custom-call(f32[128,128]{1,0:T(8,128)S(1)} %convolution_subtract_fusion.7), custom_call_target="Cholesky" | custom-call | tf_op jit(solution)/shard_map/jit(cholesky)/cholesky | solution.py:64
  171.9 4.2 while.26
  176.1 19.7 %custom-call.18 = f32[2,128,128]{1,2,0:T(8,128)S(1)} custom-call(f32[2,128,128]{2,1,0:T(8,128)S(1)} %get-tuple-element.338), custom_call_target="InvertDiagBlocksLowerTriangular" | custom-call | tf_op jit(solution)/shard_map/jit(_solve_triangular)/triangular_solve | solution.py:26
  201.4 156.2 %all-reduce.10.cloned.1.call-done = f32[4,256,256]{1,2,0:T(8,128)} async-done(((f32[4,256,256]{1,2,0:T(8,128)}), f32[4,256,256]{1,2,0:T(8,128)}) %all-reduce.10.cloned.1.call-update) | async-done | bytes 1048592 | tf_op jit(solution)/shard_map/psum | solution.py:9
  364.9 112.1 %all-reduce.12.cloned.1.call-done = f32[2,256,256]{1,2,0:T(8,128)} async-done(((f32[2,256,256]{1,2,0:T(8,128)}), f32[2,256,256]{1,2,0:T(8,128)}) %all-reduce.12.cloned.1.call-update) | async-done | bytes 524304 | tf_op jit(solution)/shard_map/psum | solution.py:9
  479.8 91.9 %while.24 = (s32[]{:T(128)}, f32[8,256,256]{2,1,0:T(8,128)}, s32[8]{0:T(128)S(1)}, s32[4]{0:T(128)S(1)}, s32[8]{0:T(128)S(1)}, /*index=5*/s32[2]{0:T(128)S(1)}, ...) while((s32[]{:T(128)}, f32[8,256,256]{2,1,0:T(8,128)}, ...), condition=%wide.region_11.15_spmd, body=%wide.region_7.14_spmd.sunk | while | flops 201392144 | bytes 2099063 | solution.py:118
  575.5 116.9 %all-reduce.14.cloned.1.call-done = f32[256,256]{0,1:T(8,128)} async-done(((f32[256,256]{0,1:T(8,128)}), f32[256,256]{0,1:T(8,128)}) %all-reduce.14.cloned.1.call-update) | async-done | bytes 262160 | tf_op jit(solution)/shard_map/psum | solution.py:9
  695.0 11.7 %cholesky.164 = f32[128,128]{1,0:T(8,128)S(1)} custom-call(f32[128,128]{1,0:T(8,128)S(1)} %cholesky.197), custom_call_target="Cholesky" | custom-call | tf_op jit(solution)/shard_map/jit(cholesky)/cholesky | solution.py:64
  707.4 9.8 custom-call.19
  719.3 11.7 %cholesky.181 = f32[128,128]{1,0:T(8,128)S(1)} custom-call(f32[128,128]{1,0:T(8,128)S(1)} %convolution_subtract_fusion.6), custom_call_target="Cholesky" | custom-call | tf_op jit(solution)/shard_map/jit(cholesky)/cholesky | solution.py:64
  736.2 5.7 while.27
  742.6 20.5 %custom-call.20 = f32[2,128,128]{1,2,0:T(8,128)S(1)} custom-call(f32[2,128,128]{2,1,0:T(8,128)} %copy-done.7), custom_call_target="InvertDiagBlocksLowerTriangular" | custom-call | tf_op jit(solution)/shard_map/jit(_solve_triangular)/triangular_solve | solution.py:26
  766.4 2.5 copy.37
  769.0 2.5 copy.39
  776.5 155.2 %all-reduce.16.cloned.1.call-done = f32[4,256,256]{1,2,0:T(8,128)} async-done(((f32[4,256,256]{1,2,0:T(8,128)}), f32[4,256,256]{1,2,0:T(8,128)}) %all-reduce.16.cloned.1.call-update) | async-done | bytes 1048592 | tf_op jit(solution)/shard_map/psum | solution.py:9
  931.7 2.7 gather_fusion.1
  938.8 2.6 copy.41
  944.0 109.0 %all-reduce.18.cloned.1.call-done = f32[2,256,256]{1,2,0:T(8,128)} async-done(((f32[2,256,256]{1,2,0:T(8,128)}), f32[2,256,256]{1,2,0:T(8,128)}) %all-reduce.18.cloned.1.call-update) | async-done | bytes 524304 | tf_op jit(solution)/shard_map/psum | solution.py:9
  1055.8 86.8 %while.25 = (s32[]{:T(128)}, f32[8,256,256]{2,1,0:T(8,128)}, s32[8]{0:T(128)S(1)}, s32[4]{0:T(128)S(1)}, s32[8]{0:T(128)S(1)}, /*index=5*/s32[2]{0:T(128)S(1)}, ...) while((s32[]{:T(128)}, f32[8,256,256]{2,1,0:T(8,128)}, ...), condition=%wide.region_20.24_spmd, body=%wide.region_16.23_spmd.sunk | while | flops 201392144 | bytes 2099063 | solution.py:118
  1145.0 3.5 copy.44
  (292 shorter events, 140.4 us)
Async XLA Ops:
  6.5 129.1 %all-reduce.8.cloned.1.call-start = ((), (), s32[]{:S(2)}) async-start(), calls=%async_computation | async-start | bytes 524288 | tf_op jit(solution)/shard_map/psum | solution.py:9
  16.2 341.4 %all-reduce.10.cloned.1.call-start = ((), (), s32[]{:S(2)}) async-start(), calls=%async_computation.1 | async-start | bytes 2097152 | tf_op jit(solution)/shard_map/psum | solution.py:9
  16.3 1.7 copy-start.8
  176.1 22.1 %copy-start.16 = (s32[2,2]{1,0:T(2,128)}, s32[2,2]{1,0:T(2,128)S(1)}, u32[]{:S(2)}) copy-start(s32[2,2]{1,0:T(2,128)S(1)} %get-tuple-element.835) | copy-start | bytes 52
  200.2 276.9 %all-reduce.12.cloned.1.call-start = ((), (), s32[]{:S(2)}) async-start(), calls=%async_computation.2 | async-start | bytes 1048576 | tf_op jit(solution)/shard_map/psum | solution.py:9
  357.6 2.9 copy-start.1
  360.4 332.0 %all-reduce.14.cloned.1.call-start = ((), (), s32[]{:S(2)}) async-start(), calls=%async_computation.3 | async-start | bytes 524288 | tf_op jit(solution)/shard_map/psum | solution.py:9
  571.7 2.5 copy-start.12
  571.7 2.5 copy-start.14
  571.7 2.6 copy-start.17
  571.7 2.6 copy-start.19
  575.2 356.5 %all-reduce.16.cloned.1.call-start = ((), (), s32[]{:S(2)}) async-start(), calls=%async_computation.4 | async-start | bytes 2097152 | tf_op jit(solution)/shard_map/psum | solution.py:9
  731.1 3.4 copy-start.3
  769.0 3.9 copy-start.9
  769.0 3.9 copy-start.10
  769.0 3.9 copy-start.11
  771.5 1.5 copy-start
  774.3 278.7 %all-reduce.18.cloned.1.call-start = ((), (), s32[]{:S(2)}) async-start(), calls=%async_computation.5 | async-start | bytes 1048576 | tf_op jit(solution)/shard_map/psum | solution.py:9
  776.5 159.8 %copy-start.5 = (f32[256,256]{0,1:T(8,128)S(1)}, f32[256,256]{0,1:T(8,128)}, u32[]{:S(2)}) copy-start(f32[256,256]{0,1:T(8,128)} %copy.40) | copy-start | bytes 786436
  931.7 4.7 copy-start.2
  944.0 111.8 %copy-start.13 = (s32[8]{0:T(128)S(1)}, s32[8]{0:T(128)}, u32[]{:S(2)}) copy-start(s32[8]{0:T(128)} %copy-done.12) | copy-start | bytes 100
  944.0 111.7 %copy-start.15 = (s32[8]{0:T(128)S(1)}, s32[8]{0:T(128)}, u32[]{:S(2)}) copy-start(s32[8]{0:T(128)} %copy-done.14) | copy-start | bytes 100
  944.0 111.7 %copy-start.18 = (s32[4]{0:T(128)S(1)}, s32[4]{0:T(128)}, u32[]{:S(2)}) copy-start(s32[4]{0:T(128)} %copy-done.17) | copy-start | bytes 52
  944.0 111.7 %copy-start.20 = (s32[2]{0:T(128)S(1)}, s32[2]{0:T(128)}, u32[]{:S(2)}) copy-start(s32[2]{0:T(128)} %copy-done.19) | copy-start | bytes 28
  (3 other events, 2.8 us)
Sparse Core Ops, SparseCore 0:
  16.3 119.2 all-reduce.7
  200.3 157.1 all-reduce.9
  360.5 116.4 all-reduce.11
  575.3 117.0 all-reduce.13
  774.4 157.2 all-reduce.15
  936.5 116.4 all-reduce.17
where the time goes:
time: 1170 us; the launch traced here: 1160 us
  waiting for transfers between devices  766 us (65%)
  other arithmetic  131 us (11%)
  local copies, waits for them, and re-layouts  117 us (10%)
  loops' own time  111 us (9%)
  between operations  18 us (2%)
  matrix products  11.9 us (1%)
    psum x6, waiting for transfers between devices, spread(): return lax.psum(kept, axis)  766 us
    another operation x2, loops' own time, update(): results = lax.map(one_tile, (rows_flat, cols_flat))  110 us
    another operation x13, other arithmetic, factor_panel(): factor = jnp.linalg.cholesky(jnp.where(in_column, received, identity))  70 us
    another operation x5, other arithmetic, solve_rows(): solved = jax.scipy.linalg.solve_triangular(factor, stacked.T, lower=True)  41.9 us
  transfers between devices with their start and end apart: 6, of which 6 were waited for; matrix products, arithmetic and copies ran while one was open for 2% of the time, Pallas kernels for 0%

commit v1 on v0

v1 whole, which is shorter than its diff:
```python
import jax
import jax.numpy as jnp
from jax import lax
from jax.experimental import pallas as pl
from jax.experimental.pallas import tpu as pltpu
from jax.sharding import PartitionSpec as P

HIGHEST = lax.Precision.HIGHEST
f32 = jnp.float32
N_ROW = 16
N_COL = 32
B = 256
HALF = 128
SMEM = pl.BlockSpec(memory_space=pltpu.SMEM)
VMEM = pl.BlockSpec(memory_space=pltpu.VMEM)


def dot_nt(a, b):
    return lax.dot_general(
        a, b, (((1,), (1,)), ((), ())), precision=HIGHEST, preferred_element_type=f32
    )


def dot_nn(a, b):
    return lax.dot_general(
        a, b, (((1,), (0,)), ((), ())), precision=HIGHEST, preferred_element_type=f32
    )


def dot_narrow(a, b):
    return lax.dot_general(
        a.astype(jnp.bfloat16),
        b.astype(jnp.bfloat16),
        (((1,), (1,)), ((), ())),
        preferred_element_type=f32,
    )


def rounded(x):
    return x.astype(jnp.bfloat16).astype(f32)


def by_level(x, level):
    return jnp.where(level == 2, x, jnp.where(level == 1, rounded(x), 0.0))


def pack_kernel(scal, prec, mat_ref, out_ref):
    k, q = scal[0], scal[2]
    col = jnp.where(q == k % N_COL, k // N_COL, (k + 1) // N_COL)
    sub = lax.broadcasted_iota(jnp.int32, (8, HALF), 0)
    levels = jnp.zeros((8, HALF), f32)
    for r in range(4):
        level = prec[r, col]
        levels = jnp.where(sub % 4 == r, level.astype(f32), levels)
        for h in range(2):
            rows = mat_ref[pl.ds(r * 1024 + col * 2 + h, B, stride=4), :]
            out_ref[:, r * 2 + h] = by_level(rows, level).reshape(32, 8, HALF)
    out_ref[:, 8] = jnp.broadcast_to(levels[None], (32, 8, HALF))


def pack(scal, prec, mat):
    return pl.pallas_call(
        pack_kernel,
        in_specs=[SMEM, SMEM, VMEM],
        out_specs=VMEM,
        out_shape=jax.ShapeDtypeStruct((N_COL, 9, 8, HALF), f32),
        compiler_params=pltpu.CompilerParams(vmem_limit_bytes=32 << 20),
    )(scal, prec, mat)


def route_kernel(scal, first_ref, second_ref, bulk_ref, even_ref, odd_ref, diag_ref):
    k, p, q = scal[0], scal[1], scal[2]
    low = q < N_ROW
    sub = lax.broadcasted_iota(jnp.int32, (8, HALF), 0)
    for t, ref in enumerate((first_ref, second_ref)):
        for r in range(4):
            for h in range(2):
                bulk_ref[t, r, h] = ref[0, 2 * r + h]
        for c in range(2):
            for h in range(2):
                even = ref[0, 4 * c + h]
                odd = ref[0, 4 * c + 2 + h]
                even_ref[t, c, h] = jnp.where(low, even, odd)
                odd_ref[t, c, h] = jnp.where(low, odd, even)
    next_r = (k + 1) // N_ROW
    here_r = jnp.where(p == k % N_ROW, k // N_ROW, next_r)
    for h in range(2):
        diag_ref[h] = first_ref[0, 2 * here_r + h]
        diag_ref[2 + h] = second_ref[0, 2 * next_r + h]
    diag_ref[4] = jnp.where(sub < 4, first_ref[0, 8], second_ref[0, 8])


def route(scal, received):
    block = (1, 9, 8, HALF)
    return pl.pallas_call(
        route_kernel,
        grid_spec=pltpu.PrefetchScalarGridSpec(
            num_scalar_prefetch=1,
            grid=(1,),
            in_specs=[
                pl.BlockSpec(block, lambda _, s: (s[0] % N_COL, 0, 0, 0)),
                pl.BlockSpec(block, lambda _, s: ((s[0] + 1) % N_COL, 0, 0, 0)),
            ],
            out_specs=[VMEM, VMEM, VMEM, VMEM],
        ),
        out_shape=[
            jax.ShapeDtypeStruct((2, 4, 2, 8, HALF), f32),
            jax.ShapeDtypeStruct((2, 2, 2, 8, HALF), f32),
            jax.ShapeDtypeStruct((2, 2, 2, 8, HALF), f32),
            jax.ShapeDtypeStruct((5, 8, HALF), f32),
        ],
    )(scal, received, received)


def factor_half(block):
    groups = HALF // 8
    sub = lax.broadcasted_iota(jnp.int32, (8, HALF), 0)
    lane = lax.broadcasted_iota(jnp.int32, (8, HALF), 1)
    up = [block[8 * g : 8 * g + 8, :] for g in range(groups)]
    inv = [jnp.where(lane == sub + 8 * g, 1.0, 0.0).astype(f32) for g in range(groups)]
    upper, lower_inv = [], []

    def row(x, j):
        return jnp.broadcast_to(x[j : j + 1, :], (8, HALF))

    def column(x, c):
        return jnp.broadcast_to(x[:, c : c + 1], (8, HALF))

    for b in range(groups):
        rows, irows = up[b], inv[b]
        cols = [column(rows, 8 * b + j) for j in range(8)]
        diag = jnp.zeros((8, HALF), f32)
        for j in range(8):
            pivot = row(cols[j], j)
            recip = 1.0 / pivot
            diag = jnp.where(sub == j, pivot, diag)
            if j < 7:
                mult = jnp.where(sub > j, cols[j] * recip, 0.0)
                for l in range(j + 1, 8):
                    cols[l] = cols[l] - mult * row(cols[l], j)
                rows = rows - mult * row(rows, j)
                irows = irows - mult * row(irows, j)
        scale = lax.rsqrt(diag)
        rows = rows * scale
        irows = irows * scale
        upper.append(jnp.where(lane >= sub + 8 * b, rows, 0.0))
        lower_inv.append(irows)
        if b + 1 < groups:
            row_each = [row(rows, j) for j in range(8)]
            irow_each = [row(irows, j) for j in range(8)]
            flipped = rows.T
            for g in range(b + 1, groups):
                part = flipped[8 * g : 8 * g + 8, :]
                for j in range(8):
                    m = column(part, j)
                    up[g] = up[g] - m * row_each[j]
                    inv[g] = inv[g] - m * irow_each[j]
    return jnp.concatenate(upper, 0), jnp.concatenate(lower_inv, 0)


def factor_kernel(scal, lev, d_ref, l_ref, li_ref, p_ref, s_ref, u_ref, v_ref):
    k = scal[0]

    def tile(n):
        return jnp.concatenate([d_ref[:, 2 * n + h].reshape(B, HALF) for h in range(2)], axis=1)

    s_ref[...] = tile(0)

    def step(t, _):
        def half(h, _):
            at = pl.ds(pl.multiple_of(h * HALF, HALF), HALF)
            u, v = factor_half(s_ref[at, at])
            u_ref[h] = u
            v_ref[h] = v

            @pl.when(h == 0)
            def _():
                l21 = dot_nt(s_ref[HALF:, 0:HALF], v)
                s_ref[HALF:, 0:HALF] = l21
                s_ref[HALF:, HALF:] = s_ref[HALF:, HALF:] - dot_nt(l21, l21)

            return 0

        lax.fori_loop(0, 2, half, 0)
        l21 = s_ref[HALF:, 0:HALF]
        zero = jnp.zeros((HALF, HALF), f32)
        v0, v1 = v_ref[0], v_ref[1]
        l_ref[t, 0:HALF, 0:HALF] = u_ref[0].T
        l_ref[t, 0:HALF, HALF:] = zero
        l_ref[t, HALF:, 0:HALF] = l21
        l_ref[t, HALF:, HALF:] = u_ref[1].T
        li_ref[t, 0:HALF, 0:HALF] = v0
        li_ref[t, 0:HALF, HALF:] = zero
        li_ref[t, HALF:, 0:HALF] = -dot_nn(v1, dot_nn(l21, v0))
        li_ref[t, HALF:, HALF:] = v1

        @pl.when(t == 0)
        def _():
            below = k + 1
            solved = by_level(dot_nt(tile(1), li_ref[0]), lev[below % N_ROW, below // N_ROW])
            p_ref[...] = solved
            s_ref[...] = tile(2) - dot_nt(solved, solved)

        return 0

    lax.fori_loop(0, 2, step, 0)


def factor_two(scal, lev, diag):
    pair = jax.ShapeDtypeStruct((2, B, B), f32)
    return pl.pallas_call(
        factor_kernel,
        in_specs=[SMEM, SMEM, VMEM],
        out_specs=[VMEM] * 3,
        out_shape=[pair, pair, jax.ShapeDtypeStruct((B, B), f32)],
        scratch_shapes=[
            pltpu.VMEM((B, B), f32),
            pltpu.VMEM((2, HALF, HALF), f32),
            pltpu.VMEM((2, HALF, HALF), f32),
        ],
        compiler_params=pltpu.CompilerParams(vmem_limit_bytes=32 << 20),
    )(scal, lev, diag)


def update_kernel(
    scal, lev, prec, rows_ref, cols_ref, l_ref, li_ref, p10_ref, mat_ref, out_ref, panel
):
    k, p, q = scal[0], scal[1], scal[2]

    def level_of(t, i):
        return lev[i % N_ROW, 4 * t + i // N_ROW]

    for t in range(2):
        for r in range(4):
            for h in range(2):
                panel[t, r, :, h * HALF : (h + 1) * HALF] = rows_ref[:, t, r, h].reshape(B, HALF)
        for c in range(2):
            for h in range(2):
                for part in range(2):
                    panel[
                        t, 4 + c, part * HALF : (part + 1) * HALF, h * HALF : (h + 1) * HALF
                    ] = cols_ref[:, part, t, c, h].reshape(HALF, HALF)

    def solve(n, _):
        i = jnp.where(n < 4, n * N_ROW + p, (n - 4) * N_COL + q)

        @pl.when(i > k)
        def _():
            panel[0, n] = by_level(dot_nt(panel[0, n], li_ref[0]), level_of(0, i))
            level = level_of(1, i)

            @pl.when((i > k + 1) & (level == 2))
            def _():
                raw = panel[1, n] - dot_nt(panel[0, n], p10_ref[...])
                panel[1, n] = dot_nt(raw, li_ref[1])

            @pl.when((i > k + 1) & (level == 1))
            def _():
                raw = rounded(panel[1, n] - dot_narrow(panel[0, n], p10_ref[...]))
                panel[1, n] = rounded(dot_nt(raw, li_ref[1]))

        return 0

    lax.fori_loop(0, 6, solve, 0)

    def trail(n, _):
        r, c = n // 2, n % 2
        i = r * N_ROW + p
        j = c * N_COL + q
        level = prec[r, c]
        active = (i >= j) & (j > k)
        halves = [pl.ds(r * 1024 + c * 2 + h, B, stride=4) for h in range(2)]

        def put(value):
            for h in range(2):
                out_ref[halves[h], :] = value[:, h * HALF : (h + 1) * HALF]

        def get():
            return jnp.concatenate([mat_ref[halves[h], :] for h in range(2)], axis=1)

        own_first = (j == k) & (i > k)
        own_second = (j == k + 1) & (i > k + 1)
        diagonal = (i == j) & ((j == k) | (j == k + 1))
        plain = jnp.logical_not(own_first | own_second | diagonal)

        @pl.when(plain & (level == 2))
        def _():
            put(get())

            @pl.when(active)
            def _():
                put(get() - dot_nt(panel[0, r], panel[0, 4 + c]) - dot_nt(panel[1, r], panel[1, 4 + c]))

        @pl.when(plain & (level == 1))
        def _():
            put(rounded(get()))

            @pl.when(active)
            def _():
                once = rounded(rounded(get()) - dot_narrow(panel[0, r], panel[0, 4 + c]))
                put(rounded(once - dot_narrow(panel[1, r], panel[1, 4 + c])))

        @pl.when(plain & (level == 0))
        def _():
            put(jnp.zeros((B, B), f32))

        @pl.when(own_first)
        def _():
            put(panel[0, r])

        @pl.when(own_second)
        def _():
            put(panel[1, r])

        @pl.when(diagonal)
        def _():
            put(l_ref[j - k])

        return 0

    lax.fori_loop(0, 8, trail, 0)


def update(scal, lev, prec, row_tiles, col_tiles, factors, inverses, p10, mat):
    return pl.pallas_call(
        update_kernel,
        in_specs=[SMEM, SMEM, SMEM] + [VMEM] * 6,
        out_specs=VMEM,
        out_shape=jax.ShapeDtypeStruct(mat.shape, f32),
        scratch_shapes=[pltpu.VMEM((2, 6, B, B), f32)],
        compiler_params=pltpu.CompilerParams(vmem_limit_bytes=40 << 20),
    )(scal, lev, prec, row_tiles, col_tiles, factors, inverses, p10, mat)


def cross_pairs(odd):
    pairs = []
    for p in range(N_ROW):
        for q in range(N_COL):
            low = q < N_ROW
            first = low != odd
            row = q if low else q - N_ROW
            col = p if first else p + N_ROW
            pairs.append((p * N_COL + q, row * N_COL + col))
    return pairs


def per_device(matrix, precision, first_col):
    p = lax.axis_index("row")
    q = lax.axis_index("col")
    k = first_col[0]
    scal = jnp.stack([k, p, q]).astype(jnp.int32)
    prec = precision.reshape(4, 2)
    mat = matrix.reshape(4096, HALF)

    sent = pack(scal, prec, mat)
    received = lax.all_to_all(sent, "col", 0, 0)
    bulk, even, odd, diag = route(scal, received)

    row_tiles = lax.all_gather(bulk, "col")
    seen = lax.all_gather(diag, "row")
    both = ("row", "col")
    first = lax.ppermute(even, both, cross_pairs(False))
    second = lax.ppermute(odd, both, cross_pairs(True))
    low = q < N_ROW
    parts = jnp.stack([jnp.where(low, first, second), jnp.where(low, second, first)])
    col_tiles = lax.all_gather(parts, "row")

    lev = seen[:, 4, :, 0].astype(jnp.int32)
    here = lax.dynamic_slice(seen, (k % N_ROW, 0, 0, 0), (1, 2, 8, HALF))[0]
    below = lax.dynamic_slice(seen, ((k + 1) % N_ROW, 0, 0, 0), (1, 4, 8, HALF))[0]
    mine = jnp.concatenate([here, below])
    diags = lax.all_to_all(
        jnp.broadcast_to(mine[None], (N_COL, 6, 8, HALF)), "col", 0, 0
    )
    factors, inverses, p10 = factor_two(scal, lev, diags)
    out = update(scal, lev, prec, row_tiles, col_tiles, factors, inverses, p10, mat)
    return out.reshape(matrix.shape)


def solution(mesh):
    in_specs = (P(None, "row", None, None, "col", None), P(None, "row", None, "col"), P())
    out_specs = P(None, "row", None, None, "col", None)
    return jax.shard_map(
        per_device, mesh=mesh, in_specs=in_specs, out_specs=out_specs, check_vma=False
    )
```

time: 1170 us -> 221 us (0.19)
  waiting for transfers between devices: 766 us -> 73.1 us
  other arithmetic: 131 us -> 0.72 us
  loops' own time: 111 us -> 0 us
  local copies, waits for them, and re-layouts: 117 us -> 9.8 us
  blocking collectives: 0 us -> 68.1 us
  Pallas kernels: 0 us -> 35.8 us
  starting transfers between devices: 0.42 us -> 15.4 us
  matrix products: 11.9 us -> 0 us
    psum x6 -> x0, waiting for transfers between devices: 766 us -> none  [spread(): return lax.psum(kept, axis)]
    another operation x18 -> x3, other arithmetic: 112 us -> 0.71 us  [the longest x2 0.63 us: per_device(): jnp.stack([jnp.where(low, first, second), jnp.where(low, second, first)])]
    another operation x20 -> x0, loops' own time: 111 us -> none  [the longest x2 110 us: update(): results = lax.map(one_tile, (rows_flat, cols_flat))]
    dynamic_slice x84 -> x0, local copies, waits for them, and re-layouts: 52.9 us -> none  [the longest x32 20.6 us: update(): results = lax.map(one_tile, (rows_flat, cols_flat))]
    all_to_all x0 -> x1, blocking collectives: none -> 44.7 us  [per_device(): received = lax.all_to_all(sent, 'col', 0, 0)]
    all_gather x0 -> x2, waiting for transfers between devices: none -> 44.1 us  [the longest x1 44.1 us: per_device(): row_tiles = lax.all_gather(bulk, 'col')]
    pallas_call x0 -> x4, Pallas kernels: none -> 35.8 us  [the longest x1 26.2 us: factor_two(): pl.pallas_call(factor_kernel, in_specs=[SMEM, SMEM, VMEM], out_specs=[VME...]
    all_gather x0 -> x1, blocking collectives: none -> 23.4 us  [per_device(): seen = lax.all_gather(diag, 'row')]
  transfers between devices with their start and end apart: 6 -> 5, of which waited for: 6 -> 3; matrix products, arithmetic and copies ran while one was open for 2% -> 1% of each run, Pallas kernels for 0% -> 12%
where the time goes in v1:
time: 221 us; the launch traced here: 217 us
  waiting for transfers between devices  73.1 us (33%)
  blocking collectives  68.1 us (31%)
  Pallas kernels  35.8 us (16%)
  starting transfers between devices  15.4 us (7%)
  between operations  14.2 us (6%)
  local copies, waits for them, and re-layouts  9.8 us (4%)
    all_to_all x1, blocking collectives, per_device(): received = lax.all_to_all(sent, 'col', 0, 0)  44.7 us
    all_gather x1, waiting for transfers between devices, per_device(): row_tiles = lax.all_gather(bulk, 'col')  44.1 us
    pallas_call x1, Pallas kernels, factor_two(): pl.pallas_call(factor_kernel, in_specs=[SMEM, SMEM, VMEM], out_specs=[VME...  26.2 us
    all_gather x1, blocking collectives, per_device(): seen = lax.all_gather(diag, 'row')  23.4 us
    all_to_all x1, waiting for transfers between devices, per_device(): lax.all_to_all(jnp.broadcast_to(mine[None], (N_COL, 6, 8, HALF)), 'col',...  21.4 us
    unnamed x21, local copies, waits for them, and re-layouts  8.02 us
    all_to_all x1, starting transfers between devices, per_device(): lax.all_to_all(jnp.broadcast_to(mine[None], (N_COL, 6, 8, HALF)), 'col',...  7.64 us
    ppermute x1, waiting for transfers between devices, per_device(): second = lax.ppermute(odd, both, cross_pairs(True))  6.92 us
  transfers between devices with their start and end apart: 5, of which 3 were waited for; matrix products, arithmetic and copies ran while one was open for 1% of the time, Pallas kernels for 12%

profile of v1, /device:TPU:1, one launch (start us, length us, event | category | flops | bytes accessed | tf_op | source)
XLA Modules:
  0.0 217.2 jit_solution(4339859512697057251)
XLA Ops:
  7.2 0.8 copy.21.prec
  8.0 1.6 copy-done
  9.6 0.7 shard_map.37
  10.4 44.7 %all_to_all.10.first_ref.second_ref = f32[32,9,8,128]{3,2,1,0:T(8,128)} all-to-all(f32[32,9,8,128]{3,2,1,0:T(8,128)S(1)} %shard_map.37), channel_id=1, replica_groups=mesh['row'=16,'col'=32] {'col'}, dimensions={0} | all-to-all | bytes 2359296 | tf_op jit(solution)/shard_map/all_to_all | solution.py:356
  55.0 2.1 shard_map.38
  57.1 4.4 %collective-permute-start = (f32[2,2,2,8,128]{4,3,2,1,0:T(8,128)}, f32[2,2,2,8,128]{4,3,2,1,0:T(8,128)S(1)}, u32[]{:S(2)}, u32[]{:S(2)}) collective-permute-start(f32[2,2,2,8,128]{4,3,2,1,0:T(8,128)} %get-tuple-element.14), channel_id=1, source_target_pairs={{0,0},{1,32},{2,64},{3,96},{4,128},{5,160},{6,192},{7,224},{8,256}... | collective-permute-start | bytes 98312 | tf_op jit(solution)/shard_map/ppermute | solution.py:362
  61.6 3.3 %collective-permute-start.1 = (f32[2,2,2,8,128]{4,3,2,1,0:T(8,128)}, f32[2,2,2,8,128]{4,3,2,1,0:T(8,128)S(1)}, u32[]{:S(2)}, u32[]{:S(2)}) collective-permute-start(f32[2,2,2,8,128]{4,3,2,1,0:T(8,128)} %get-tuple-element.15), channel_id=1, source_target_pairs={{0,16},{1,48},{2,80},{3,112},{4,144},{5,176},{6,208},{7,240},{8,27... | collective-permute-start | bytes 98312 | tf_op jit(solution)/shard_map/ppermute | solution.py:363
  64.9 6.9 %collective-permute-done.1 = f32[2,2,2,8,128]{4,3,2,1,0:T(8,128)S(1)} collective-permute-done((f32[2,2,2,8,128]{4,3,2,1,0:T(8,128)}, f32[2,2,2,8,128]{4,3,2,1,0:T(8,128)S(1)}, u32[]{:S(2)}, u32[]{:S(2)}) %collective-permute-start.1) | collective-permute-done | bytes 32800 | tf_op jit(solution)/shard_map/ppermute | solution.py:363
  71.9 0.6 pad_maximum_fusion
  72.6 0.7 all-gather.6.cloned.1.call-update
  73.3 23.4 %all-gather = f32[80,8,128]{2,1,0:T(8,128)S(1)} all-gather(f32[5,8,128]{2,1,0:T(8,128)} %get-tuple-element.12), channel_id=2, replica_groups=mesh['row'=16,'col'=32] {'row'}, dimensions={0}, use_global_device_ids=true | all-gather | bytes 348160 | tf_op jit(solution)/shard_map/all_gather | solution.py:360
  96.7 0.9 broadcast_in_dim.2
  97.7 7.6 %all-to-all-start.1 = ((f32[32,6,8,128]{3,2,1,0:T(8,128)}), f32[32,6,8,128]{3,2,1,0:T(8,128)S(1)}, u32[]{:S(2)}, u32[]{:S(2)}) async-start(f32[32,6,8,128]{3,2,1,0:T(8,128)} %broadcast_in_dim.2), calls=%async_computation.1 | async-start | bytes 1572864 | tf_op jit(solution)/shard_map/all_to_all | solution.py:372
  105.3 0.1 copy.27
  105.5 21.4 %all-to-all-done.1.d_ref = f32[32,6,8,128]{3,2,1,0:T(8,128)S(1)} async-done(((f32[32,6,8,128]{3,2,1,0:T(8,128)}), f32[32,6,8,128]{3,2,1,0:T(8,128)S(1)}, u32[]{:S(2)}, u32[]{:S(2)}) %all-to-all-start.1) | async-done | bytes 786464 | tf_op jit(solution)/shard_map/all_to_all | solution.py:372
  127.0 26.2 %shard_map.39 = (f32[2,256,256]{2,1,0:T(8,128)S(1)}, f32[2,256,256]{2,1,0:T(8,128)S(1)}, f32[256,256]{1,0:T(8,128)S(1)}) custom-call(s32[3]{0:T(128)S(1)} %copy-done.9, s32[16,8]{1,0:T(8,128)S(1)} %copy.24.lev, f32[32,6,8,128]{3,2,1,0:T(8,128)S(1)} %all-to-all-done.1.d_ref), custom_call_target="tpu_custom_call" | custom-call | tf_op jit(solution)/shard_map/pallas_call | solution.py:211
  153.2 0.8 copy-done.4
  154.0 0.7 copy-done.6
  154.7 44.1 %all-gather.6.cloned.1.call-done = f32[64,4,2,8,128]{4,3,2,1,0:T(8,128)} async-done(((f32[2,4,2,8,128]{4,3,2,1,0:T(8,128)}), f32[64,4,2,8,128]{4,3,2,1,0:T(8,128)}) %all-gather.6.cloned.1.call-update) | async-done | bytes 2097168 | tf_op jit(solution)/shard_map/all_gather | solution.py:359
  198.8 1.6 copy-done.2
  200.4 1.2 copy-done.3
  201.6 1.0 copy-done.5
  202.6 0.9 copy-done.7
  203.6 6.8 %shard_map.40 = f32[4096,128]{1,0:T(8,128)} custom-call(s32[3]{0:T(128)S(1)} %copy-done.9, s32[16,8]{1,0:T(8,128)S(1)} %copy.24.lev, s32[4,2]{1,0:T(4,128)S(1)} %copy.21.prec, f32[32,2,4,2,8,128]{5,4,3,2,1,0:T(8,128)S(1)} %bitcast.25, f32[16,2,2,2,2,8,128]{6,5,4,3,2,1,0:T(8,128)S(1)} %bitcast.26, f32[2,256,256]{2,1,0:T(8,128)S(1)} %get-tuple-element.16.l_ref, ...), custom_call_target="tpu_custom_call" | custom-call | tf_op jit(solution)/shard_map/pallas_call | solution.py:325
  (26 shorter events, 0.3 us)
Async XLA Ops:
  6.5 148.1 %all-gather.8.cloned.1.call-start = ((), (), s32[]{:S(2)}) async-start(), calls=%async_computation.3 | async-start | bytes 1114112 | tf_op jit(solution)/shard_map/all_gather | solution.py:366
  8.0 47.0 %copy-start.8 = (s32[3]{0:T(128)}, s32[3]{0:T(128)S(1)}, u32[]{:S(2)}) copy-start(s32[3]{0:T(128)S(1)} %pad_add_fusion.scal) | copy-start | bytes 40
  8.0 1.6 copy-start
  57.1 69.8 %copy-start.9 = (s32[3]{0:T(128)S(1)}, s32[3]{0:T(128)}, u32[]{:S(2)}) copy-start(s32[3]{0:T(128)} %copy-done.8) | copy-start | bytes 40
  57.1 7.8 %collective-permute-start = (f32[2,2,2,8,128]{4,3,2,1,0:T(8,128)}, f32[2,2,2,8,128]{4,3,2,1,0:T(8,128)S(1)}, u32[]{:S(2)}, u32[]{:S(2)}) collective-permute-start(f32[2,2,2,8,128]{4,3,2,1,0:T(8,128)} %get-tuple-element.14), channel_id=1, source_target_pairs={{0,0},{1,32},{2,64},{3,96},{4,128},{5,160},{6,192},{7,224},{8,256}... | collective-permute-start | bytes 98312 | tf_op jit(solution)/shard_map/ppermute | solution.py:362
  61.6 10.2 %collective-permute-start.1 = (f32[2,2,2,8,128]{4,3,2,1,0:T(8,128)}, f32[2,2,2,8,128]{4,3,2,1,0:T(8,128)S(1)}, u32[]{:S(2)}, u32[]{:S(2)}) collective-permute-start(f32[2,2,2,8,128]{4,3,2,1,0:T(8,128)} %get-tuple-element.15), channel_id=1, source_target_pairs={{0,16},{1,48},{2,80},{3,112},{4,144},{5,176},{6,208},{7,240},{8,27... | collective-permute-start | bytes 98312 | tf_op jit(solution)/shard_map/ppermute | solution.py:363
  71.8 126.9 %copy-start.1 = (f32[4,1,256,2,1,256]{5,4,3,2,1,0:T(1,128)S(1)}, f32[4,1,256,2,1,256]{5,4,3,2,1,0:T(1,128)}, u32[]{:S(2)}) copy-start(f32[4,1,256,2,1,256]{5,4,3,2,1,0:T(1,128)} %param.3) | copy-start | bytes 6291460
  72.5 126.3 %all-gather.6.cloned.1.call-start = ((), (), s32[]{:S(2)}) async-start(), calls=%async_computation.2 | async-start | bytes 2162688 | tf_op jit(solution)/shard_map/all_gather | solution.py:359
  97.7 29.3 %all-to-all-start.1 = ((f32[32,6,8,128]{3,2,1,0:T(8,128)}), f32[32,6,8,128]{3,2,1,0:T(8,128)S(1)}, u32[]{:S(2)}, u32[]{:S(2)}) async-start(f32[32,6,8,128]{3,2,1,0:T(8,128)} %broadcast_in_dim.2), calls=%async_computation.1 | async-start | bytes 1572864 | tf_op jit(solution)/shard_map/all_to_all | solution.py:372
  153.2 0.8 copy-start.4
  154.0 0.7 copy-start.6
  198.8 1.6 copy-start.2
  200.4 1.2 copy-start.3
  201.6 1.0 copy-start.5
  202.6 0.9 copy-start.7
Sparse Core Ops, SparseCore 0:
  72.6 44.0 all-gather.7
  119.9 78.8 all-gather.5

commit v2 on v1

--- a/solution.py
+++ b/solution.py
@@ -44,9 +44,10 @@
     return jnp.where(level == 2, x, jnp.where(level == 1, rounded(x), 0.0))
 
 
-def pack_kernel(scal, prec, mat_ref, out_ref):
-    k, q = scal[0], scal[2]
+def pack_kernel(scal, prec, mat_ref, diag_ref, bulk_ref):
+    k, p, q = scal[0], scal[1], scal[2]
     col = jnp.where(q == k % N_COL, k // N_COL, (k + 1) // N_COL)
+    here_r = jnp.where(p == k % N_ROW, k // N_ROW, (k + 1) // N_ROW)
     sub = lax.broadcasted_iota(jnp.int32, (8, HALF), 0)
     levels = jnp.zeros((8, HALF), f32)
     for r in range(4):
@@ -54,44 +55,94 @@
         levels = jnp.where(sub % 4 == r, level.astype(f32), levels)
         for h in range(2):
             rows = mat_ref[pl.ds(r * 1024 + col * 2 + h, B, stride=4), :]
-            out_ref[:, r * 2 + h] = by_level(rows, level).reshape(32, 8, HALF)
-    out_ref[:, 8] = jnp.broadcast_to(levels[None], (32, 8, HALF))
+            rows = by_level(rows, level).reshape(32, 8, HALF)
+            bulk_ref[:, r * 2 + h] = rows
+
+            @pl.when(here_r == r)
+            def _():
+                diag_ref[:, h] = rows
+
+    diag_ref[:, 2] = jnp.broadcast_to(levels[None], (32, 8, HALF))
 
 
 def pack(scal, prec, mat):
     return pl.pallas_call(
         pack_kernel,
         in_specs=[SMEM, SMEM, VMEM],
-        out_specs=VMEM,
-        out_shape=jax.ShapeDtypeStruct((N_COL, 9, 8, HALF), f32),
-        compiler_params=pltpu.CompilerParams(vmem_limit_bytes=32 << 20),
+        out_specs=[VMEM, VMEM],
+        out_shape=[
+            jax.ShapeDtypeStruct((N_COL, 3, 8, HALF), f32),
+            jax.ShapeDtypeStruct((N_COL, 8, 8, HALF), f32),
+        ],
+        compiler_params=pltpu.CompilerParams(vmem_limit_bytes=8 << 20),
     )(scal, prec, mat)
 
 
-def route_kernel(scal, first_ref, second_ref, bulk_ref, even_ref, odd_ref, diag_ref):
-    k, p, q = scal[0], scal[1], scal[2]
-    low = q < N_ROW
+def diag_kernel(scal, first_ref, second_ref, out_ref):
+    k, p = scal[0], scal[1]
     sub = lax.broadcasted_iota(jnp.int32, (8, HALF), 0)
+    out_ref[0:2] = first_ref[0, 0:2]
+    out_ref[2:4] = second_ref[0, 0:2]
+    out_ref[4] = jnp.where(sub < 4, first_ref[0, 2], second_ref[0, 2])
+
+
+def diag_parts(scal, received):
+    block = (1, 3, 8, HALF)
+    return pl.pallas_call(
+        diag_kernel,
+        grid_spec=pltpu.PrefetchScalarGridSpec(
+            num_scalar_prefetch=1,
+            grid=(1,),
+            in_specs=[
+                pl.BlockSpec(block, lambda _, s: (s[0] % N_COL, 0, 0, 0)),
+                pl.BlockSpec(block, lambda _, s: ((s[0] + 1) % N_COL, 0, 0, 0)),
+            ],
+            out_specs=VMEM,
+        ),
+        out_shape=jax.ShapeDtypeStruct((5, 8, HALF), f32),
+    )(scal, received, received)
+
+
+def copies_kernel(scal, here_ref, below_ref, out_ref):
+    out_ref[:, 0:2] = jnp.broadcast_to(here_ref[:, 0:2], (N_COL, 2, 8, HALF))
+    out_ref[:, 2:6] = jnp.broadcast_to(below_ref[:, 0:4], (N_COL, 4, 8, HALF))
+
+
+def diag_copies(scal, seen):
+    block = (1, 5, 8, HALF)
+    return pl.pallas_call(
+        copies_kernel,
+        grid_spec=pltpu.PrefetchScalarGridSpec(
+            num_scalar_prefetch=1,
+            grid=(1,),
+            in_specs=[
+                pl.BlockSpec(block, lambda _, s: (s[0] % N_ROW, 0, 0, 0)),
+                pl.BlockSpec(block, lambda _, s: ((s[0] + 1) % N_ROW, 0, 0, 0)),
+            ],
+            out_specs=VMEM,
+        ),
+        out_shape=jax.ShapeDtypeStruct((N_COL, 6, 8, HALF), f32),
+    )(scal, seen, seen)
+
+
+def route_kernel(scal, first_ref, second_ref, bulk_ref, even_ref, odd_ref):
+    low = scal[2] < N_ROW
     for t, ref in enumerate((first_ref, second_ref)):
         for r in range(4):
             for h in range(2):
-                bulk_ref[t, r, h] = ref[0, 2 * r + h]
+                part = ref[0, 2 * r + h]
+                for z in range(8):
+                    bulk_ref[z, t, r, h] = part
         for c in range(2):
             for h in range(2):
                 even = ref[0, 4 * c + h]
                 odd = ref[0, 4 * c + 2 + h]
                 even_ref[t, c, h] = jnp.where(low, even, odd)
                 odd_ref[t, c, h] = jnp.where(low, odd, even)
-    next_r = (k + 1) // N_ROW
-    here_r = jnp.where(p == k % N_ROW, k // N_ROW, next_r)
-    for h in range(2):
-        diag_ref[h] = first_ref[0, 2 * here_r + h]
-        diag_ref[2 + h] = second_ref[0, 2 * next_r + h]
-    diag_ref[4] = jnp.where(sub < 4, first_ref[0, 8], second_ref[0, 8])
 
 
 def route(scal, received):
-    block = (1, 9, 8, HALF)
+    block = (1, 8, 8, HALF)
     return pl.pallas_call(
         route_kernel,
         grid_spec=pltpu.PrefetchScalarGridSpec(
@@ -101,15 +152,33 @@
                 pl.BlockSpec(block, lambda _, s: (s[0] % N_COL, 0, 0, 0)),
                 pl.BlockSpec(block, lambda _, s: ((s[0] + 1) % N_COL, 0, 0, 0)),
             ],
-            out_specs=[VMEM, VMEM, VMEM, VMEM],
+            out_specs=[VMEM, VMEM, VMEM],
         ),
         out_shape=[
-            jax.ShapeDtypeStruct((2, 4, 2, 8, HALF), f32),
+            jax.ShapeDtypeStruct((8, 2, 4, 2, 8, HALF), f32),
             jax.ShapeDtypeStruct((2, 2, 2, 8, HALF), f32),
             jax.ShapeDtypeStruct((2, 2, 2, 8, HALF), f32),
-            jax.ShapeDtypeStruct((5, 8, HALF), f32),
         ],
     )(scal, received, received)
+
+
+def cols_kernel(scal, first_ref, second_ref, out_ref):
+    low = scal[2] < N_ROW
+    first, second = first_ref[...], second_ref[...]
+    lo = jnp.where(low, first, second)
+    hi = jnp.where(low, second, first)
+    for y in range(N_ROW):
+        out_ref[y, 0] = lo
+        out_ref[y, 1] = hi
+
+
+def col_copies(scal, first, second):
+    return pl.pallas_call(
+        cols_kernel,
+        in_specs=[SMEM, VMEM, VMEM],
+        out_specs=VMEM,
+        out_shape=jax.ShapeDtypeStruct((N_ROW, 2, 2, 2, 2, 8, HALF), f32),
+    )(scal, first, second)
 
 
 def factor_half(block):
@@ -218,7 +287,8 @@
             pltpu.VMEM((2, HALF, HALF), f32),
             pltpu.VMEM((2, HALF, HALF), f32),
         ],
-        compiler_params=pltpu.CompilerParams(vmem_limit_bytes=32 << 20),
+        compiler_params=pltpu.CompilerParams(vmem_limit_bytes=8 << 20),
+        cost_estimate=pl.CostEstimate(flops=3 * 10**10, bytes_accessed=10**6, transcendentals=0),
     )(scal, lev, diag)
 
 
@@ -231,15 +301,17 @@
         return lev[i % N_ROW, 4 * t + i // N_ROW]
 
     for t in range(2):
-        for r in range(4):
-            for h in range(2):
-                panel[t, r, :, h * HALF : (h + 1) * HALF] = rows_ref[:, t, r, h].reshape(B, HALF)
-        for c in range(2):
-            for h in range(2):
+        for h in range(2):
+            lanes = slice(h * HALF, (h + 1) * HALF)
+            for r in range(4):
+                for x in range(4):
+                    for z in range(8):
+                        at = 8 * (4 * z + x)
+                        panel[t, r, at : at + 8, lanes] = rows_ref[x, z, t, r, h]
+            for c in range(2):
                 for part in range(2):
-                    panel[
-                        t, 4 + c, part * HALF : (part + 1) * HALF, h * HALF : (h + 1) * HALF
-                    ] = cols_ref[:, part, t, c, h].reshape(HALF, HALF)
+                    at = slice(part * HALF, (part + 1) * HALF)
+                    panel[t, 4 + c, at, lanes] = cols_ref[:, part, t, c, h].reshape(HALF, HALF)
 
     def solve(n, _):
         i = jnp.where(n < 4, n * N_ROW + p, (n - 4) * N_COL + q)
@@ -328,7 +400,8 @@
         out_specs=VMEM,
         out_shape=jax.ShapeDtypeStruct(mat.shape, f32),
         scratch_shapes=[pltpu.VMEM((2, 6, B, B), f32)],
-        compiler_params=pltpu.CompilerParams(vmem_limit_bytes=40 << 20),
+        compiler_params=pltpu.CompilerParams(vmem_limit_bytes=12 << 20),
+        cost_estimate=pl.CostEstimate(flops=10**10, bytes_accessed=10**7, transcendentals=0),
     )(scal, lev, prec, row_tiles, col_tiles, factors, inverses, p10, mat)
 
 
@@ -352,28 +425,31 @@
     prec = precision.reshape(4, 2)
     mat = matrix.reshape(4096, HALF)
 
-    sent = pack(scal, prec, mat)
-    received = lax.all_to_all(sent, "col", 0, 0)
-    bulk, even, odd, diag = route(scal, received)
-
-    row_tiles = lax.all_gather(bulk, "col")
-    seen = lax.all_gather(diag, "row")
+    z_groups = [[4 * z + x for z in range(8)] for x in range(4)]
+    x_groups = [[4 * z + x for x in range(4)] for z in range(8)]
+
+    sent_diag, sent_bulk = pack(scal, prec, mat)
+    got_diag = lax.all_to_all(sent_diag, "col", 0, 0)
+    seen = lax.all_gather(diag_parts(scal, got_diag), "row")
+    got_bulk = lax.all_to_all(sent_bulk, "col", 0, 0)
+    bulk, even, odd = route(scal, got_bulk)
+    diags = lax.all_to_all(diag_copies(scal, seen), "col", 0, 0)
+    lev = seen[:, 4, :, 0].astype(jnp.int32)
+
     both = ("row", "col")
     first = lax.ppermute(even, both, cross_pairs(False))
     second = lax.ppermute(odd, both, cross_pairs(True))
-    low = q < N_ROW
-    parts = jnp.stack([jnp.where(low, first, second), jnp.where(low, second, first)])
-    col_tiles = lax.all_gather(parts, "row")
-
-    lev = seen[:, 4, :, 0].astype(jnp.int32)
-    here = lax.dynamic_slice(seen, (k % N_ROW, 0, 0, 0), (1, 2, 8, HALF))[0]
-    below = lax.dynamic_slice(seen, ((k + 1) % N_ROW, 0, 0, 0), (1, 4, 8, HALF))[0]
-    mine = jnp.concatenate([here, below])
-    diags = lax.all_to_all(
-        jnp.broadcast_to(mine[None], (N_COL, 6, 8, HALF)), "col", 0, 0
+    slab = lax.all_to_all(bulk, "col", 0, 0, axis_index_groups=z_groups)
+    diags, first, second, slab = lax.optimization_barrier((diags, first, second, slab))
+
+    col_tiles = lax.all_to_all(col_copies(scal, first, second), "row", 0, 0)
+    row_tiles = lax.all_to_all(
+        jnp.broadcast_to(slab[None], (4,) + slab.shape), "col", 0, 0, axis_index_groups=x_groups
     )
     factors, inverses, p10 = factor_two(scal, lev, diags)
-    out = update(scal, lev, prec, row_tiles, col_tiles, factors, inverses, p10, mat)
+    out = update(
+        scal, lev, prec, row_tiles, col_tiles, factors, inverses, p10, mat
+    )
     return out.reshape(matrix.shape)
 
 

time: 221 us -> 196 us (0.89); the launches traced: 217 us -> 195 us
  starting transfers between devices: 15.4 us -> 38.3 us
  blocking collectives: 68.1 us -> 49.1 us
  waiting for transfers between devices: 73.1 us -> 54.8 us
  between operations: 14.2 us -> 0.78 us
  Pallas kernels: 35.8 us -> 40.6 us
    all_gather x2 -> x0, waiting for transfers between devices: 44.1 us -> none  [the longest x1 44.1 us: per_device(): row_tiles = lax.all_gather(bulk, 'col')]
    all_to_all x1 -> x5, waiting for transfers between devices: 21.4 us -> 42.8 us  [the longest x1 23.5 us: per_device(): lax.all_to_all(jnp.broadcast_to(slab[None], (4,) + slab.shape), 'col', 0,...]
    all_to_all x1 -> x5, starting transfers between devices: 7.64 us -> 26.4 us  [the longest x1 9.5 us: per_device(): diags = lax.all_to_all(diag_copies(scal, seen), 'col', 0, 0)]
    all_to_all x1, blocking collectives: 44.7 us -> 27.4 us  [per_device(): got_diag = lax.all_to_all(sent_diag, 'col', 0, 0)]
    pallas_call x1 -> x4, Pallas kernels: 0.72 us -> 8.03 us  [the longest x1 2.37 us: diag_copies(): pl.pallas_call(copies_kernel, grid_spec=pltpu.PrefetchScalarGridSpec(num_...]
    ppermute x1, waiting for transfers between devices: 6.92 us -> 12 us  [per_device(): second = lax.ppermute(odd, both, cross_pairs(True))]
    ppermute x1, starting transfers between devices: 3.31 us -> 7.19 us  [per_device(): second = lax.ppermute(odd, both, cross_pairs(True))]
    pallas_call x1, Pallas kernels: 6.78 us -> 4.01 us  [update(): pl.pallas_call(update_kernel, in_specs=[SMEM, SMEM, SMEM] + [VMEM] * 6, o...]
  transfers between devices with their start and end apart: 5 -> 7, of which waited for: 3 -> 3; matrix products, arithmetic and copies ran while one was open for 1% -> 1% of each run, Pallas kernels for 12% -> 18%
where the time goes in v2:
time: 196 us; the launch traced here: 195 us
  waiting for transfers between devices  54.8 us (28%)
  blocking collectives  49.1 us (25%)
  Pallas kernels  40.6 us (21%)
  starting transfers between devices  38.3 us (20%)
  local copies, waits for them, and re-layouts  10.5 us (5%)
    all_to_all x1, blocking collectives, per_device(): got_diag = lax.all_to_all(sent_diag, 'col', 0, 0)  27.4 us
    pallas_call x1, Pallas kernels, factor_two(): pl.pallas_call(factor_kernel, in_specs=[SMEM, SMEM, VMEM], out_specs=[VME...  26.2 us
    all_to_all x1, waiting for transfers between devices, per_device(): lax.all_to_all(jnp.broadcast_to(slab[None], (4,) + slab.shape), 'col', 0,...  23.5 us
    all_gather x1, blocking collectives, per_device(): seen = lax.all_gather(diag_parts(scal, got_diag), 'row')  21.7 us
    all_to_all x1, waiting for transfers between devices, per_device(): diags = lax.all_to_all(diag_copies(scal, seen), 'col', 0, 0)  19.3 us
    ppermute x1, waiting for transfers between devices, per_device(): second = lax.ppermute(odd, both, cross_pairs(True))  12 us
    all_to_all x1, starting transfers between devices, per_device(): diags = lax.all_to_all(diag_copies(scal, seen), 'col', 0, 0)  9.5 us
    unnamed x30, local copies, waits for them, and re-layouts  8.04 us
  transfers between devices with their start and end apart: 7, of which 3 were waited for; matrix products, arithmetic and copies ran while one was open for 1% of the time, Pallas kernels for 18%

profile of v2, /device:TPU:1, one launch (start us, length us, event | category | flops | bytes accessed | tf_op | source)
XLA Modules:
  0.0 195.0 jit_solution(13655692441155743139)
XLA Ops:
  1.5 1.6 copy-done
  3.1 1.8 shard_map.37
  4.9 27.4 %all_to_all.30.first_ref.second_ref = f32[32,3,8,128]{3,2,1,0:T(8,128)} all-to-all(f32[32,3,8,128]{3,2,1,0:T(8,128)S(1)} %get-tuple-element.17), channel_id=1, replica_groups=mesh['row'=16,'col'=32] {'col'}, dimensions={0} | all-to-all | bytes 786432 | tf_op jit(solution)/shard_map/all_to_all | solution.py:432
  32.3 5.0 %all-to-all-start.2 = ((f32[32,8,8,128]{3,2,1,0:T(8,128)}), f32[32,8,8,128]{3,2,1,0:T(8,128)S(1)}, u32[]{:S(2)}, u32[]{:S(2)}) async-start(f32[32,8,8,128]{3,2,1,0:T(8,128)} %get-tuple-element.18), calls=%async_computation.2 | async-start | bytes 2097152 | tf_op jit(solution)/shard_map/all_to_all | solution.py:434
  37.3 2.0 %shard_map.38 = f32[5,8,128]{2,1,0:T(8,128)} custom-call(s32[3]{0:T(128)} %copy-done.6, f32[32,3,8,128]{3,2,1,0:T(8,128)} %all_to_all.30.first_ref.second_ref, f32[32,3,8,128]{3,2,1,0:T(8,128)} %all_to_all.30.first_ref.second_ref), custom_call_target="tpu_custom_call" | custom-call | tf_op jit(solution)/shard_map/pallas_call | solution.py:91
  39.3 21.7 %all-gather = f32[80,8,128]{2,1,0:T(8,128)} all-gather(f32[5,8,128]{2,1,0:T(8,128)} %shard_map.38), channel_id=2, replica_groups=mesh['row'=16,'col'=32] {'row'}, dimensions={0}, use_global_device_ids=true | all-gather | bytes 348160 | tf_op jit(solution)/shard_map/all_gather | solution.py:433
  61.0 2.4 %shard_map.39 = f32[32,6,8,128]{3,2,1,0:T(8,128)} custom-call(s32[3]{0:T(128)} %copy-done.6, f32[16,5,8,128]{3,2,1,0:T(8,128)} %bitcast.12, f32[16,5,8,128]{3,2,1,0:T(8,128)} %bitcast.13), custom_call_target="tpu_custom_call" | custom-call | tf_op jit(solution)/shard_map/pallas_call | solution.py:113
  63.4 9.5 %all-to-all-start.1 = ((f32[32,6,8,128]{3,2,1,0:T(8,128)}), f32[32,6,8,128]{3,2,1,0:T(8,128)S(1)}, u32[]{:S(2)}, u32[]{:S(2)}) async-start(f32[32,6,8,128]{3,2,1,0:T(8,128)} %shard_map.39), calls=%async_computation.1 | async-start | bytes 1572864 | tf_op jit(solution)/shard_map/all_to_all | solution.py:436
  72.9 2.3 %shard_map.40 = (f32[8,2,4,2,8,128]{5,4,3,2,1,0:T(8,128)}, f32[2,2,2,8,128]{4,3,2,1,0:T(8,128)}, f32[2,2,2,8,128]{4,3,2,1,0:T(8,128)}) custom-call(s32[3]{0:T(128)} %copy-done.6, f32[32,8,8,128]{3,2,1,0:T(8,128)} %copy-done.12, f32[32,8,8,128]{3,2,1,0:T(8,128)} %copy-done.12), custom_call_target="tpu_custom_call" | custom-call | tf_op jit(solution)/shard_map/pallas_call | solution.py:146
  75.2 19.3 %all-to-all-done.1.d_ref = f32[32,6,8,128]{3,2,1,0:T(8,128)S(1)} async-done(((f32[32,6,8,128]{3,2,1,0:T(8,128)}), f32[32,6,8,128]{3,2,1,0:T(8,128)S(1)}, u32[]{:S(2)}, u32[]{:S(2)}) %all-to-all-start.1) | async-done | bytes 786464 | tf_op jit(solution)/shard_map/all_to_all | solution.py:436
  94.5 3.8 %all-to-all-start.3 = ((f32[8,2,4,2,8,128]{5,4,3,2,1,0:T(8,128)}), f32[8,2,4,2,8,128]{5,4,3,2,1,0:T(8,128)S(1)}, u32[]{:S(2)}, u32[]{:S(2)}) async-start(f32[8,2,4,2,8,128]{5,4,3,2,1,0:T(8,128)} %get-tuple-element.21), calls=%async_computation.3 | async-start | bytes 1048576 | tf_op jit(solution)/shard_map/all_to_all | solution.py:442
  98.3 4.8 %collective-permute-start = (f32[2,2,2,8,128]{4,3,2,1,0:T(8,128)}, f32[2,2,2,8,128]{4,3,2,1,0:T(8,128)S(1)}, u32[]{:S(2)}, u32[]{:S(2)}) collective-permute-start(f32[2,2,2,8,128]{4,3,2,1,0:T(8,128)} %get-tuple-element.19), channel_id=1, source_target_pairs={{0,0},{1,32},{2,64},{3,96},{4,128},{5,160},{6,192},{7,224},{8,256}... | collective-permute-start | bytes 98312 | tf_op jit(solution)/shard_map/ppermute | solution.py:440
  103.1 7.2 %collective-permute-start.1 = (f32[2,2,2,8,128]{4,3,2,1,0:T(8,128)}, f32[2,2,2,8,128]{4,3,2,1,0:T(8,128)S(1)}, u32[]{:S(2)}, u32[]{:S(2)}) collective-permute-start(f32[2,2,2,8,128]{4,3,2,1,0:T(8,128)} %get-tuple-element.20), channel_id=1, source_target_pairs={{0,16},{1,48},{2,80},{3,112},{4,144},{5,176},{6,208},{7,240},{8,27... | collective-permute-start | bytes 98312 | tf_op jit(solution)/shard_map/ppermute | solution.py:441
  110.3 12.0 %collective-permute-done.1.second_ref = f32[2,2,2,8,128]{4,3,2,1,0:T(8,128)S(1)} collective-permute-done((f32[2,2,2,8,128]{4,3,2,1,0:T(8,128)}, f32[2,2,2,8,128]{4,3,2,1,0:T(8,128)S(1)}, u32[]{:S(2)}, u32[]{:S(2)}) %collective-permute-start.1) | collective-permute-done | bytes 32800 | tf_op jit(solution)/shard_map/ppermute | solution.py:441
  122.3 1.6 broadcast_in_dim.2
  123.9 3.6 %all-to-all-start.4 = ((f32[4,8,2,4,2,8,128]{6,5,4,3,2,1,0:T(8,128)}), f32[4,8,2,4,2,8,128]{6,5,4,3,2,1,0:T(8,128)S(1)}, u32[]{:S(2)}, u32[]{:S(2)}) async-start(f32[4,8,2,4,2,8,128]{6,5,4,3,2,1,0:T(8,128)} %broadcast_in_dim.2), calls=%async_computation.4 | async-start | bytes 4194304 | tf_op jit(solution)/shard_map/all_to_all | solution.py:446
  128.5 1.9 shard_map.41
  130.4 23.5 %all-to-all-done.4.rows_ref = f32[4,8,2,4,2,8,128]{6,5,4,3,2,1,0:T(8,128)S(1)} async-done(((f32[4,8,2,4,2,8,128]{6,5,4,3,2,1,0:T(8,128)}), f32[4,8,2,4,2,8,128]{6,5,4,3,2,1,0:T(8,128)S(1)}, u32[]{:S(2)}, u32[]{:S(2)}) %all-to-all-start.4) | async-done | bytes 2097184 | tf_op jit(solution)/shard_map/all_to_all | solution.py:446
  153.9 4.4 %all-to-all-start.5 = ((f32[16,2,2,2,2,8,128]{6,5,4,3,2,1,0:T(8,128)}), f32[16,2,2,2,2,8,128]{6,5,4,3,2,1,0:T(8,128)S(1)}, u32[]{:S(2)}, u32[]{:S(2)}) async-start(f32[16,2,2,2,2,8,128]{6,5,4,3,2,1,0:T(8,128)} %shard_map.41), calls=%async_computation.5 | async-start | bytes 2097152 | tf_op jit(solution)/shard_map/all_to_all | solution.py:445
  158.4 1.1 copy-done.5
  159.5 26.2 %shard_map.42 = (f32[2,256,256]{2,1,0:T(8,128)S(1)}, f32[2,256,256]{2,1,0:T(8,128)S(1)}, f32[256,256]{1,0:T(8,128)S(1)}) custom-call(s32[3]{0:T(128)S(1)} %copy-done.7, s32[16,8]{1,0:T(8,128)S(1)} %bitcast.10, f32[32,6,8,128]{3,2,1,0:T(8,128)S(1)} %copy-done.5), custom_call_target="tpu_custom_call" | custom-call | flops 30000001024 | bytes 1000000 | tf_op jit(solution)/shard_map/pallas_call | solution.py:280
  187.4 1.6 copy-done.3
  189.0 1.0 copy-done.9
  191.0 4.0 %shard_map.43 = f32[4096,128]{1,0:T(8,128)} custom-call(s32[3]{0:T(128)S(1)} %copy-done.7, s32[16,8]{1,0:T(8,128)S(1)} %bitcast.11, s32[4,2]{1,0:T(4,128)S(1)} %copy.16.prec, f32[4,8,2,4,2,8,128]{6,5,4,3,2,1,0:T(8,128)S(1)} %copy-done.3, f32[16,2,2,2,2,8,128]{6,5,4,3,2,1,0:T(8,128)S(1)} %all-to-all-done.5.cols_ref, f32[2,256,256]{2,1,0:T(8,128)S(1)} %copy-done.9, ...), custom_call_target="tpu_custom_call" | custom-call | flops 10000000000 | bytes 10000000 | tf_op jit(solution)/shard_map/pallas_call | solution.py:397
  (34 shorter events, 4.5 us)
Async XLA Ops:
  1.5 30.8 %copy-start.6 = (s32[3]{0:T(128)}, s32[3]{0:T(128)S(1)}, u32[]{:S(2)}) copy-start(s32[3]{0:T(128)S(1)} %pad_add_fusion.scal) | copy-start | bytes 40
  1.5 1.6 copy-start
  32.3 31.1 %all-to-all-start.2 = ((f32[32,8,8,128]{3,2,1,0:T(8,128)}), f32[32,8,8,128]{3,2,1,0:T(8,128)S(1)}, u32[]{:S(2)}, u32[]{:S(2)}) async-start(f32[32,8,8,128]{3,2,1,0:T(8,128)} %get-tuple-element.18), calls=%async_computation.2 | async-start | bytes 2097152 | tf_op jit(solution)/shard_map/all_to_all | solution.py:434
  63.4 9.5 %copy-start.12 = (f32[32,8,8,128]{3,2,1,0:T(8,128)}, f32[32,8,8,128]{3,2,1,0:T(8,128)S(1)}, u32[]{:S(2)}) copy-start(f32[32,8,8,128]{3,2,1,0:T(8,128)S(1)} %all-to-all-done.2.first_ref.second_ref) | copy-start | bytes 3145732
  63.4 31.1 %all-to-all-start.1 = ((f32[32,6,8,128]{3,2,1,0:T(8,128)}), f32[32,6,8,128]{3,2,1,0:T(8,128)S(1)}, u32[]{:S(2)}, u32[]{:S(2)}) async-start(f32[32,6,8,128]{3,2,1,0:T(8,128)} %shard_map.39), calls=%async_computation.1 | async-start | bytes 1572864 | tf_op jit(solution)/shard_map/all_to_all | solution.py:436
  94.5 29.4 %copy-start.4 = (f32[32,6,8,128]{3,2,1,0:T(8,128)}, f32[32,6,8,128]{3,2,1,0:T(8,128)S(1)}, u32[]{:S(2)}) copy-start(f32[32,6,8,128]{3,2,1,0:T(8,128)S(1)} %all-to-all-done.1.d_ref) | copy-start | bytes 2359300
  94.5 27.8 %all-to-all-start.3 = ((f32[8,2,4,2,8,128]{5,4,3,2,1,0:T(8,128)}), f32[8,2,4,2,8,128]{5,4,3,2,1,0:T(8,128)S(1)}, u32[]{:S(2)}, u32[]{:S(2)}) async-start(f32[8,2,4,2,8,128]{5,4,3,2,1,0:T(8,128)} %get-tuple-element.21), calls=%async_computation.3 | async-start | bytes 1048576 | tf_op jit(solution)/shard_map/all_to_all | solution.py:442
  98.3 12.0 %collective-permute-start = (f32[2,2,2,8,128]{4,3,2,1,0:T(8,128)}, f32[2,2,2,8,128]{4,3,2,1,0:T(8,128)S(1)}, u32[]{:S(2)}, u32[]{:S(2)}) collective-permute-start(f32[2,2,2,8,128]{4,3,2,1,0:T(8,128)} %get-tuple-element.19), channel_id=1, source_target_pairs={{0,0},{1,32},{2,64},{3,96},{4,128},{5,160},{6,192},{7,224},{8,256}... | collective-permute-start | bytes 98312 | tf_op jit(solution)/shard_map/ppermute | solution.py:440
  103.1 19.2 %collective-permute-start.1 = (f32[2,2,2,8,128]{4,3,2,1,0:T(8,128)}, f32[2,2,2,8,128]{4,3,2,1,0:T(8,128)S(1)}, u32[]{:S(2)}, u32[]{:S(2)}) collective-permute-start(f32[2,2,2,8,128]{4,3,2,1,0:T(8,128)} %get-tuple-element.20), channel_id=1, source_target_pairs={{0,16},{1,48},{2,80},{3,112},{4,144},{5,176},{6,208},{7,240},{8,27... | collective-permute-start | bytes 98312 | tf_op jit(solution)/shard_map/ppermute | solution.py:441
  110.3 13.6 %copy-start.13 = (f32[2,2,2,8,128]{4,3,2,1,0:T(8,128)}, f32[2,2,2,8,128]{4,3,2,1,0:T(8,128)S(1)}, u32[]{:S(2)}) copy-start(f32[2,2,2,8,128]{4,3,2,1,0:T(8,128)S(1)} %collective-permute-done.first_ref) | copy-start | bytes 98308
  122.3 1.6 copy-start.14
  123.9 30.0 %all-to-all-start.4 = ((f32[4,8,2,4,2,8,128]{6,5,4,3,2,1,0:T(8,128)}), f32[4,8,2,4,2,8,128]{6,5,4,3,2,1,0:T(8,128)S(1)}, u32[]{:S(2)}, u32[]{:S(2)}) async-start(f32[4,8,2,4,2,8,128]{6,5,4,3,2,1,0:T(8,128)} %broadcast_in_dim.2), calls=%async_computation.4 | async-start | bytes 4194304 | tf_op jit(solution)/shard_map/all_to_all | solution.py:446
  127.5 30.8 %copy-start.7 = (s32[3]{0:T(128)S(1)}, s32[3]{0:T(128)}, u32[]{:S(2)}) copy-start(s32[3]{0:T(128)} %copy-done.6) | copy-start | bytes 40
  153.9 4.4 %copy-start.2 = (f32[4,8,2,4,2,8,128]{6,5,4,3,2,1,0:T(8,128)}, f32[4,8,2,4,2,8,128]{6,5,4,3,2,1,0:T(8,128)S(1)}, u32[]{:S(2)}) copy-start(f32[4,8,2,4,2,8,128]{6,5,4,3,2,1,0:T(8,128)S(1)} %all-to-all-done.4.rows_ref) | copy-start | bytes 6291460
  153.9 33.4 %all-to-all-start.5 = ((f32[16,2,2,2,2,8,128]{6,5,4,3,2,1,0:T(8,128)}), f32[16,2,2,2,2,8,128]{6,5,4,3,2,1,0:T(8,128)S(1)}, u32[]{:S(2)}, u32[]{:S(2)}) async-start(f32[16,2,2,2,2,8,128]{6,5,4,3,2,1,0:T(8,128)} %shard_map.41), calls=%async_computation.5 | async-start | bytes 2097152 | tf_op jit(solution)/shard_map/all_to_all | solution.py:445
  158.4 1.1 copy-start.5
  159.5 27.9 %copy-start.1 = (f32[4,1,256,2,1,256]{5,4,3,2,1,0:T(1,128)S(1)}, f32[4,1,256,2,1,256]{5,4,3,2,1,0:T(1,128)}, u32[]{:S(2)}) copy-start(f32[4,1,256,2,1,256]{5,4,3,2,1,0:T(1,128)} %param.3) | copy-start | bytes 6291460
  185.7 0.8 copy-start.8
  186.5 0.8 copy-start.10
  187.4 1.6 copy-start.3
  189.0 1.0 copy-start.9
  190.0 1.0 copy-start.11

commit v3 on v2

--- a/solution.py
+++ b/solution.py
@@ -103,15 +103,15 @@
     )(scal, received, received)
 
 
-def copies_kernel(scal, here_ref, below_ref, out_ref):
-    out_ref[:, 0:2] = jnp.broadcast_to(here_ref[:, 0:2], (N_COL, 2, 8, HALF))
-    out_ref[:, 2:6] = jnp.broadcast_to(below_ref[:, 0:4], (N_COL, 4, 8, HALF))
-
-
-def diag_copies(scal, seen):
+def choose_kernel(scal, here_ref, below_ref, out_ref):
+    out_ref[0:2] = here_ref[0, 0:2]
+    out_ref[2:6] = below_ref[0, 0:4]
+
+
+def diag_choice(scal, seen):
     block = (1, 5, 8, HALF)
     return pl.pallas_call(
-        copies_kernel,
+        choose_kernel,
         grid_spec=pltpu.PrefetchScalarGridSpec(
             num_scalar_prefetch=1,
             grid=(1,),
@@ -121,7 +121,7 @@
             ],
             out_specs=VMEM,
         ),
-        out_shape=jax.ShapeDtypeStruct((N_COL, 6, 8, HALF), f32),
+        out_shape=jax.ShapeDtypeStruct((6, 8, HALF), f32),
     )(scal, seen, seen)
 
 
@@ -130,9 +130,7 @@
     for t, ref in enumerate((first_ref, second_ref)):
         for r in range(4):
             for h in range(2):
-                part = ref[0, 2 * r + h]
-                for z in range(8):
-                    bulk_ref[z, t, r, h] = part
+                bulk_ref[t, r, h] = ref[0, 2 * r + h]
         for c in range(2):
             for h in range(2):
                 even = ref[0, 4 * c + h]
@@ -155,7 +153,7 @@
             out_specs=[VMEM, VMEM, VMEM],
         ),
         out_shape=[
-            jax.ShapeDtypeStruct((8, 2, 4, 2, 8, HALF), f32),
+            jax.ShapeDtypeStruct((2, 4, 2, 8, HALF), f32),
             jax.ShapeDtypeStruct((2, 2, 2, 8, HALF), f32),
             jax.ShapeDtypeStruct((2, 2, 2, 8, HALF), f32),
         ],
@@ -165,20 +163,48 @@
 def cols_kernel(scal, first_ref, second_ref, out_ref):
     low = scal[2] < N_ROW
     first, second = first_ref[...], second_ref[...]
-    lo = jnp.where(low, first, second)
-    hi = jnp.where(low, second, first)
-    for y in range(N_ROW):
-        out_ref[y, 0] = lo
-        out_ref[y, 1] = hi
-
-
-def col_copies(scal, first, second):
+    out_ref[0] = jnp.where(low, first, second)
+    out_ref[1] = jnp.where(low, second, first)
+
+
+def order_cols(scal, first, second):
     return pl.pallas_call(
         cols_kernel,
         in_specs=[SMEM, VMEM, VMEM],
         out_specs=VMEM,
-        out_shape=jax.ShapeDtypeStruct((N_ROW, 2, 2, 2, 2, 8, HALF), f32),
+        out_shape=jax.ShapeDtypeStruct((2, 2, 2, 2, 8, HALF), f32),
     )(scal, first, second)
+
+
+def line_kernel(scal, *refs):
+    z = scal[2] // 4
+    for d in range(8):
+        refs[8][(z + 8 - d) % 8] = refs[d][...]
+
+
+def z_line(scal, part):
+    shifts = [
+        lax.ppermute(part, "col", [(i, (i + 4 * d) % N_COL) for i in range(N_COL)])
+        for d in range(1, 8)
+    ]
+    return [part] + shifts
+
+
+def in_order(scal, parts):
+    return pl.pallas_call(
+        line_kernel,
+        in_specs=[SMEM] + [VMEM] * 8,
+        out_specs=VMEM,
+        out_shape=jax.ShapeDtypeStruct((8,) + parts[0].shape, f32),
+    )(scal, *parts)
+
+
+def x_line(slab):
+    shifts = [
+        lax.ppermute(slab, "col", [(i, i - i % 4 + (i + d) % 4) for i in range(N_COL)])
+        for d in range(1, 4)
+    ]
+    return [slab] + shifts
 
 
 def factor_half(block):
@@ -227,8 +253,12 @@
     return jnp.concatenate(upper, 0), jnp.concatenate(lower_inv, 0)
 
 
-def factor_kernel(scal, lev, d_ref, l_ref, li_ref, p_ref, s_ref, u_ref, v_ref):
-    k = scal[0]
+def factor_kernel(scal, lev, d0, d1, d2, d3, out_ref, d_ref, s_ref, u_ref, v_ref):
+    k, x = scal[0], scal[2] % 4
+    for d, ref in enumerate((d0, d1, d2, d3)):
+        from_x = (x + 4 - d) % 4
+        for z in range(8):
+            d_ref[4 * z + from_x] = ref[z]
 
     def tile(n):
         return jnp.concatenate([d_ref[:, 2 * n + h].reshape(B, HALF) for h in range(2)], axis=1)
@@ -254,20 +284,20 @@
         l21 = s_ref[HALF:, 0:HALF]
         zero = jnp.zeros((HALF, HALF), f32)
         v0, v1 = v_ref[0], v_ref[1]
-        l_ref[t, 0:HALF, 0:HALF] = u_ref[0].T
-        l_ref[t, 0:HALF, HALF:] = zero
-        l_ref[t, HALF:, 0:HALF] = l21
-        l_ref[t, HALF:, HALF:] = u_ref[1].T
-        li_ref[t, 0:HALF, 0:HALF] = v0
-        li_ref[t, 0:HALF, HALF:] = zero
-        li_ref[t, HALF:, 0:HALF] = -dot_nn(v1, dot_nn(l21, v0))
-        li_ref[t, HALF:, HALF:] = v1
+        out_ref[t, 0:HALF, 0:HALF] = u_ref[0].T
+        out_ref[t, 0:HALF, HALF:] = zero
+        out_ref[t, HALF:, 0:HALF] = l21
+        out_ref[t, HALF:, HALF:] = u_ref[1].T
+        out_ref[2 + t, 0:HALF, 0:HALF] = v0
+        out_ref[2 + t, 0:HALF, HALF:] = zero
+        out_ref[2 + t, HALF:, 0:HALF] = -dot_nn(v1, dot_nn(l21, v0))
+        out_ref[2 + t, HALF:, HALF:] = v1
 
         @pl.when(t == 0)
         def _():
             below = k + 1
-            solved = by_level(dot_nt(tile(1), li_ref[0]), lev[below % N_ROW, below // N_ROW])
-            p_ref[...] = solved
+            solved = by_level(dot_nt(tile(1), out_ref[2]), lev[below % N_ROW, below // N_ROW])
+            out_ref[4] = solved
             s_ref[...] = tile(2) - dot_nt(solved, solved)
 
         return 0
@@ -275,27 +305,28 @@
     lax.fori_loop(0, 2, step, 0)
 
 
-def factor_two(scal, lev, diag):
-    pair = jax.ShapeDtypeStruct((2, B, B), f32)
+def factor_two(scal, lev, diags):
     return pl.pallas_call(
         factor_kernel,
-        in_specs=[SMEM, SMEM, VMEM],
-        out_specs=[VMEM] * 3,
-        out_shape=[pair, pair, jax.ShapeDtypeStruct((B, B), f32)],
+        in_specs=[SMEM, SMEM] + [VMEM] * 4,
+        out_specs=VMEM,
+        out_shape=jax.ShapeDtypeStruct((5, B, B), f32),
         scratch_shapes=[
+            pltpu.VMEM((N_COL, 6, 8, HALF), f32),
             pltpu.VMEM((B, B), f32),
             pltpu.VMEM((2, HALF, HALF), f32),
             pltpu.VMEM((2, HALF, HALF), f32),
         ],
         compiler_params=pltpu.CompilerParams(vmem_limit_bytes=8 << 20),
         cost_estimate=pl.CostEstimate(flops=3 * 10**10, bytes_accessed=10**6, transcendentals=0),
-    )(scal, lev, diag)
+    )(scal, lev, *diags)
 
 
 def update_kernel(
-    scal, lev, prec, rows_ref, cols_ref, l_ref, li_ref, p10_ref, mat_ref, out_ref, panel
+    scal, lev, prec, row0, row1, row2, row3, cols_ref, f_ref, mat_ref, out_ref, panel
 ):
     k, p, q = scal[0], scal[1], scal[2]
+    x = q % 4
 
     def level_of(t, i):
         return lev[i % N_ROW, 4 * t + i // N_ROW]
@@ -304,10 +335,10 @@
         for h in range(2):
             lanes = slice(h * HALF, (h + 1) * HALF)
             for r in range(4):
-                for x in range(4):
+                for d, ref in enumerate((row0, row1, row2, row3)):
                     for z in range(8):
-                        at = 8 * (4 * z + x)
-                        panel[t, r, at : at + 8, lanes] = rows_ref[x, z, t, r, h]
+                        at = pl.ds(pl.multiple_of(32 * z + 8 * ((x + 4 - d) % 4), 8), 8)
+                        panel[t, r, at, lanes] = ref[z, t, r, h]
             for c in range(2):
                 for part in range(2):
                     at = slice(part * HALF, (part + 1) * HALF)
@@ -318,18 +349,18 @@
 
         @pl.when(i > k)
         def _():
-            panel[0, n] = by_level(dot_nt(panel[0, n], li_ref[0]), level_of(0, i))
+            panel[0, n] = by_level(dot_nt(panel[0, n], f_ref[2]), level_of(0, i))
             level = level_of(1, i)
 
             @pl.when((i > k + 1) & (level == 2))
             def _():
-                raw = panel[1, n] - dot_nt(panel[0, n], p10_ref[...])
-                panel[1, n] = dot_nt(raw, li_ref[1])
+                raw = panel[1, n] - dot_nt(panel[0, n], f_ref[4])
+                panel[1, n] = dot_nt(raw, f_ref[3])
 
             @pl.when((i > k + 1) & (level == 1))
             def _():
-                raw = rounded(panel[1, n] - dot_narrow(panel[0, n], p10_ref[...]))
-                panel[1, n] = rounded(dot_nt(raw, li_ref[1]))
+                raw = rounded(panel[1, n] - dot_narrow(panel[0, n], f_ref[4]))
+                panel[1, n] = rounded(dot_nt(raw, f_ref[3]))
 
         return 0
 
@@ -386,23 +417,23 @@
 
         @pl.when(diagonal)
         def _():
-            put(l_ref[j - k])
+            put(f_ref[j - k])
 
         return 0
 
     lax.fori_loop(0, 8, trail, 0)
 
 
-def update(scal, lev, prec, row_tiles, col_tiles, factors, inverses, p10, mat):
+def update(scal, lev, prec, row_tiles, col_tiles, factors, mat):
     return pl.pallas_call(
         update_kernel,
-        in_specs=[SMEM, SMEM, SMEM] + [VMEM] * 6,
+        in_specs=[SMEM, SMEM, SMEM] + [VMEM] * 7,
         out_specs=VMEM,
         out_shape=jax.ShapeDtypeStruct(mat.shape, f32),
         scratch_shapes=[pltpu.VMEM((2, 6, B, B), f32)],
         compiler_params=pltpu.CompilerParams(vmem_limit_bytes=12 << 20),
         cost_estimate=pl.CostEstimate(flops=10**10, bytes_accessed=10**7, transcendentals=0),
-    )(scal, lev, prec, row_tiles, col_tiles, factors, inverses, p10, mat)
+    )(scal, lev, prec, *row_tiles, col_tiles, factors, mat)
 
 
 def cross_pairs(odd):
@@ -425,31 +456,26 @@
     prec = precision.reshape(4, 2)
     mat = matrix.reshape(4096, HALF)
 
-    z_groups = [[4 * z + x for z in range(8)] for x in range(4)]
-    x_groups = [[4 * z + x for x in range(4)] for z in range(8)]
-
     sent_diag, sent_bulk = pack(scal, prec, mat)
     got_diag = lax.all_to_all(sent_diag, "col", 0, 0)
     seen = lax.all_gather(diag_parts(scal, got_diag), "row")
     got_bulk = lax.all_to_all(sent_bulk, "col", 0, 0)
     bulk, even, odd = route(scal, got_bulk)
-    diags = lax.all_to_all(diag_copies(scal, seen), "col", 0, 0)
     lev = seen[:, 4, :, 0].astype(jnp.int32)
 
     both = ("row", "col")
     first = lax.ppermute(even, both, cross_pairs(False))
     second = lax.ppermute(odd, both, cross_pairs(True))
-    slab = lax.all_to_all(bulk, "col", 0, 0, axis_index_groups=z_groups)
-    diags, first, second, slab = lax.optimization_barrier((diags, first, second, slab))
-
-    col_tiles = lax.all_to_all(col_copies(scal, first, second), "row", 0, 0)
-    row_tiles = lax.all_to_all(
-        jnp.broadcast_to(slab[None], (4,) + slab.shape), "col", 0, 0, axis_index_groups=x_groups
-    )
-    factors, inverses, p10 = factor_two(scal, lev, diags)
-    out = update(
-        scal, lev, prec, row_tiles, col_tiles, factors, inverses, p10, mat
-    )
+    col_tiles = lax.all_gather(order_cols(scal, first, second), "row")
+
+    diag_line = z_line(scal, diag_choice(scal, seen))
+    diag_slab = in_order(scal, diag_line)
+    slab = in_order(scal, z_line(scal, bulk))
+    diag_slab, slab = lax.optimization_barrier((diag_slab, slab))
+    diags = x_line(diag_slab)
+    row_tiles = x_line(slab)
+    factors = factor_two(scal, lev, diags)
+    out = update(scal, lev, prec, row_tiles, col_tiles, factors, mat)
     return out.reshape(matrix.shape)
 
 

time: 196 us -> 220 us (1.12)
  waiting for transfers between devices: 54.8 us -> 3.19 us
  starting transfers between devices: 38.3 us -> 86.5 us
  between operations: 0.78 us -> 14.6 us
  Pallas kernels: 40.6 us -> 47.1 us
  local copies, waits for them, and re-layouts: 10.5 us -> 15.7 us
    ppermute x0 -> x20, starting transfers between devices: none -> 68.7 us  [the longest x14 51.4 us: z_line(): lax.ppermute(part, 'col', [(i, (i + 4 * d) % N_COL) for i in range(N_COL)])]
    all_to_all x4 -> x0, waiting for transfers between devices: 42.8 us -> none  [the longest x1 23.5 us: per_device(): lax.all_to_all(jnp.broadcast_to(slab[None], (4,) + slab.shape), 'col', 0,...]
    all_to_all x4 -> x0, starting transfers between devices: 21.4 us -> none  [the longest x1 9.5 us: per_device(): diags = lax.all_to_all(diag_copies(scal, seen), 'col', 0, 0)]
    ppermute x1, waiting for transfers between devices: 12 us -> 0.01 us  [per_device(): second = lax.ppermute(odd, both, cross_pairs(True))]
    pallas_call x4 -> x6, Pallas kernels: 34.5 us -> 41.3 us  [the longest x1 26.3 us: factor_two(): pl.pallas_call(factor_kernel, in_specs=[SMEM, SMEM] + [VMEM] * 4, out_spe...]
    unnamed x30 -> x66, local copies, waits for them, and re-layouts: 8.04 us -> 14.8 us
    all_gather x0 -> x1, waiting for transfers between devices: none -> 3.11 us  [per_device(): col_tiles = lax.all_gather(order_cols(scal, first, second), 'row')]
  transfers between devices with their start and end apart: 7 -> 24, of which waited for: 3 -> 1; matrix products, arithmetic and copies ran while one was open for 1% -> 0% of each run, Pallas kernels for 18% -> 17%
where the time goes in v3:
time: 220 us; the launch traced here: 217 us
  starting transfers between devices  86.5 us (39%)
  blocking collectives  49.1 us (22%)
  Pallas kernels  47.1 us (21%)
  local copies, waits for them, and re-layouts  15.7 us (7%)
  between operations  14.6 us (7%)
  waiting for transfers between devices  3.19 us (1%)
    ppermute x14, starting transfers between devices, z_line(): lax.ppermute(part, 'col', [(i, (i + 4 * d) % N_COL) for i in range(N_COL)])  51.4 us
    all_to_all x1, blocking collectives, per_device(): got_diag = lax.all_to_all(sent_diag, 'col', 0, 0)  27.4 us
    pallas_call x1, Pallas kernels, factor_two(): pl.pallas_call(factor_kernel, in_specs=[SMEM, SMEM] + [VMEM] * 4, out_spe...  26.3 us
    all_gather x1, blocking collectives, per_device(): seen = lax.all_gather(diag_parts(scal, got_diag), 'row')  21.7 us
    ppermute x6, starting transfers between devices, x_line(): lax.ppermute(slab, 'col', [(i, i - i % 4 + (i + d) % 4) for i in range(N_...  17.3 us
    unnamed x66, local copies, waits for them, and re-layouts  14.8 us
    pallas_call x1, Pallas kernels, update(): pl.pallas_call(update_kernel, in_specs=[SMEM, SMEM, SMEM] + [VMEM] * 7, o...  8.02 us
    ppermute x1, starting transfers between devices, per_device(): first = lax.ppermute(even, both, cross_pairs(False))  6.79 us
  transfers between devices with their start and end apart: 24, of which 1 were waited for; matrix products, arithmetic and copies ran while one was open for 0% of the time, Pallas kernels for 17%

profile of v3, /device:TPU:1, one launch (start us, length us, event | category | flops | bytes accessed | tf_op | source)
XLA Modules:
  0.0 217.2 jit_solution(9196321786141633642)
XLA Ops:
  11.4 27.4 %all_to_all.10.first_ref.second_ref = f32[32,3,8,128]{3,2,1,0:T(8,128)} all-to-all(f32[32,3,8,128]{3,2,1,0:T(8,128)S(1)} %get-tuple-element.12), channel_id=1, replica_groups=mesh['row'=16,'col'=32] {'col'}, dimensions={0} | all-to-all | bytes 786432 | tf_op jit(solution)/shard_map/all_to_all | solution.py:460
  38.8 5.0 %all-to-all-start.1 = ((f32[32,8,8,128]{3,2,1,0:T(8,128)}), f32[32,8,8,128]{3,2,1,0:T(8,128)S(1)}, u32[]{:S(2)}, u32[]{:S(2)}) async-start(f32[32,8,8,128]{3,2,1,0:T(8,128)} %get-tuple-element.13), calls=%async_computation.1 | async-start | bytes 2097152 | tf_op jit(solution)/shard_map/all_to_all | solution.py:462
  45.9 21.7 %all-gather = f32[80,8,128]{2,1,0:T(8,128)} all-gather(f32[5,8,128]{2,1,0:T(8,128)} %shard_map.38), channel_id=2, replica_groups=mesh['row'=16,'col'=32] {'row'}, dimensions={0}, use_global_device_ids=true | all-gather | bytes 348160 | tf_op jit(solution)/shard_map/all_gather | solution.py:461
  69.6 4.8 %collective-permute-start.6 = (f32[6,8,128]{2,1,0:T(8,128)}, f32[6,8,128]{2,1,0:T(8,128)S(1)}, u32[]{:S(2)}, u32[]{:S(2)}) collective-permute-start(f32[6,8,128]{2,1,0:T(8,128)} %shard_map.39.refs_0_), channel_id=1, source_target_pairs={{0,28},{1,29},{2,30},{3,31},{4,0},{5,1},{6,2},{7,3},{8,4},{9,5},{1... | collective-permute-start | bytes 73736 | tf_op jit(solution)/shard_map/ppermute | solution.py:187
  77.5 3.1 %collective-permute-start.13 = (f32[2,4,2,8,128]{4,3,2,1,0:T(8,128)}, f32[2,4,2,8,128]{4,3,2,1,0:T(8,128)S(1)}, u32[]{:S(2)}, u32[]{:S(2)}) collective-permute-start(f32[2,4,2,8,128]{4,3,2,1,0:T(8,128)} %get-tuple-element.14.refs_0_), channel_id=1, source_target_pairs={{0,28},{1,29},{2,30},{3,31},{4,0},{5,1},{6,2},{7,3},{8,4},{9,5},{1... | collective-permute-start | bytes 196616 | tf_op jit(solution)/shard_map/ppermute | solution.py:187
  80.5 4.0 %collective-permute-start.12 = (f32[2,4,2,8,128]{4,3,2,1,0:T(8,128)}, f32[2,4,2,8,128]{4,3,2,1,0:T(8,128)S(1)}, u32[]{:S(2)}, u32[]{:S(2)}) collective-permute-start(f32[2,4,2,8,128]{4,3,2,1,0:T(8,128)} %get-tuple-element.14.refs_0_), channel_id=1, source_target_pairs={{0,24},{1,25},{2,26},{3,27},{4,28},{5,29},{6,30},{7,31},{8,0},{9,1... | collective-permute-start | bytes 196616 | tf_op jit(solution)/shard_map/ppermute | solution.py:187
  86.7 4.4 %collective-permute-start.4 = (f32[6,8,128]{2,1,0:T(8,128)S(1)}, f32[6,8,128]{2,1,0:T(8,128)S(1)}, u32[]{:S(2)}, u32[]{:S(2)}) collective-permute-start(f32[6,8,128]{2,1,0:T(8,128)S(1)} %copy-done.16), channel_id=1, source_target_pairs={{0,20},{1,21},{2,22},{3,23},{4,24},{5,25},{6,26},{7,27},{8,28},{9,... | collective-permute-start | bytes 73736 | tf_op jit(solution)/shard_map/ppermute | solution.py:187
  91.1 4.8 %collective-permute-start.3 = (f32[6,8,128]{2,1,0:T(8,128)S(1)}, f32[6,8,128]{2,1,0:T(8,128)S(1)}, u32[]{:S(2)}, u32[]{:S(2)}) collective-permute-start(f32[6,8,128]{2,1,0:T(8,128)S(1)} %copy-done.16), channel_id=1, source_target_pairs={{0,16},{1,17},{2,18},{3,19},{4,20},{5,21},{6,22},{7,23},{8,24},{9,... | collective-permute-start | bytes 73736 | tf_op jit(solution)/shard_map/ppermute | solution.py:187
  95.9 3.1 %collective-permute-start.2 = (f32[6,8,128]{2,1,0:T(8,128)S(1)}, f32[6,8,128]{2,1,0:T(8,128)S(1)}, u32[]{:S(2)}, u32[]{:S(2)}) collective-permute-start(f32[6,8,128]{2,1,0:T(8,128)S(1)} %copy-done.16), channel_id=1, source_target_pairs={{0,12},{1,13},{2,14},{3,15},{4,16},{5,17},{6,18},{7,19},{8,20},{9,... | collective-permute-start | bytes 73736 | tf_op jit(solution)/shard_map/ppermute | solution.py:187
  101.1 3.4 %collective-permute-start = (f32[6,8,128]{2,1,0:T(8,128)S(1)}, f32[6,8,128]{2,1,0:T(8,128)S(1)}, u32[]{:S(2)}, u32[]{:S(2)}) collective-permute-start(f32[6,8,128]{2,1,0:T(8,128)S(1)} %copy-done.16), channel_id=1, source_target_pairs={{0,4},{1,5},{2,6},{3,7},{4,8},{5,9},{6,10},{7,11},{8,12},{9,13},{1... | collective-permute-start | bytes 73736 | tf_op jit(solution)/shard_map/ppermute | solution.py:187
  104.5 5.1 %collective-permute-start.11 = (f32[2,4,2,8,128]{4,3,2,1,0:T(8,128)}, f32[2,4,2,8,128]{4,3,2,1,0:T(8,128)S(1)}, u32[]{:S(2)}, u32[]{:S(2)}) collective-permute-start(f32[2,4,2,8,128]{4,3,2,1,0:T(8,128)} %get-tuple-element.14.refs_0_), channel_id=1, source_target_pairs={{0,20},{1,21},{2,22},{3,23},{4,24},{5,25},{6,26},{7,27},{8,28},{9,... | collective-permute-start | bytes 196616 | tf_op jit(solution)/shard_map/ppermute | solution.py:187
  109.7 3.9 %collective-permute-start.10 = (f32[2,4,2,8,128]{4,3,2,1,0:T(8,128)}, f32[2,4,2,8,128]{4,3,2,1,0:T(8,128)S(1)}, u32[]{:S(2)}, u32[]{:S(2)}) collective-permute-start(f32[2,4,2,8,128]{4,3,2,1,0:T(8,128)} %get-tuple-element.14.refs_0_), channel_id=1, source_target_pairs={{0,16},{1,17},{2,18},{3,19},{4,20},{5,21},{6,22},{7,23},{8,24},{9,... | collective-permute-start | bytes 196616 | tf_op jit(solution)/shard_map/ppermute | solution.py:187
  113.6 4.0 %collective-permute-start.9 = (f32[2,4,2,8,128]{4,3,2,1,0:T(8,128)}, f32[2,4,2,8,128]{4,3,2,1,0:T(8,128)S(1)}, u32[]{:S(2)}, u32[]{:S(2)}) collective-permute-start(f32[2,4,2,8,128]{4,3,2,1,0:T(8,128)} %get-tuple-element.14.refs_0_), channel_id=1, source_target_pairs={{0,12},{1,13},{2,14},{3,15},{4,16},{5,17},{6,18},{7,19},{8,20},{9,... | collective-permute-start | bytes 196616 | tf_op jit(solution)/shard_map/ppermute | solution.py:187
  117.7 4.7 %collective-permute-start.8 = (f32[2,4,2,8,128]{4,3,2,1,0:T(8,128)}, f32[2,4,2,8,128]{4,3,2,1,0:T(8,128)S(1)}, u32[]{:S(2)}, u32[]{:S(2)}) collective-permute-start(f32[2,4,2,8,128]{4,3,2,1,0:T(8,128)} %get-tuple-element.14.refs_0_), channel_id=1, source_target_pairs={{0,8},{1,9},{2,10},{3,11},{4,12},{5,13},{6,14},{7,15},{8,16},{9,17... | collective-permute-start | bytes 196616 | tf_op jit(solution)/shard_map/ppermute | solution.py:187
  126.0 6.8 %collective-permute-start.17 = (f32[2,2,2,8,128]{4,3,2,1,0:T(8,128)}, f32[2,2,2,8,128]{4,3,2,1,0:T(8,128)S(1)}, u32[]{:S(2)}, u32[]{:S(2)}) collective-permute-start(f32[2,2,2,8,128]{4,3,2,1,0:T(8,128)} %get-tuple-element.16), channel_id=1, source_target_pairs={{0,0},{1,32},{2,64},{3,96},{4,128},{5,160},{6,192},{7,224},{8,256}... | collective-permute-start | bytes 98312 | tf_op jit(solution)/shard_map/ppermute | solution.py:467
  132.8 6.0 %collective-permute-start.18 = (f32[2,2,2,8,128]{4,3,2,1,0:T(8,128)}, f32[2,2,2,8,128]{4,3,2,1,0:T(8,128)S(1)}, u32[]{:S(2)}, u32[]{:S(2)}) collective-permute-start(f32[2,2,2,8,128]{4,3,2,1,0:T(8,128)} %get-tuple-element.17), channel_id=1, source_target_pairs={{0,16},{1,48},{2,80},{3,112},{4,144},{5,176},{6,208},{7,240},{8,27... | collective-permute-start | bytes 98312 | tf_op jit(solution)/shard_map/ppermute | solution.py:468
  142.0 3.0 %collective-permute-start.21 = (f32[8,6,8,128]{3,2,1,0:T(8,128)}, f32[8,6,8,128]{3,2,1,0:T(8,128)S(1)}, u32[]{:S(2)}, u32[]{:S(2)}) collective-permute-start(f32[8,6,8,128]{3,2,1,0:T(8,128)} %shard_map.40.d0), channel_id=1, source_target_pairs={{0,3},{1,0},{2,1},{3,2},{4,7},{5,4},{6,5},{7,6},{8,11},{9,8},{10,9... | collective-permute-start | bytes 589832 | tf_op jit(solution)/shard_map/ppermute | solution.py:204
  147.2 2.8 %collective-permute-start.19 = (f32[8,6,8,128]{3,2,1,0:T(8,128)}, f32[8,6,8,128]{3,2,1,0:T(8,128)S(1)}, u32[]{:S(2)}, u32[]{:S(2)}) collective-permute-start(f32[8,6,8,128]{3,2,1,0:T(8,128)} %shard_map.40.d0), channel_id=1, source_target_pairs={{0,1},{1,2},{2,3},{3,0},{4,5},{5,6},{6,7},{7,4},{8,9},{9,10},{10,1... | collective-permute-start | bytes 589832 | tf_op jit(solution)/shard_map/ppermute | solution.py:204
  153.6 3.7 %collective-permute-start.16 = (f32[8,2,4,2,8,128]{5,4,3,2,1,0:T(8,128)}, f32[8,2,4,2,8,128]{5,4,3,2,1,0:T(8,128)S(1)}, u32[]{:S(2)}, u32[]{:S(2)}) collective-permute-start(f32[8,2,4,2,8,128]{5,4,3,2,1,0:T(8,128)} %shard_map.42.row0), channel_id=1, source_target_pairs={{0,3},{1,0},{2,1},{3,2},{4,7},{5,4},{6,5},{7,6},{8,11},{9,8},{10,9... | collective-permute-start | bytes 1572872 | tf_op jit(solution)/shard_map/ppermute | solution.py:204
  157.3 3.4 %collective-permute-start.15 = (f32[8,2,4,2,8,128]{5,4,3,2,1,0:T(8,128)}, f32[8,2,4,2,8,128]{5,4,3,2,1,0:T(8,128)S(1)}, u32[]{:S(2)}, u32[]{:S(2)}) collective-permute-start(f32[8,2,4,2,8,128]{5,4,3,2,1,0:T(8,128)} %shard_map.42.row0), channel_id=1, source_target_pairs={{0,2},{1,3},{2,0},{3,1},{4,6},{5,7},{6,4},{7,5},{8,10},{9,11},{10,... | collective-permute-start | bytes 1572872 | tf_op jit(solution)/shard_map/ppermute | solution.py:204
  160.8 2.3 %collective-permute-start.14 = (f32[8,2,4,2,8,128]{5,4,3,2,1,0:T(8,128)}, f32[8,2,4,2,8,128]{5,4,3,2,1,0:T(8,128)S(1)}, u32[]{:S(2)}, u32[]{:S(2)}) collective-permute-start(f32[8,2,4,2,8,128]{5,4,3,2,1,0:T(8,128)} %shard_map.42.row0), channel_id=1, source_target_pairs={{0,1},{1,2},{2,3},{3,0},{4,5},{5,6},{6,7},{7,4},{8,9},{9,10},{10,1... | collective-permute-start | bytes 1572872 | tf_op jit(solution)/shard_map/ppermute | solution.py:204
  165.6 26.3 %shard_map.44.f_ref = f32[5,256,256]{2,1,0:T(8,128)S(1)} custom-call(s32[3]{0:T(128)S(1)} %copy-done.5, s32[16,8]{1,0:T(8,128)S(1)} %bitcast.11, f32[8,6,8,128]{3,2,1,0:T(8,128)S(1)} %copy-done.3, f32[8,6,8,128]{3,2,1,0:T(8,128)S(1)} %copy-done.12, f32[8,6,8,128]{3,2,1,0:T(8,128)S(1)} %collective-permute-done.20.d2, ...), custom_call_target="tpu_custom_call" | custom-call | flops 30000001024 | bytes 1000000 | tf_op jit(solution)/shard_map/pallas_call | solution.py:309
  194.6 3.1 %all-gather.4.cloned.1.call-done = f32[32,2,2,2,8,128]{5,4,3,2,1,0:T(8,128)} async-done(((f32[2,2,2,2,8,128]{5,4,3,2,1,0:T(8,128)}), f32[32,2,2,2,8,128]{5,4,3,2,1,0:T(8,128)}) %all-gather.4.cloned.1.call-update) | async-done | bytes 1048592 | tf_op jit(solution)/shard_map/all_gather | solution.py:469
  202.3 8.0 %shard_map.45 = f32[4096,128]{1,0:T(8,128)} custom-call(s32[3]{0:T(128)S(1)} %copy-done.5, s32[16,8]{1,0:T(8,128)S(1)} %bitcast.12, s32[4,2]{1,0:T(4,128)S(1)} %copy.16.prec, f32[8,2,4,2,8,128]{5,4,3,2,1,0:T(8,128)S(1)} %copy-done.2, f32[8,2,4,2,8,128]{5,4,3,2,1,0:T(8,128)S(1)} %copy-done.10, f32[8,2,4,2,8,128]{5,4,3,2,1,0:T(8,128)S(1)} %copy-done.8, ...), custom_call_target="tpu_custom_call" | custom-call | flops 10000000000 | bytes 10000000 | tf_op jit(solution)/shard_map/pallas_call | solution.py:428
  (106 shorter events, 37.7 us)
Async XLA Ops:
  38.8 35.6 %all-to-all-start.1 = ((f32[32,8,8,128]{3,2,1,0:T(8,128)}), f32[32,8,8,128]{3,2,1,0:T(8,128)S(1)}, u32[]{:S(2)}, u32[]{:S(2)}) async-start(f32[32,8,8,128]{3,2,1,0:T(8,128)} %get-tuple-element.13), calls=%async_computation.1 | async-start | bytes 2097152 | tf_op jit(solution)/shard_map/all_to_all | solution.py:462
  43.8 153.8 %all-gather.4.cloned.1.call-start = ((), (), s32[]{:S(2)}) async-start(), calls=%async_computation.2 | async-start | bytes 1114112 | tf_op jit(solution)/shard_map/all_gather | solution.py:469
  69.6 21.5 %collective-permute-start.6 = (f32[6,8,128]{2,1,0:T(8,128)}, f32[6,8,128]{2,1,0:T(8,128)S(1)}, u32[]{:S(2)}, u32[]{:S(2)}) collective-permute-start(f32[6,8,128]{2,1,0:T(8,128)} %shard_map.39.refs_0_), channel_id=1, source_target_pairs={{0,28},{1,29},{2,30},{3,31},{4,0},{5,1},{6,2},{7,3},{8,4},{9,5},{1... | collective-permute-start | bytes 73736 | tf_op jit(solution)/shard_map/ppermute | solution.py:187
  77.5 40.2 %collective-permute-start.13 = (f32[2,4,2,8,128]{4,3,2,1,0:T(8,128)}, f32[2,4,2,8,128]{4,3,2,1,0:T(8,128)S(1)}, u32[]{:S(2)}, u32[]{:S(2)}) collective-permute-start(f32[2,4,2,8,128]{4,3,2,1,0:T(8,128)} %get-tuple-element.14.refs_0_), channel_id=1, source_target_pairs={{0,28},{1,29},{2,30},{3,31},{4,0},{5,1},{6,2},{7,3},{8,4},{9,5},{1... | collective-permute-start | bytes 196616 | tf_op jit(solution)/shard_map/ppermute | solution.py:187
  80.5 41.8 %collective-permute-start.12 = (f32[2,4,2,8,128]{4,3,2,1,0:T(8,128)}, f32[2,4,2,8,128]{4,3,2,1,0:T(8,128)S(1)}, u32[]{:S(2)}, u32[]{:S(2)}) collective-permute-start(f32[2,4,2,8,128]{4,3,2,1,0:T(8,128)} %get-tuple-element.14.refs_0_), channel_id=1, source_target_pairs={{0,24},{1,25},{2,26},{3,27},{4,28},{5,29},{6,30},{7,31},{8,0},{9,1... | collective-permute-start | bytes 196616 | tf_op jit(solution)/shard_map/ppermute | solution.py:187
  84.5 11.4 %collective-permute-start.5 = (f32[6,8,128]{2,1,0:T(8,128)S(1)}, f32[6,8,128]{2,1,0:T(8,128)S(1)}, u32[]{:S(2)}, u32[]{:S(2)}) collective-permute-start(f32[6,8,128]{2,1,0:T(8,128)S(1)} %copy-done.16), channel_id=1, source_target_pairs={{0,24},{1,25},{2,26},{3,27},{4,28},{5,29},{6,30},{7,31},{8,0},{9,1... | collective-permute-start | bytes 73736 | tf_op jit(solution)/shard_map/ppermute | solution.py:187
  86.7 12.4 %collective-permute-start.4 = (f32[6,8,128]{2,1,0:T(8,128)S(1)}, f32[6,8,128]{2,1,0:T(8,128)S(1)}, u32[]{:S(2)}, u32[]{:S(2)}) collective-permute-start(f32[6,8,128]{2,1,0:T(8,128)S(1)} %copy-done.16), channel_id=1, source_target_pairs={{0,20},{1,21},{2,22},{3,23},{4,24},{5,25},{6,26},{7,27},{8,28},{9,... | collective-permute-start | bytes 73736 | tf_op jit(solution)/shard_map/ppermute | solution.py:187
  91.1 9.9 %collective-permute-start.3 = (f32[6,8,128]{2,1,0:T(8,128)S(1)}, f32[6,8,128]{2,1,0:T(8,128)S(1)}, u32[]{:S(2)}, u32[]{:S(2)}) collective-permute-start(f32[6,8,128]{2,1,0:T(8,128)S(1)} %copy-done.16), channel_id=1, source_target_pairs={{0,16},{1,17},{2,18},{3,19},{4,20},{5,21},{6,22},{7,23},{8,24},{9,... | collective-permute-start | bytes 73736 | tf_op jit(solution)/shard_map/ppermute | solution.py:187
  95.9 8.5 %collective-permute-start.2 = (f32[6,8,128]{2,1,0:T(8,128)S(1)}, f32[6,8,128]{2,1,0:T(8,128)S(1)}, u32[]{:S(2)}, u32[]{:S(2)}) collective-permute-start(f32[6,8,128]{2,1,0:T(8,128)S(1)} %copy-done.16), channel_id=1, source_target_pairs={{0,12},{1,13},{2,14},{3,15},{4,16},{5,17},{6,18},{7,19},{8,20},{9,... | collective-permute-start | bytes 73736 | tf_op jit(solution)/shard_map/ppermute | solution.py:187
  99.1 10.6 %collective-permute-start.1 = (f32[6,8,128]{2,1,0:T(8,128)S(1)}, f32[6,8,128]{2,1,0:T(8,128)S(1)}, u32[]{:S(2)}, u32[]{:S(2)}) collective-permute-start(f32[6,8,128]{2,1,0:T(8,128)S(1)} %copy-done.16), channel_id=1, source_target_pairs={{0,8},{1,9},{2,10},{3,11},{4,12},{5,13},{6,14},{7,15},{8,16},{9,17... | collective-permute-start | bytes 73736 | tf_op jit(solution)/shard_map/ppermute | solution.py:187
  101.1 12.6 %collective-permute-start = (f32[6,8,128]{2,1,0:T(8,128)S(1)}, f32[6,8,128]{2,1,0:T(8,128)S(1)}, u32[]{:S(2)}, u32[]{:S(2)}) collective-permute-start(f32[6,8,128]{2,1,0:T(8,128)S(1)} %copy-done.16), channel_id=1, source_target_pairs={{0,4},{1,5},{2,6},{3,7},{4,8},{5,9},{6,10},{7,11},{8,12},{9,13},{1... | collective-permute-start | bytes 73736 | tf_op jit(solution)/shard_map/ppermute | solution.py:187
  104.5 21.5 %collective-permute-start.11 = (f32[2,4,2,8,128]{4,3,2,1,0:T(8,128)}, f32[2,4,2,8,128]{4,3,2,1,0:T(8,128)S(1)}, u32[]{:S(2)}, u32[]{:S(2)}) collective-permute-start(f32[2,4,2,8,128]{4,3,2,1,0:T(8,128)} %get-tuple-element.14.refs_0_), channel_id=1, source_target_pairs={{0,20},{1,21},{2,22},{3,23},{4,24},{5,25},{6,26},{7,27},{8,28},{9,... | collective-permute-start | bytes 196616 | tf_op jit(solution)/shard_map/ppermute | solution.py:187
  109.7 23.1 %collective-permute-start.10 = (f32[2,4,2,8,128]{4,3,2,1,0:T(8,128)}, f32[2,4,2,8,128]{4,3,2,1,0:T(8,128)S(1)}, u32[]{:S(2)}, u32[]{:S(2)}) collective-permute-start(f32[2,4,2,8,128]{4,3,2,1,0:T(8,128)} %get-tuple-element.14.refs_0_), channel_id=1, source_target_pairs={{0,16},{1,17},{2,18},{3,19},{4,20},{5,21},{6,22},{7,23},{8,24},{9,... | collective-permute-start | bytes 196616 | tf_op jit(solution)/shard_map/ppermute | solution.py:187
  113.6 25.2 %collective-permute-start.9 = (f32[2,4,2,8,128]{4,3,2,1,0:T(8,128)}, f32[2,4,2,8,128]{4,3,2,1,0:T(8,128)S(1)}, u32[]{:S(2)}, u32[]{:S(2)}) collective-permute-start(f32[2,4,2,8,128]{4,3,2,1,0:T(8,128)} %get-tuple-element.14.refs_0_), channel_id=1, source_target_pairs={{0,12},{1,13},{2,14},{3,15},{4,16},{5,17},{6,18},{7,19},{8,20},{9,... | collective-permute-start | bytes 196616 | tf_op jit(solution)/shard_map/ppermute | solution.py:187
  117.7 21.1 %collective-permute-start.8 = (f32[2,4,2,8,128]{4,3,2,1,0:T(8,128)}, f32[2,4,2,8,128]{4,3,2,1,0:T(8,128)S(1)}, u32[]{:S(2)}, u32[]{:S(2)}) collective-permute-start(f32[2,4,2,8,128]{4,3,2,1,0:T(8,128)} %get-tuple-element.14.refs_0_), channel_id=1, source_target_pairs={{0,8},{1,9},{2,10},{3,11},{4,12},{5,13},{6,14},{7,15},{8,16},{9,17... | collective-permute-start | bytes 196616 | tf_op jit(solution)/shard_map/ppermute | solution.py:187
  122.4 16.5 %collective-permute-start.7 = (f32[2,4,2,8,128]{4,3,2,1,0:T(8,128)}, f32[2,4,2,8,128]{4,3,2,1,0:T(8,128)S(1)}, u32[]{:S(2)}, u32[]{:S(2)}) collective-permute-start(f32[2,4,2,8,128]{4,3,2,1,0:T(8,128)} %get-tuple-element.14.refs_0_), channel_id=1, source_target_pairs={{0,4},{1,5},{2,6},{3,7},{4,8},{5,9},{6,10},{7,11},{8,12},{9,13},{1... | collective-permute-start | bytes 196616 | tf_op jit(solution)/shard_map/ppermute | solution.py:187
  126.0 25.0 %collective-permute-start.17 = (f32[2,2,2,8,128]{4,3,2,1,0:T(8,128)}, f32[2,2,2,8,128]{4,3,2,1,0:T(8,128)S(1)}, u32[]{:S(2)}, u32[]{:S(2)}) collective-permute-start(f32[2,2,2,8,128]{4,3,2,1,0:T(8,128)} %get-tuple-element.16), channel_id=1, source_target_pairs={{0,0},{1,32},{2,64},{3,96},{4,128},{5,160},{6,192},{7,224},{8,256}... | collective-permute-start | bytes 98312 | tf_op jit(solution)/shard_map/ppermute | solution.py:467
  132.8 18.1 %collective-permute-start.18 = (f32[2,2,2,8,128]{4,3,2,1,0:T(8,128)}, f32[2,2,2,8,128]{4,3,2,1,0:T(8,128)S(1)}, u32[]{:S(2)}, u32[]{:S(2)}) collective-permute-start(f32[2,2,2,8,128]{4,3,2,1,0:T(8,128)} %get-tuple-element.17), channel_id=1, source_target_pairs={{0,16},{1,48},{2,80},{3,112},{4,144},{5,176},{6,208},{7,240},{8,27... | collective-permute-start | bytes 98312 | tf_op jit(solution)/shard_map/ppermute | solution.py:468
  142.0 18.8 %collective-permute-start.21 = (f32[8,6,8,128]{3,2,1,0:T(8,128)}, f32[8,6,8,128]{3,2,1,0:T(8,128)S(1)}, u32[]{:S(2)}, u32[]{:S(2)}) collective-permute-start(f32[8,6,8,128]{3,2,1,0:T(8,128)} %shard_map.40.d0), channel_id=1, source_target_pairs={{0,3},{1,0},{2,1},{3,2},{4,7},{5,4},{6,5},{7,6},{8,11},{9,8},{10,9... | collective-permute-start | bytes 589832 | tf_op jit(solution)/shard_map/ppermute | solution.py:204
  145.0 18.0 %collective-permute-start.20 = (f32[8,6,8,128]{3,2,1,0:T(8,128)}, f32[8,6,8,128]{3,2,1,0:T(8,128)S(1)}, u32[]{:S(2)}, u32[]{:S(2)}) collective-permute-start(f32[8,6,8,128]{3,2,1,0:T(8,128)} %shard_map.40.d0), channel_id=1, source_target_pairs={{0,2},{1,3},{2,0},{3,1},{4,6},{5,7},{6,4},{7,5},{8,10},{9,11},{10,... | collective-permute-start | bytes 589832 | tf_op jit(solution)/shard_map/ppermute | solution.py:204
  147.2 15.9 %collective-permute-start.19 = (f32[8,6,8,128]{3,2,1,0:T(8,128)}, f32[8,6,8,128]{3,2,1,0:T(8,128)S(1)}, u32[]{:S(2)}, u32[]{:S(2)}) collective-permute-start(f32[8,6,8,128]{3,2,1,0:T(8,128)} %shard_map.40.d0), channel_id=1, source_target_pairs={{0,1},{1,2},{2,3},{3,0},{4,5},{5,6},{6,7},{7,4},{8,9},{9,10},{10,1... | collective-permute-start | bytes 589832 | tf_op jit(solution)/shard_map/ppermute | solution.py:204
  153.6 39.4 %collective-permute-start.16 = (f32[8,2,4,2,8,128]{5,4,3,2,1,0:T(8,128)}, f32[8,2,4,2,8,128]{5,4,3,2,1,0:T(8,128)S(1)}, u32[]{:S(2)}, u32[]{:S(2)}) collective-permute-start(f32[8,2,4,2,8,128]{5,4,3,2,1,0:T(8,128)} %shard_map.42.row0), channel_id=1, source_target_pairs={{0,3},{1,0},{2,1},{3,2},{4,7},{5,4},{6,5},{7,6},{8,11},{9,8},{10,9... | collective-permute-start | bytes 1572872 | tf_op jit(solution)/shard_map/ppermute | solution.py:204
  157.3 35.6 %collective-permute-start.15 = (f32[8,2,4,2,8,128]{5,4,3,2,1,0:T(8,128)}, f32[8,2,4,2,8,128]{5,4,3,2,1,0:T(8,128)S(1)}, u32[]{:S(2)}, u32[]{:S(2)}) collective-permute-start(f32[8,2,4,2,8,128]{5,4,3,2,1,0:T(8,128)} %shard_map.42.row0), channel_id=1, source_target_pairs={{0,2},{1,3},{2,0},{3,1},{4,6},{5,7},{6,4},{7,5},{8,10},{9,11},{10,... | collective-permute-start | bytes 1572872 | tf_op jit(solution)/shard_map/ppermute | solution.py:204
  160.8 33.0 %collective-permute-start.14 = (f32[8,2,4,2,8,128]{5,4,3,2,1,0:T(8,128)}, f32[8,2,4,2,8,128]{5,4,3,2,1,0:T(8,128)S(1)}, u32[]{:S(2)}, u32[]{:S(2)}) collective-permute-start(f32[8,2,4,2,8,128]{5,4,3,2,1,0:T(8,128)} %shard_map.42.row0), channel_id=1, source_target_pairs={{0,1},{1,2},{2,3},{3,0},{4,5},{5,6},{6,7},{7,4},{8,9},{9,10},{10,1... | collective-permute-start | bytes 1572872 | tf_op jit(solution)/shard_map/ppermute | solution.py:204
  (33 other events, 431.6 us)
Sparse Core Ops, SparseCore 0:
  153.7 43.9 all-gather.3

commit v4 on v2

--- a/solution.py
+++ b/solution.py
@@ -13,6 +13,7 @@
 HALF = 128
 SMEM = pl.BlockSpec(memory_space=pltpu.SMEM)
 VMEM = pl.BlockSpec(memory_space=pltpu.VMEM)
+HBM = pl.BlockSpec(memory_space=pltpu.HBM)
 
 
 def dot_nt(a, b):
@@ -130,9 +131,7 @@
     for t, ref in enumerate((first_ref, second_ref)):
         for r in range(4):
             for h in range(2):
-                part = ref[0, 2 * r + h]
-                for z in range(8):
-                    bulk_ref[z, t, r, h] = part
+                bulk_ref[t, r, h] = ref[0, 2 * r + h]
         for c in range(2):
             for h in range(2):
                 even = ref[0, 4 * c + h]
@@ -155,7 +154,7 @@
             out_specs=[VMEM, VMEM, VMEM],
         ),
         out_shape=[
-            jax.ShapeDtypeStruct((8, 2, 4, 2, 8, HALF), f32),
+            jax.ShapeDtypeStruct((2, 4, 2, 8, HALF), f32),
             jax.ShapeDtypeStruct((2, 2, 2, 8, HALF), f32),
             jax.ShapeDtypeStruct((2, 2, 2, 8, HALF), f32),
         ],
@@ -165,19 +164,16 @@
 def cols_kernel(scal, first_ref, second_ref, out_ref):
     low = scal[2] < N_ROW
     first, second = first_ref[...], second_ref[...]
-    lo = jnp.where(low, first, second)
-    hi = jnp.where(low, second, first)
-    for y in range(N_ROW):
-        out_ref[y, 0] = lo
-        out_ref[y, 1] = hi
-
-
-def col_copies(scal, first, second):
+    out_ref[0] = jnp.where(low, first, second)
+    out_ref[1] = jnp.where(low, second, first)
+
+
+def order_cols(scal, first, second):
     return pl.pallas_call(
         cols_kernel,
         in_specs=[SMEM, VMEM, VMEM],
         out_specs=VMEM,
-        out_shape=jax.ShapeDtypeStruct((N_ROW, 2, 2, 2, 2, 8, HALF), f32),
+        out_shape=jax.ShapeDtypeStruct((2, 2, 2, 2, 8, HALF), f32),
     )(scal, first, second)
 
 
@@ -227,8 +223,11 @@
     return jnp.concatenate(upper, 0), jnp.concatenate(lower_inv, 0)
 
 
-def factor_kernel(scal, lev, d_ref, l_ref, li_ref, p_ref, s_ref, u_ref, v_ref):
+def factor_kernel(scal, lev, d_ref, out_hbm, out_ref, s_ref, u_ref, v_ref, sems):
     k = scal[0]
+
+    def send(n):
+        return pltpu.make_async_copy(out_ref.at[n], out_hbm.at[n], sems.at[n])
 
     def tile(n):
         return jnp.concatenate([d_ref[:, 2 * n + h].reshape(B, HALF) for h in range(2)], axis=1)
@@ -254,38 +253,45 @@
         l21 = s_ref[HALF:, 0:HALF]
         zero = jnp.zeros((HALF, HALF), f32)
         v0, v1 = v_ref[0], v_ref[1]
-        l_ref[t, 0:HALF, 0:HALF] = u_ref[0].T
-        l_ref[t, 0:HALF, HALF:] = zero
-        l_ref[t, HALF:, 0:HALF] = l21
-        l_ref[t, HALF:, HALF:] = u_ref[1].T
-        li_ref[t, 0:HALF, 0:HALF] = v0
-        li_ref[t, 0:HALF, HALF:] = zero
-        li_ref[t, HALF:, 0:HALF] = -dot_nn(v1, dot_nn(l21, v0))
-        li_ref[t, HALF:, HALF:] = v1
+        out_ref[t, 0:HALF, 0:HALF] = u_ref[0].T
+        out_ref[t, 0:HALF, HALF:] = zero
+        out_ref[t, HALF:, 0:HALF] = l21
+        out_ref[t, HALF:, HALF:] = u_ref[1].T
+        out_ref[2 + t, 0:HALF, 0:HALF] = v0
+        out_ref[2 + t, 0:HALF, HALF:] = zero
+        out_ref[2 + t, HALF:, 0:HALF] = -dot_nn(v1, dot_nn(l21, v0))
+        out_ref[2 + t, HALF:, HALF:] = v1
 
         @pl.when(t == 0)
         def _():
             below = k + 1
-            solved = by_level(dot_nt(tile(1), li_ref[0]), lev[below % N_ROW, below // N_ROW])
-            p_ref[...] = solved
+            solved = by_level(dot_nt(tile(1), out_ref[2]), lev[below % N_ROW, below // N_ROW])
+            out_ref[4] = solved
             s_ref[...] = tile(2) - dot_nt(solved, solved)
+            for n in (0, 2, 4):
+                send(n).start()
 
         return 0
 
     lax.fori_loop(0, 2, step, 0)
+    for n in (1, 3):
+        send(n).start()
+    for n in range(5):
+        send(n).wait()
 
 
 def factor_two(scal, lev, diag):
-    pair = jax.ShapeDtypeStruct((2, B, B), f32)
     return pl.pallas_call(
         factor_kernel,
         in_specs=[SMEM, SMEM, VMEM],
-        out_specs=[VMEM] * 3,
-        out_shape=[pair, pair, jax.ShapeDtypeStruct((B, B), f32)],
+        out_specs=HBM,
+        out_shape=jax.ShapeDtypeStruct((5, B, B), f32),
         scratch_shapes=[
+            pltpu.VMEM((5, B, B), f32),
             pltpu.VMEM((B, B), f32),
             pltpu.VMEM((2, HALF, HALF), f32),
             pltpu.VMEM((2, HALF, HALF), f32),
+            pltpu.SemaphoreType.DMA((5,)),
         ],
         compiler_params=pltpu.CompilerParams(vmem_limit_bytes=8 << 20),
         cost_estimate=pl.CostEstimate(flops=3 * 10**10, bytes_accessed=10**6, transcendentals=0),
@@ -293,13 +299,38 @@
 
 
 def update_kernel(
-    scal, lev, prec, rows_ref, cols_ref, l_ref, li_ref, p10_ref, mat_ref, out_ref, panel
+    scal,
+    lev,
+    prec,
+    rows_hbm,
+    cols_hbm,
+    f_hbm,
+    mat_hbm,
+    out_hbm,
+    rows_ref,
+    cols_ref,
+    f_ref,
+    mat_ref,
+    out_ref,
+    panel,
+    sems,
+    out_sems,
 ):
     k, p, q = scal[0], scal[1], scal[2]
+    pairs = ((cols_hbm, cols_ref), (rows_hbm, rows_ref), (f_hbm, f_ref), (mat_hbm, mat_ref))
+    fetches = [pltpu.make_async_copy(a, b, sems.at[n]) for n, (a, b) in enumerate(pairs)]
+    for fetch in fetches:
+        fetch.start()
+
+    def store(r):
+        at = pl.ds(pl.multiple_of(r * 1024, 1024), 1024)
+        return pltpu.make_async_copy(out_ref.at[at], out_hbm.at[at], out_sems.at[r])
 
     def level_of(t, i):
         return lev[i % N_ROW, 4 * t + i // N_ROW]
 
+    fetches[0].wait()
+    fetches[1].wait()
     for t in range(2):
         for h in range(2):
             lanes = slice(h * HALF, (h + 1) * HALF)
@@ -312,28 +343,30 @@
                 for part in range(2):
                     at = slice(part * HALF, (part + 1) * HALF)
                     panel[t, 4 + c, at, lanes] = cols_ref[:, part, t, c, h].reshape(HALF, HALF)
+    fetches[2].wait()
 
     def solve(n, _):
         i = jnp.where(n < 4, n * N_ROW + p, (n - 4) * N_COL + q)
 
         @pl.when(i > k)
         def _():
-            panel[0, n] = by_level(dot_nt(panel[0, n], li_ref[0]), level_of(0, i))
+            panel[0, n] = by_level(dot_nt(panel[0, n], f_ref[2]), level_of(0, i))
             level = level_of(1, i)
 
             @pl.when((i > k + 1) & (level == 2))
             def _():
-                raw = panel[1, n] - dot_nt(panel[0, n], p10_ref[...])
-                panel[1, n] = dot_nt(raw, li_ref[1])
+                raw = panel[1, n] - dot_nt(panel[0, n], f_ref[4])
+                panel[1, n] = dot_nt(raw, f_ref[3])
 
             @pl.when((i > k + 1) & (level == 1))
             def _():
-                raw = rounded(panel[1, n] - dot_narrow(panel[0, n], p10_ref[...]))
-                panel[1, n] = rounded(dot_nt(raw, li_ref[1]))
+                raw = rounded(panel[1, n] - dot_narrow(panel[0, n], f_ref[4]))
+                panel[1, n] = rounded(dot_nt(raw, f_ref[3]))
 
         return 0
 
     lax.fori_loop(0, 6, solve, 0)
+    fetches[3].wait()
 
     def trail(n, _):
         r, c = n // 2, n % 2
@@ -386,23 +419,36 @@
 
         @pl.when(diagonal)
         def _():
-            put(l_ref[j - k])
+            put(f_ref[j - k])
+
+        @pl.when(c == 1)
+        def _():
+            store(r).start()
 
         return 0
 
     lax.fori_loop(0, 8, trail, 0)
-
-
-def update(scal, lev, prec, row_tiles, col_tiles, factors, inverses, p10, mat):
+    for r in range(4):
+        store(r).wait()
+
+
+def update(scal, lev, prec, row_tiles, col_tiles, factors, mat):
+    operands = (row_tiles, col_tiles, factors, mat)
     return pl.pallas_call(
         update_kernel,
-        in_specs=[SMEM, SMEM, SMEM] + [VMEM] * 6,
-        out_specs=VMEM,
+        in_specs=[SMEM, SMEM, SMEM] + [HBM] * 4,
+        out_specs=HBM,
         out_shape=jax.ShapeDtypeStruct(mat.shape, f32),
-        scratch_shapes=[pltpu.VMEM((2, 6, B, B), f32)],
-        compiler_params=pltpu.CompilerParams(vmem_limit_bytes=12 << 20),
+        scratch_shapes=[pltpu.VMEM(x.shape, f32) for x in operands]
+        + [
+            pltpu.VMEM(mat.shape, f32),
+            pltpu.VMEM((2, 6, B, B), f32),
+            pltpu.SemaphoreType.DMA((4,)),
+            pltpu.SemaphoreType.DMA((4,)),
+        ],
+        compiler_params=pltpu.CompilerParams(vmem_limit_bytes=20 << 20),
         cost_estimate=pl.CostEstimate(flops=10**10, bytes_accessed=10**7, transcendentals=0),
-    )(scal, lev, prec, row_tiles, col_tiles, factors, inverses, p10, mat)
+    )(scal, lev, prec, *operands)
 
 
 def cross_pairs(odd):
@@ -439,17 +485,15 @@
     both = ("row", "col")
     first = lax.ppermute(even, both, cross_pairs(False))
     second = lax.ppermute(odd, both, cross_pairs(True))
-    slab = lax.all_to_all(bulk, "col", 0, 0, axis_index_groups=z_groups)
-    diags, first, second, slab = lax.optimization_barrier((diags, first, second, slab))
-
-    col_tiles = lax.all_to_all(col_copies(scal, first, second), "row", 0, 0)
+    col_tiles = lax.all_gather(order_cols(scal, first, second), "row")
+    slab = lax.all_gather(bulk, "col", axis_index_groups=z_groups)
+    diags, slab = lax.optimization_barrier((diags, slab))
+
     row_tiles = lax.all_to_all(
         jnp.broadcast_to(slab[None], (4,) + slab.shape), "col", 0, 0, axis_index_groups=x_groups
     )
-    factors, inverses, p10 = factor_two(scal, lev, diags)
-    out = update(
-        scal, lev, prec, row_tiles, col_tiles, factors, inverses, p10, mat
-    )
+    factors = factor_two(scal, lev, diags)
+    out = update(scal, lev, prec, row_tiles, col_tiles, factors, mat)
     return out.reshape(matrix.shape)
 
 

time: 196 us -> 182 us (0.929)
  waiting for transfers between devices: 54.8 us -> 10.3 us
  blocking collectives: 49.1 us -> 74.3 us
  between operations: 0.78 us -> 14.2 us
  starting transfers between devices: 38.3 us -> 29.6 us
    all_gather x0 -> x1, blocking collectives: none -> 25.2 us  [per_device(): slab = lax.all_gather(bulk, 'col', axis_index_groups=z_groups)]
    all_to_all x1, waiting for transfers between devices: 23.5 us -> 0.01 us  [per_device(): lax.all_to_all(jnp.broadcast_to(slab[None], (4,) + slab.shape), 'col', 0,...]
    all_to_all x1, waiting for transfers between devices: 19.3 us -> 0.01 us  [per_device(): diags = lax.all_to_all(diag_copies(scal, seen), 'col', 0, 0)]
    ppermute x1, waiting for transfers between devices: 12 us -> 0.01 us  [per_device(): second = lax.ppermute(odd, both, cross_pairs(True))]
    all_gather x0 -> x1, waiting for transfers between devices: none -> 10.3 us  [per_device(): col_tiles = lax.all_gather(order_cols(scal, first, second), 'row')]
    all_to_all x2 -> x0, starting transfers between devices: 8.25 us -> none  [the longest x1 4.43 us: per_device(): col_tiles = lax.all_to_all(col_copies(scal, first, second), 'row', 0, 0)]
    unnamed x30 -> x20, local copies, waits for them, and re-layouts: 8.04 us -> 6.44 us
  transfers between devices with their start and end apart: 7 -> 6, of which waited for: 3 -> 1; matrix products, arithmetic and copies ran while one was open for 1% -> 1% of each run, Pallas kernels for 18% -> 19%
where the time goes in v4:
time: 182 us; the launch traced here: 180 us
  blocking collectives  74.3 us (41%)
  Pallas kernels  41.3 us (23%)
  starting transfers between devices  29.6 us (16%)
  between operations  14.2 us (8%)
  waiting for transfers between devices  10.3 us (6%)
  local copies, waits for them, and re-layouts  8.95 us (5%)
    all_to_all x1, blocking collectives, per_device(): got_diag = lax.all_to_all(sent_diag, 'col', 0, 0)  27.4 us
    pallas_call x1, Pallas kernels, factor_two(): pl.pallas_call(factor_kernel, in_specs=[SMEM, SMEM, VMEM], out_specs=HBM,...  26.4 us
    all_gather x1, blocking collectives, per_device(): slab = lax.all_gather(bulk, 'col', axis_index_groups=z_groups)  25.2 us
    all_gather x1, blocking collectives, per_device(): seen = lax.all_gather(diag_parts(scal, got_diag), 'row')  21.7 us
    all_gather x1, waiting for transfers between devices, per_device(): col_tiles = lax.all_gather(order_cols(scal, first, second), 'row')  10.3 us
    all_to_all x1, starting transfers between devices, per_device(): diags = lax.all_to_all(diag_copies(scal, seen), 'col', 0, 0)  9.5 us
    ppermute x1, starting transfers between devices, per_device(): second = lax.ppermute(odd, both, cross_pairs(True))  6.73 us
    unnamed x20, local copies, waits for them, and re-layouts  6.44 us
  transfers between devices with their start and end apart: 6, of which 1 were waited for; matrix products, arithmetic and copies ran while one was open for 1% of the time, Pallas kernels for 19%

profile of v4, /device:TPU:1, one launch (start us, length us, event | category | flops | bytes accessed | tf_op | source)
XLA Modules:
  0.0 179.5 jit_solution(3039483727100099583)
XLA Ops:
  7.2 0.8 copy.16.prec
  8.0 1.6 copy-done
  9.6 1.8 shard_map.37
  11.4 27.4 %all_to_all.20.first_ref.second_ref = f32[32,3,8,128]{3,2,1,0:T(8,128)} all-to-all(f32[32,3,8,128]{3,2,1,0:T(8,128)S(1)} %get-tuple-element.12), channel_id=1, replica_groups=mesh['row'=16,'col'=32] {'col'}, dimensions={0} | all-to-all | bytes 786432 | tf_op jit(solution)/shard_map/all_to_all | solution.py:478
  38.8 5.0 %all-to-all-start.2 = ((f32[32,8,8,128]{3,2,1,0:T(8,128)}), f32[32,8,8,128]{3,2,1,0:T(8,128)S(1)}, u32[]{:S(2)}, u32[]{:S(2)}) async-start(f32[32,8,8,128]{3,2,1,0:T(8,128)} %get-tuple-element.13), calls=%async_computation.2 | async-start | bytes 2097152 | tf_op jit(solution)/shard_map/all_to_all | solution.py:480
  43.8 2.0 %shard_map.38 = f32[5,8,128]{2,1,0:T(8,128)} custom-call(s32[3]{0:T(128)} %copy-done.2, f32[32,3,8,128]{3,2,1,0:T(8,128)} %all_to_all.20.first_ref.second_ref, f32[32,3,8,128]{3,2,1,0:T(8,128)} %all_to_all.20.first_ref.second_ref), custom_call_target="tpu_custom_call" | custom-call | tf_op jit(solution)/shard_map/pallas_call | solution.py:92
  45.8 21.7 %all-gather = f32[80,8,128]{2,1,0:T(8,128)} all-gather(f32[5,8,128]{2,1,0:T(8,128)} %shard_map.38), channel_id=2, replica_groups=mesh['row'=16,'col'=32] {'row'}, dimensions={0}, use_global_device_ids=true | all-gather | bytes 348160 | tf_op jit(solution)/shard_map/all_gather | solution.py:479
  67.5 2.4 %shard_map.39 = f32[32,6,8,128]{3,2,1,0:T(8,128)} custom-call(s32[3]{0:T(128)} %copy-done.2, f32[16,5,8,128]{3,2,1,0:T(8,128)} %bitcast.15, f32[16,5,8,128]{3,2,1,0:T(8,128)} %bitcast.16), custom_call_target="tpu_custom_call" | custom-call | tf_op jit(solution)/shard_map/pallas_call | solution.py:114
  69.9 9.5 %all-to-all-start.1 = ((f32[32,6,8,128]{3,2,1,0:T(8,128)}), f32[32,6,8,128]{3,2,1,0:T(8,128)S(1)}, u32[]{:S(2)}, u32[]{:S(2)}) async-start(f32[32,6,8,128]{3,2,1,0:T(8,128)} %shard_map.39), calls=%async_computation.1 | async-start | bytes 1572864 | tf_op jit(solution)/shard_map/all_to_all | solution.py:482
  79.4 0.8 slice_convert_fusion
  80.4 2.1 %shard_map.40 = (f32[2,4,2,8,128]{4,3,2,1,0:T(8,128)}, f32[2,2,2,8,128]{4,3,2,1,0:T(8,128)}, f32[2,2,2,8,128]{4,3,2,1,0:T(8,128)}) custom-call(s32[3]{0:T(128)} %copy-done.2, f32[32,8,8,128]{3,2,1,0:T(8,128)} %copy-done.7, f32[32,8,8,128]{3,2,1,0:T(8,128)} %copy-done.7), custom_call_target="tpu_custom_call" | custom-call | tf_op jit(solution)/shard_map/pallas_call | solution.py:145
  82.5 3.7 %collective-permute-start = (f32[2,2,2,8,128]{4,3,2,1,0:T(8,128)}, f32[2,2,2,8,128]{4,3,2,1,0:T(8,128)S(1)}, u32[]{:S(2)}, u32[]{:S(2)}) collective-permute-start(f32[2,2,2,8,128]{4,3,2,1,0:T(8,128)} %get-tuple-element.16), channel_id=1, source_target_pairs={{0,0},{1,32},{2,64},{3,96},{4,128},{5,160},{6,192},{7,224},{8,256}... | collective-permute-start | bytes 98312 | tf_op jit(solution)/shard_map/ppermute | solution.py:486
  86.3 6.7 %collective-permute-start.1 = (f32[2,2,2,8,128]{4,3,2,1,0:T(8,128)}, f32[2,2,2,8,128]{4,3,2,1,0:T(8,128)S(1)}, u32[]{:S(2)}, u32[]{:S(2)}) collective-permute-start(f32[2,2,2,8,128]{4,3,2,1,0:T(8,128)} %get-tuple-element.17), channel_id=1, source_target_pairs={{0,16},{1,48},{2,80},{3,112},{4,144},{5,176},{6,208},{7,240},{8,27... | collective-permute-start | bytes 98312 | tf_op jit(solution)/shard_map/ppermute | solution.py:487
  93.0 25.2 %all-gather.1 = f32[16,4,2,8,128]{4,3,2,1,0:T(8,128)S(1)} all-gather(f32[2,4,2,8,128]{4,3,2,1,0:T(8,128)} %get-tuple-element.14), channel_id=3, replica_groups={{0,4,8,12,16,20,24,28},{1,5,9,13,17,21,25,29},{2,6,10,14,18,22,26,30},{..., dimensions={0}, use_global_device_ids=true | all-gather | bytes 589824 | tf_op jit(solution)/shard_map/all_gather | solution.py:489
  118.8 0.6 copy-done.9
  119.4 1.4 shard_map.41
  120.9 1.6 broadcast_in_dim.2
  122.5 4.6 %all-to-all-start.3 = ((f32[4,8,2,4,2,8,128]{6,5,4,3,2,1,0:T(8,128)}), f32[4,8,2,4,2,8,128]{6,5,4,3,2,1,0:T(8,128)}, u32[]{:S(2)}, u32[]{:S(2)}) async-start(f32[4,8,2,4,2,8,128]{6,5,4,3,2,1,0:T(8,128)} %broadcast_in_dim.2), calls=%async_computation.3 | async-start | bytes 4194304 | tf_op jit(solution)/shard_map/all_to_all | solution.py:492
  127.1 26.4 %shard_map.42.f_hbm = f32[5,256,256]{2,1,0:T(8,128)S(1)} custom-call(s32[3]{0:T(128)S(1)} %copy-done.3, s32[16,8]{1,0:T(8,128)S(1)} %bitcast.12, f32[32,6,8,128]{3,2,1,0:T(8,128)S(1)} %all-to-all-done.1.d_ref), custom_call_target="tpu_custom_call" | custom-call | flops 30000001024 | bytes 1000000 | tf_op jit(solution)/shard_map/pallas_call | solution.py:284
  153.5 1.1 copy-done.5
  154.6 10.3 %all-gather.5.cloned.1.call-done = f32[32,2,2,2,8,128]{5,4,3,2,1,0:T(8,128)} async-done(((f32[2,2,2,2,8,128]{5,4,3,2,1,0:T(8,128)}), f32[32,2,2,2,8,128]{5,4,3,2,1,0:T(8,128)}) %all-gather.5.cloned.1.call-update) | async-done | bytes 1048592 | tf_op jit(solution)/shard_map/all_gather | solution.py:488
  164.9 1.2 copy-done.4
  166.1 1.3 copy-done.6
  167.4 5.3 %shard_map.43 = f32[4096,128]{1,0:T(8,128)} custom-call(s32[3]{0:T(128)S(1)} %copy-done.3, s32[16,8]{1,0:T(8,128)S(1)} %bitcast.13, s32[4,2]{1,0:T(4,128)S(1)} %copy.16.prec, f32[4,8,2,4,2,8,128]{6,5,4,3,2,1,0:T(8,128)} %all-to-all-done.3.rows_hbm, f32[16,2,2,2,2,8,128]{6,5,4,3,2,1,0:T(8,128)S(1)} %bitcast.14, f32[5,256,256]{2,1,0:T(8,128)S(1)} %copy-done.6, ...), custom_call_target="tpu_custom_call" | custom-call | flops 10000000000 | bytes 10000000 | tf_op jit(solution)/shard_map/pallas_call | solution.py:437
  (24 shorter events, 0.9 us)
Async XLA Ops:
  8.0 30.8 %copy-start.2 = (s32[3]{0:T(128)}, s32[3]{0:T(128)S(1)}, u32[]{:S(2)}) copy-start(s32[3]{0:T(128)S(1)} %pad_add_fusion.scal) | copy-start | bytes 40
  8.0 1.6 copy-start
  38.8 31.0 %all-to-all-start.2 = ((f32[32,8,8,128]{3,2,1,0:T(8,128)}), f32[32,8,8,128]{3,2,1,0:T(8,128)S(1)}, u32[]{:S(2)}, u32[]{:S(2)}) async-start(f32[32,8,8,128]{3,2,1,0:T(8,128)} %get-tuple-element.13), calls=%async_computation.2 | async-start | bytes 2097152 | tf_op jit(solution)/shard_map/all_to_all | solution.py:480
  69.9 10.6 %copy-start.7 = (f32[32,8,8,128]{3,2,1,0:T(8,128)}, f32[32,8,8,128]{3,2,1,0:T(8,128)S(1)}, u32[]{:S(2)}) copy-start(f32[32,8,8,128]{3,2,1,0:T(8,128)S(1)} %all-to-all-done.2.first_ref.second_ref) | copy-start | bytes 3145732
  69.9 51.0 %all-to-all-start.1 = ((f32[32,6,8,128]{3,2,1,0:T(8,128)}), f32[32,6,8,128]{3,2,1,0:T(8,128)S(1)}, u32[]{:S(2)}, u32[]{:S(2)}) async-start(f32[32,6,8,128]{3,2,1,0:T(8,128)} %shard_map.39), calls=%async_computation.1 | async-start | bytes 1572864 | tf_op jit(solution)/shard_map/all_to_all | solution.py:482
  79.4 85.5 %all-gather.5.cloned.1.call-start = ((), (), s32[]{:S(2)}) async-start(), calls=%async_computation.4 | async-start | bytes 1114112 | tf_op jit(solution)/shard_map/all_gather | solution.py:488
  82.5 35.7 %collective-permute-start = (f32[2,2,2,8,128]{4,3,2,1,0:T(8,128)}, f32[2,2,2,8,128]{4,3,2,1,0:T(8,128)S(1)}, u32[]{:S(2)}, u32[]{:S(2)}) collective-permute-start(f32[2,2,2,8,128]{4,3,2,1,0:T(8,128)} %get-tuple-element.16), channel_id=1, source_target_pairs={{0,0},{1,32},{2,64},{3,96},{4,128},{5,160},{6,192},{7,224},{8,256}... | collective-permute-start | bytes 98312 | tf_op jit(solution)/shard_map/ppermute | solution.py:486
  86.3 31.9 %collective-permute-start.1 = (f32[2,2,2,8,128]{4,3,2,1,0:T(8,128)}, f32[2,2,2,8,128]{4,3,2,1,0:T(8,128)S(1)}, u32[]{:S(2)}, u32[]{:S(2)}) collective-permute-start(f32[2,2,2,8,128]{4,3,2,1,0:T(8,128)} %get-tuple-element.17), channel_id=1, source_target_pairs={{0,16},{1,48},{2,80},{3,112},{4,144},{5,176},{6,208},{7,240},{8,27... | collective-permute-start | bytes 98312 | tf_op jit(solution)/shard_map/ppermute | solution.py:487
  118.2 0.6 copy-start.8
  118.8 0.6 copy-start.9
  122.5 4.6 %copy-start.3 = (s32[3]{0:T(128)S(1)}, s32[3]{0:T(128)}, u32[]{:S(2)}) copy-start(s32[3]{0:T(128)} %copy-done.2) | copy-start | bytes 40
  122.5 32.1 %all-to-all-start.3 = ((f32[4,8,2,4,2,8,128]{6,5,4,3,2,1,0:T(8,128)}), f32[4,8,2,4,2,8,128]{6,5,4,3,2,1,0:T(8,128)}, u32[]{:S(2)}, u32[]{:S(2)}) async-start(f32[4,8,2,4,2,8,128]{6,5,4,3,2,1,0:T(8,128)} %broadcast_in_dim.2), calls=%async_computation.3 | async-start | bytes 4194304 | tf_op jit(solution)/shard_map/all_to_all | solution.py:492
  127.1 37.8 %copy-start.1 = (f32[4,1,256,2,1,256]{5,4,3,2,1,0:T(1,128)S(1)}, f32[4,1,256,2,1,256]{5,4,3,2,1,0:T(1,128)}, u32[]{:S(2)}) copy-start(f32[4,1,256,2,1,256]{5,4,3,2,1,0:T(1,128)} %param.3) | copy-start | bytes 6291460
  153.5 1.1 copy-start.5
  164.9 1.2 copy-start.4
  166.1 1.3 copy-start.6
Sparse Core Ops, SparseCore 0:
  121.0 43.7 all-gather.4

commit v5 on v4

v5 whole, which is shorter than its diff:
```python
import functools

import jax
import jax.numpy as jnp
from jax import lax
from jax.experimental import pallas as pl
from jax.experimental.pallas import tpu as pltpu
from jax.sharding import PartitionSpec as P

HIGHEST = lax.Precision.HIGHEST
f32 = jnp.float32
N_ROW = 16
N_COL = 32
B = 256
HALF = 128
SMEM = pl.BlockSpec(memory_space=pltpu.SMEM)
VMEM = pl.BlockSpec(memory_space=pltpu.VMEM)
HBM = pl.BlockSpec(memory_space=pltpu.HBM)


def dot_nt(a, b):
    return lax.dot_general(
        a, b, (((1,), (1,)), ((), ())), precision=HIGHEST, preferred_element_type=f32
    )


def dot_nn(a, b):
    return lax.dot_general(
        a, b, (((1,), (0,)), ((), ())), precision=HIGHEST, preferred_element_type=f32
    )


def dot_narrow(a, b):
    return lax.dot_general(
        a.astype(jnp.bfloat16),
        b.astype(jnp.bfloat16),
        (((1,), (1,)), ((), ())),
        preferred_element_type=f32,
    )


def rounded(x):
    return x.astype(jnp.bfloat16).astype(f32)


def by_level(x, level):
    return jnp.where(level == 2, x, jnp.where(level == 1, rounded(x), 0.0))


def pack_kernel(r0, scal, prec, mat_ref, diag_ref, bulk_ref):
    k, p, q = scal[0], scal[1], scal[2]
    col = jnp.where(q == k % N_COL, k // N_COL, (k + 1) // N_COL)
    here_r = jnp.where(p == k % N_ROW, k // N_ROW, (k + 1) // N_ROW)
    sub = lax.broadcasted_iota(jnp.int32, (8, HALF), 0)
    levels = jnp.zeros((8, HALF), f32)
    for r in range(4):
        level = prec[r, col]
        levels = jnp.where(sub % 4 == r, level.astype(f32), levels)
    diag_ref[:, 2] = jnp.broadcast_to(levels[None], (32, 8, HALF))
    for r in range(r0, 4):
        for h in range(2):
            rows = mat_ref[pl.ds(r * 1024 + col * 2 + h, B, stride=4), :]
            rows = by_level(rows, prec[r, col]).reshape(32, 8, HALF)
            bulk_ref[:, (r - r0) * 2 + h] = rows

            @pl.when(here_r == r)
            def _():
                diag_ref[:, h] = rows


def pack(r0, scal, prec, mat):
    return pl.pallas_call(
        functools.partial(pack_kernel, r0),
        in_specs=[SMEM, SMEM, VMEM],
        out_specs=[VMEM, VMEM],
        out_shape=[
            jax.ShapeDtypeStruct((N_COL, 3, 8, HALF), f32),
            jax.ShapeDtypeStruct((N_COL, 8 - 2 * r0, 8, HALF), f32),
        ],
        compiler_params=pltpu.CompilerParams(vmem_limit_bytes=8 << 20),
    )(scal, prec, mat)


def diag_kernel(scal, first_ref, second_ref, out_ref):
    k, p = scal[0], scal[1]
    sub = lax.broadcasted_iota(jnp.int32, (8, HALF), 0)
    out_ref[0:2] = first_ref[0, 0:2]
    out_ref[2:4] = second_ref[0, 0:2]
    out_ref[4] = jnp.where(sub < 4, first_ref[0, 2], second_ref[0, 2])


def diag_parts(scal, received):
    block = (1, 3, 8, HALF)
    return pl.pallas_call(
        diag_kernel,
        grid_spec=pltpu.PrefetchScalarGridSpec(
            num_scalar_prefetch=1,
            grid=(1,),
            in_specs=[
                pl.BlockSpec(block, lambda _, s: (s[0] % N_COL, 0, 0, 0)),
                pl.BlockSpec(block, lambda _, s: ((s[0] + 1) % N_COL, 0, 0, 0)),
            ],
            out_specs=VMEM,
        ),
        out_shape=jax.ShapeDtypeStruct((5, 8, HALF), f32),
    )(scal, received, received)


def route_kernel(r0, c0, scal, first_ref, second_ref, here_ref, below_ref, line_ref, even_ref, odd_ref):
    low = scal[2] < N_ROW
    rows = 4 - r0
    for z in range(8):
        for t, ref in enumerate((first_ref, second_ref)):
            line_ref[z, 2 * rows * t : 2 * rows * (t + 1)] = ref[0]
        line_ref[z, 4 * rows : 4 * rows + 2] = here_ref[0, 0:2]
        line_ref[z, 4 * rows + 2 : 4 * rows + 6] = below_ref[0, 0:4]
    for t, ref in enumerate((first_ref, second_ref)):
        for c in range(c0, 2):
            for h in range(2):
                even = ref[0, 2 * max(2 * c - r0, 0) + h]
                odd = ref[0, 2 * (2 * c + 1 - r0) + h]
                even_ref[t, c - c0, h] = jnp.where(low, even, odd)
                odd_ref[t, c - c0, h] = jnp.where(low, odd, even)


def route(r0, c0, scal, received, seen):
    block = (1, 8 - 2 * r0, 8, HALF)
    part = (1, 5, 8, HALF)
    cross = jax.ShapeDtypeStruct((2, 2 - c0, 2, 8, HALF), f32)
    return pl.pallas_call(
        functools.partial(route_kernel, r0, c0),
        grid_spec=pltpu.PrefetchScalarGridSpec(
            num_scalar_prefetch=1,
            grid=(1,),
            in_specs=[
                pl.BlockSpec(block, lambda _, s: (s[0] % N_COL, 0, 0, 0)),
                pl.BlockSpec(block, lambda _, s: ((s[0] + 1) % N_COL, 0, 0, 0)),
                pl.BlockSpec(part, lambda _, s: (s[0] % N_ROW, 0, 0, 0)),
                pl.BlockSpec(part, lambda _, s: ((s[0] + 1) % N_ROW, 0, 0, 0)),
            ],
            out_specs=[VMEM, VMEM, VMEM],
        ),
        out_shape=[jax.ShapeDtypeStruct((8, 22 - 4 * r0, 8, HALF), f32), cross, cross],
    )(scal, received, received, seen, seen)


def cols_kernel(scal, first_ref, second_ref, out_ref):
    low = scal[2] < N_ROW
    first, second = first_ref[...], second_ref[...]
    for y in range(8):
        out_ref[y, 0] = jnp.where(low, first, second)
        out_ref[y, 1] = jnp.where(low, second, first)


def col_copies(scal, first, second):
    return pl.pallas_call(
        cols_kernel,
        in_specs=[SMEM, VMEM, VMEM],
        out_specs=VMEM,
        out_shape=jax.ShapeDtypeStruct((8, 2) + first.shape, f32),
    )(scal, first, second)


def factor_half(block):
    groups = HALF // 8
    sub = lax.broadcasted_iota(jnp.int32, (8, HALF), 0)
    lane = lax.broadcasted_iota(jnp.int32, (8, HALF), 1)
    up = [block[8 * g : 8 * g + 8, :] for g in range(groups)]
    inv = [jnp.where(lane == sub + 8 * g, 1.0, 0.0).astype(f32) for g in range(groups)]
    upper, lower_inv = [], []

    def row(x, j):
        return jnp.broadcast_to(x[j : j + 1, :], (8, HALF))

    def column(x, c):
        return jnp.broadcast_to(x[:, c : c + 1], (8, HALF))

    for b in range(groups):
        rows, irows = up[b], inv[b]
        cols = [column(rows, 8 * b + j) for j in range(8)]
        diag = jnp.zeros((8, HALF), f32)
        for j in range(8):
            pivot = row(cols[j], j)
            recip = 1.0 / pivot
            diag = jnp.where(sub == j, pivot, diag)
            if j < 7:
                mult = jnp.where(sub > j, cols[j] * recip, 0.0)
                for l in range(j + 1, 8):
                    cols[l] = cols[l] - mult * row(cols[l], j)
                rows = rows - mult * row(rows, j)
                irows = irows - mult * row(irows, j)
        scale = lax.rsqrt(diag)
        rows = rows * scale
        irows = irows * scale
        upper.append(jnp.where(lane >= sub + 8 * b, rows, 0.0))
        lower_inv.append(irows)
        if b + 1 < groups:
            row_each = [row(rows, j) for j in range(8)]
            irow_each = [row(irows, j) for j in range(8)]
            flipped = rows.T
            for g in range(b + 1, groups):
                part = flipped[8 * g : 8 * g + 8, :]
                for j in range(8):
                    m = column(part, j)
                    up[g] = up[g] - m * row_each[j]
                    inv[g] = inv[g] - m * irow_each[j]
    return jnp.concatenate(upper, 0), jnp.concatenate(lower_inv, 0)


def factor_tile(out_ref, s_ref, u_ref, v_ref):
    def half(h, _):
        at = pl.ds(pl.multiple_of(h * HALF, HALF), HALF)
        u, v = factor_half(s_ref[at, at])
        u_ref[h] = u
        v_ref[h] = v

        @pl.when(h == 0)
        def _():
            l21 = dot_nt(s_ref[HALF:, 0:HALF], v)
            s_ref[HALF:, 0:HALF] = l21
            s_ref[HALF:, HALF:] = s_ref[HALF:, HALF:] - dot_nt(l21, l21)

        return 0

    lax.fori_loop(0, 2, half, 0)
    l21 = s_ref[HALF:, 0:HALF]
    zero = jnp.zeros((HALF, HALF), f32)
    v0, v1 = v_ref[0], v_ref[1]
    out_ref[0, 0:HALF, 0:HALF] = u_ref[0].T
    out_ref[0, 0:HALF, HALF:] = zero
    out_ref[0, HALF:, 0:HALF] = l21
    out_ref[0, HALF:, HALF:] = u_ref[1].T
    out_ref[1, 0:HALF, 0:HALF] = v0
    out_ref[1, 0:HALF, HALF:] = zero
    out_ref[1, HALF:, 0:HALF] = -dot_nn(v1, dot_nn(l21, v0))
    out_ref[1, HALF:, HALF:] = v1


FACTOR_SCRATCH = [
    pltpu.VMEM((B, B), f32),
    pltpu.VMEM((2, HALF, HALF), f32),
    pltpu.VMEM((2, HALF, HALF), f32),
]


def first_kernel(scal, lev, d_ref, out_ref, d_rows, s_ref, u_ref, v_ref):
    below = scal[0] + 1
    for x in range(4):
        for z in range(8):
            d_rows[4 * z + x] = d_ref[x, z]

    def tile(n):
        return jnp.concatenate([d_rows[:, 2 * n + h].reshape(B, HALF) for h in range(2)], axis=1)

    s_ref[...] = tile(0)
    factor_tile(out_ref, s_ref, u_ref, v_ref)
    solved = by_level(dot_nt(tile(1), out_ref[1]), lev[below % N_ROW, below // N_ROW])
    out_ref[2] = solved
    out_ref[3] = tile(2) - dot_nt(solved, solved)


def factor_first(scal, lev, diags):
    return pl.pallas_call(
        first_kernel,
        in_specs=[SMEM, SMEM, VMEM],
        out_specs=VMEM,
        out_shape=jax.ShapeDtypeStruct((4, B, B), f32),
        scratch_shapes=[pltpu.VMEM((N_COL, 6, 8, HALF), f32)] + FACTOR_SCRATCH,
        compiler_params=pltpu.CompilerParams(vmem_limit_bytes=8 << 20),
        cost_estimate=pl.CostEstimate(flops=15 * 10**9, bytes_accessed=10**6, transcendentals=0),
    )(scal, lev, diags)


def second_kernel(tile_hbm, out_ref, s_ref, u_ref, v_ref, sem):
    fetch = pltpu.make_async_copy(tile_hbm.at[3], s_ref, sem)
    fetch.start()
    fetch.wait()
    factor_tile(out_ref, s_ref, u_ref, v_ref)


def factor_second(tiles):
    return pl.pallas_call(
        second_kernel,
        in_specs=[HBM],
        out_specs=VMEM,
        out_shape=jax.ShapeDtypeStruct((2, B, B), f32),
        scratch_shapes=FACTOR_SCRATCH + [pltpu.SemaphoreType.DMA(())],
        compiler_params=pltpu.CompilerParams(vmem_limit_bytes=8 << 20),
        cost_estimate=pl.CostEstimate(flops=15 * 10**9, bytes_accessed=10**6, transcendentals=0),
    )(tiles)


def update_kernel(
    r0,
    c0,
    scal,
    lev,
    prec,
    own_hbm,
    other_hbm,
    f_hbm,
    g_hbm,
    mat_hbm,
    rows_hbm,
    out_hbm,
    own_ref,
    other_ref,
    f_ref,
    g_ref,
    mat_ref,
    rows_ref,
    out_ref,
    panel,
    sems,
    out_sems,
):
    k, p, q = scal[0], scal[1], scal[2]
    core = p % 2
    rows = 4 - r0
    tiles = rows + 2 - c0
    pairs = (
        (own_hbm, own_ref),
        (other_hbm, other_ref),
        (rows_hbm, rows_ref),
        (f_hbm, f_ref),
        (g_hbm, g_ref),
        (mat_hbm, mat_ref),
    )
    fetches = [pltpu.make_async_copy(a, b, sems.at[n]) for n, (a, b) in enumerate(pairs)]
    for fetch in fetches:
        fetch.start()

    def store(r):
        at = pl.ds(pl.multiple_of(r * 1024, 1024), 1024)
        return pltpu.make_async_copy(out_ref.at[at], out_hbm.at[at], out_sems.at[r])

    def level_of(t, i):
        return lev[i % N_ROW, 4 * t + i // N_ROW]

    for fetch in fetches[:3]:
        fetch.wait()
    for t in range(2):
        for h in range(2):
            lanes = slice(h * HALF, (h + 1) * HALF)
            for c in range(2 - c0):
                for part in range(2):
                    for y in range(8):
                        at = 8 * (16 * part + 2 * y)
                        for ref, side in ((own_ref, core), (other_ref, 1 - core)):
                            to = pl.ds(pl.multiple_of(at + 8 * side, 8), 8)
                            panel[t, rows + c, to, lanes] = ref[y, part, t, c, h]
            for r in range(rows):
                for x in range(4):
                    for z in range(8):
                        at = 8 * (4 * z + x)
                        panel[t, r, at : at + 8, lanes] = rows_ref[x, z, 2 * rows * t + 2 * r + h]
    fetches[3].wait()
    fetches[4].wait()

    def solve(n, _):
        i = jnp.where(n < rows, (n + r0) * N_ROW + p, (n - rows + c0) * N_COL + q)

        @pl.when(i > k)
        def _():
            panel[0, n] = by_level(dot_nt(panel[0, n], f_ref[1]), level_of(0, i))
            level = level_of(1, i)

            @pl.when((i > k + 1) & (level == 2))
            def _():
                raw = panel[1, n] - dot_nt(panel[0, n], f_ref[2])
                panel[1, n] = dot_nt(raw, g_ref[1])

            @pl.when((i > k + 1) & (level == 1))
            def _():
                raw = rounded(panel[1, n] - dot_narrow(panel[0, n], f_ref[2]))
                panel[1, n] = rounded(dot_nt(raw, g_ref[1]))

        return 0

    lax.fori_loop(0, tiles, solve, 0)
    fetches[5].wait()

    def trail(n, _):
        r, c = n // 2, n % 2
        i = r * N_ROW + p
        j = c * N_COL + q
        level = prec[r, c]
        active = (i >= j) & (j > k)
        row_at = jnp.maximum(r - r0, 0)
        col_at = rows + jnp.maximum(c - c0, 0)
        halves = [pl.ds(r * 1024 + c * 2 + h, B, stride=4) for h in range(2)]

        def put(value):
            for h in range(2):
                out_ref[halves[h], :] = value[:, h * HALF : (h + 1) * HALF]

        def get():
            return jnp.concatenate([mat_ref[halves[h], :] for h in range(2)], axis=1)

        own_first = (j == k) & (i > k)
        own_second = (j == k + 1) & (i > k + 1)
        diagonal = (i == j) & ((j == k) | (j == k + 1))
        plain = jnp.logical_not(own_first | own_second | diagonal)

        @pl.when(plain & (level == 2))
        def _():
            put(get())

            @pl.when(active)
            def _():
                put(get() - dot_nt(panel[0, row_at], panel[0, col_at]) - dot_nt(panel[1, row_at], panel[1, col_at]))

        @pl.when(plain & (level == 1))
        def _():
            put(rounded(get()))

            @pl.when(active)
            def _():
                once = rounded(rounded(get()) - dot_narrow(panel[0, row_at], panel[0, col_at]))
                put(rounded(once - dot_narrow(panel[1, row_at], panel[1, col_at])))

        @pl.when(plain & (level == 0))
        def _():
            put(jnp.zeros((B, B), f32))

        @pl.when(own_first)
        def _():
            put(panel[0, row_at])

        @pl.when(own_second)
        def _():
            put(panel[1, row_at])

        @pl.when(diagonal & (j == k))
        def _():
            put(f_ref[0])

        @pl.when(diagonal & (j == k + 1))
        def _():
            put(g_ref[0])

        @pl.when(c == 1)
        def _():
            store(r).start()

        return 0

    lax.fori_loop(0, 8, trail, 0)
    for r in range(4):
        store(r).wait()


def update(r0, c0, scal, lev, prec, *operands):
    mat = operands[4]
    return pl.pallas_call(
        functools.partial(update_kernel, r0, c0),
        in_specs=[SMEM, SMEM, SMEM] + [HBM] * 6,
        out_specs=HBM,
        out_shape=jax.ShapeDtypeStruct(mat.shape, f32),
        scratch_shapes=[pltpu.VMEM(x.shape, f32) for x in operands]
        + [
            pltpu.VMEM(mat.shape, f32),
            pltpu.VMEM((2, 6 - r0 - c0, B, B), f32),
            pltpu.SemaphoreType.DMA((6,)),
            pltpu.SemaphoreType.DMA((4,)),
        ],
        compiler_params=pltpu.CompilerParams(vmem_limit_bytes=20 << 20),
        cost_estimate=pl.CostEstimate(flops=10**10, bytes_accessed=10**7, transcendentals=0),
    )(scal, lev, prec, *operands)


def cross_pairs(odd):
    pairs = []
    for p in range(N_ROW):
        for q in range(N_COL):
            low = q < N_ROW
            first = low != odd
            row = q if low else q - N_ROW
            col = p if first else p + N_ROW
            pairs.append((p * N_COL + q, row * N_COL + col))
    return pairs


def two_steps(r0, c0, scal, prec, mat):
    both = ("row", "col")
    z_groups = [[4 * z + x for z in range(8)] for x in range(4)]
    x_groups = [[4 * z + x for x in range(4)] for z in range(8)]
    y_groups = [[2 * y + c for y in range(8)] for c in range(2)]
    split = 16 - 4 * r0

    sent_diag, sent_bulk = pack(r0, scal, prec, mat)
    got_diag = lax.all_to_all(sent_diag, "col", 0, 0)
    seen = lax.all_gather(diag_parts(scal, got_diag), "row")
    got_bulk = lax.all_to_all(sent_bulk, "col", 0, 0)
    lev = seen[:, 4, :, 0].astype(jnp.int32)

    line, even, odd = route(r0, c0, scal, got_bulk, seen)
    line = lax.all_to_all(line, "col", 0, 0, axis_index_groups=z_groups)
    first = lax.ppermute(even, both, cross_pairs(False))
    second = lax.ppermute(odd, both, cross_pairs(True))

    diag_line = jnp.broadcast_to(line[None, :, split:], (4, 8, 6, 8, HALF))
    diags = lax.all_to_all(diag_line, "col", 0, 0, axis_index_groups=x_groups)
    copies = col_copies(scal, first, second)
    diags, copies = lax.optimization_barrier((diags, copies))

    own_cols = lax.all_to_all(copies, "row", 0, 0, axis_index_groups=y_groups)
    factors = factor_first(scal, lev, diags)
    own_cols, factors, line = lax.optimization_barrier((own_cols, factors, line))

    other_cols = lax.ppermute(own_cols, "row", [(i, i ^ 1) for i in range(N_ROW)])
    bulk_line = jnp.broadcast_to(line[None, :, :split], (4, 8, split, 8, HALF))
    row_tiles = lax.all_to_all(bulk_line, "col", 0, 0, axis_index_groups=x_groups)
    seconds = factor_second(factors)
    return update(
        r0, c0, scal, lev, prec, own_cols, other_cols, factors, seconds, mat, row_tiles
    )


def per_device(matrix, precision, first_col):
    p = lax.axis_index("row")
    q = lax.axis_index("col")
    k = first_col[0]
    scal = jnp.stack([k, p, q]).astype(jnp.int32)
    prec = precision.reshape(4, 2)
    mat = matrix.reshape(4096, HALF)
    out = two_steps(0, 0, scal, prec, mat)
    return out.reshape(matrix.shape)


def solution(mesh):
    in_specs = (P(None, "row", None, None, "col", None), P(None, "row", None, "col"), P())
    out_specs = P(None, "row", None, None, "col", None)
    return jax.shard_map(
        per_device, mesh=mesh, in_specs=in_specs, out_specs=out_specs, check_vma=False
    )
```

time: 182 us -> 184 us (1.011)
  between operations: 14.2 us -> 0.95 us
  starting transfers between devices: 29.6 us -> 37.8 us
  waiting for transfers between devices: 10.3 us -> 17.3 us
  local copies, waits for them, and re-layouts: 8.95 us -> 11 us
  blocking collectives: 74.3 us -> 72.4 us
    all_gather x2 -> x1, blocking collectives: 46.8 us -> 21.7 us  [two_steps(): seen = lax.all_gather(diag_parts(scal, got_diag), 'row')]
    all_to_all x1 -> x2, blocking collectives: 27.4 us -> 50.7 us  [the longest x1 27.4 us: two_steps(): got_diag = lax.all_to_all(sent_diag, 'col', 0, 0)]
    all_gather x1 -> x0, waiting for transfers between devices: 10.3 us -> none  [per_device(): col_tiles = lax.all_gather(order_cols(scal, first, second), 'row')]
    all_to_all x3 -> x4, waiting for transfers between devices: 0.01 us -> 10.2 us  [the longest x1 5.85 us: two_steps(): lax.all_to_all(bulk_line, 'col', 0, 0, axis_index_groups=x_groups)]
    ppermute x2 -> x3, waiting for transfers between devices: 0.01 us -> 7.1 us  [the longest x1 5.64 us: two_steps(): second = lax.ppermute(odd, both, cross_pairs(True))]
    all_to_all x3 -> x4, starting transfers between devices: 19.1 us -> 23.8 us  [the longest x1 10.2 us: two_steps(): own_cols = lax.all_to_all(copies, 'row', 0, 0, axis_index_groups=y_groups)]
    ppermute x2 -> x3, starting transfers between devices: 10.5 us -> 14 us  [the longest x1 7.82 us: two_steps(): first = lax.ppermute(even, both, cross_pairs(False))]
    unnamed x20 -> x28, local copies, waits for them, and re-layouts: 6.44 us -> 7.48 us
  transfers between devices with their start and end apart: 6 -> 7, of which waited for: 1 -> 5; matrix products, arithmetic and copies ran while one was open for 1% -> 1% of each run, Pallas kernels for 19% -> 16%
where the time goes in v5:
time: 184 us; the launch traced here: 183 us
  blocking collectives  72.4 us (39%)
  Pallas kernels  42.2 us (23%)
  starting transfers between devices  37.8 us (21%)
  waiting for transfers between devices  17.3 us (9%)
  local copies, waits for them, and re-layouts  11 us (6%)
    all_to_all x1, blocking collectives, two_steps(): got_diag = lax.all_to_all(sent_diag, 'col', 0, 0)  27.4 us
    all_to_all x1, blocking collectives, two_steps(): line = lax.all_to_all(line, 'col', 0, 0, axis_index_groups=z_groups)  23.3 us
    all_gather x1, blocking collectives, two_steps(): seen = lax.all_gather(diag_parts(scal, got_diag), 'row')  21.7 us
    pallas_call x1, Pallas kernels, factor_first(): pl.pallas_call(first_kernel, in_specs=[SMEM, SMEM, VMEM], out_specs=VMEM,...  14 us
    pallas_call x1, Pallas kernels, factor_second(): pl.pallas_call(second_kernel, in_specs=[HBM], out_specs=VMEM, out_shape=j...  12.2 us
    all_to_all x1, starting transfers between devices, two_steps(): own_cols = lax.all_to_all(copies, 'row', 0, 0, axis_index_groups=y_groups)  10.2 us
    pallas_call x1, Pallas kernels, update(): pl.pallas_call(functools.partial(update_kernel, r0, c0), in_specs=[SMEM,...  8.17 us
    ppermute x1, starting transfers between devices, two_steps(): first = lax.ppermute(even, both, cross_pairs(False))  7.82 us
  transfers between devices with their start and end apart: 7, of which 5 were waited for; matrix products, arithmetic and copies ran while one was open for 1% of the time, Pallas kernels for 16%

profile of v5, /device:TPU:1, one launch (start us, length us, event | category | flops | bytes accessed | tf_op | source)
XLA Modules:
  0.0 182.5 jit_solution(5474460635941333190)
XLA Ops:
  1.5 1.6 copy-done
  3.1 1.8 shard_map.37
  4.9 27.4 %all_to_all.30.first_ref.second_ref = f32[32,3,8,128]{3,2,1,0:T(8,128)} all-to-all(f32[32,3,8,128]{3,2,1,0:T(8,128)S(1)} %get-tuple-element.15), channel_id=1, replica_groups=mesh['row'=16,'col'=32] {'col'}, dimensions={0} | all-to-all | bytes 786432 | tf_op jit(solution)/shard_map/all_to_all | solution.py:492
  32.3 5.0 %all-to-all-start.1 = ((f32[32,8,8,128]{3,2,1,0:T(8,128)}), f32[32,8,8,128]{3,2,1,0:T(8,128)S(1)}, u32[]{:S(2)}, u32[]{:S(2)}) async-start(f32[32,8,8,128]{3,2,1,0:T(8,128)} %get-tuple-element.16), calls=%async_computation.1 | async-start | bytes 2097152 | tf_op jit(solution)/shard_map/all_to_all | solution.py:494
  37.3 2.0 %shard_map.38 = f32[5,8,128]{2,1,0:T(8,128)} custom-call(s32[3]{0:T(128)} %copy-done.2, f32[32,3,8,128]{3,2,1,0:T(8,128)} %all_to_all.30.first_ref.second_ref, f32[32,3,8,128]{3,2,1,0:T(8,128)} %all_to_all.30.first_ref.second_ref), custom_call_target="tpu_custom_call" | custom-call | tf_op jit(solution)/shard_map/pallas_call | solution.py:94
  39.3 21.7 %all-gather = f32[80,8,128]{2,1,0:T(8,128)} all-gather(f32[5,8,128]{2,1,0:T(8,128)} %shard_map.38), channel_id=2, replica_groups=mesh['row'=16,'col'=32] {'row'}, dimensions={0}, use_global_device_ids=true | all-gather | bytes 348160 | tf_op jit(solution)/shard_map/all_gather | solution.py:493
  61.0 2.0 %all-to-all-done.1.first_ref.second_ref = f32[32,8,8,128]{3,2,1,0:T(8,128)S(1)} async-done(((f32[32,8,8,128]{3,2,1,0:T(8,128)}), f32[32,8,8,128]{3,2,1,0:T(8,128)S(1)}, u32[]{:S(2)}, u32[]{:S(2)}) %all-to-all-start.1) | async-done | bytes 1048608 | tf_op jit(solution)/shard_map/all_to_all | solution.py:494
  63.9 2.4 %shard_map.39 = (f32[8,22,8,128]{3,2,1,0:T(8,128)}, f32[2,2,2,8,128]{4,3,2,1,0:T(8,128)}, f32[2,2,2,8,128]{4,3,2,1,0:T(8,128)}) custom-call(s32[3]{0:T(128)} %copy-done.2, f32[32,8,8,128]{3,2,1,0:T(8,128)} %copy-done.9, f32[32,8,8,128]{3,2,1,0:T(8,128)} %copy-done.9, f32[16,5,8,128]{3,2,1,0:T(8,128)} %bitcast.12, f32[16,5,8,128]{3,2,1,0:T(8,128)} %bitcast.13), custom_call_target="tpu_custom_call" | custom-call | tf_op jit(solution)/shard_map/pallas_call | solution.py:130
  66.3 23.3 %all_to_all.31 = f32[8,22,8,128]{3,2,1,0:T(8,128)S(1)} all-to-all(f32[8,22,8,128]{3,2,1,0:T(8,128)} %get-tuple-element.17), channel_id=1, replica_groups={{0,4,8,12,16,20,24,28},{1,5,9,13,17,21,25,29},{2,6,10,14,18,22,26,30},{..., dimensions={0} | all-to-all | bytes 1441792 | tf_op jit(solution)/shard_map/all_to_all | solution.py:498
  90.6 4.2 %all-to-all-start.3 = ((f32[4,8,6,8,128]{4,3,2,1,0:T(8,128)}), f32[4,8,6,8,128]{4,3,2,1,0:T(8,128)S(1)}, u32[]{:S(2)}, u32[]{:S(2)}) async-start(f32[4,8,6,8,128]{4,3,2,1,0:T(8,128)} %broadcast_in_dim.4), calls=%async_computation.3 | async-start | bytes 1572864 | tf_op jit(solution)/shard_map/all_to_all | solution.py:503
  94.8 7.8 %collective-permute-start = (f32[2,2,2,8,128]{4,3,2,1,0:T(8,128)S(1)}, f32[2,2,2,8,128]{4,3,2,1,0:T(8,128)S(1)}, u32[]{:S(2)}, u32[]{:S(2)}) collective-permute-start(f32[2,2,2,8,128]{4,3,2,1,0:T(8,128)S(1)} %copy-done.13), channel_id=1, source_target_pairs={{0,0},{1,32},{2,64},{3,96},{4,128},{5,160},{6,192},{7,224},{8,256}... | collective-permute-start | bytes 98312 | tf_op jit(solution)/shard_map/ppermute | solution.py:499
  102.6 1.9 %collective-permute-start.1 = (f32[2,2,2,8,128]{4,3,2,1,0:T(8,128)S(1)}, f32[2,2,2,8,128]{4,3,2,1,0:T(8,128)S(1)}, u32[]{:S(2)}, u32[]{:S(2)}) collective-permute-start(f32[2,2,2,8,128]{4,3,2,1,0:T(8,128)S(1)} %copy-done.12), channel_id=1, source_target_pairs={{0,16},{1,48},{2,80},{3,112},{4,144},{5,176},{6,208},{7,240},{8,27... | collective-permute-start | bytes 98312 | tf_op jit(solution)/shard_map/ppermute | solution.py:500
  105.5 1.5 collective-permute-done.first_ref
  107.0 5.6 %collective-permute-done.1.second_ref = f32[2,2,2,8,128]{4,3,2,1,0:T(8,128)S(1)} collective-permute-done((f32[2,2,2,8,128]{4,3,2,1,0:T(8,128)S(1)}, f32[2,2,2,8,128]{4,3,2,1,0:T(8,128)S(1)}, u32[]{:S(2)}, u32[]{:S(2)}) %collective-permute-start.1) | collective-permute-done | bytes 32800 | tf_op jit(solution)/shard_map/ppermute | solution.py:500
  113.2 1.6 shard_map.40
  114.9 10.2 %all-to-all-start.4 = ((f32[8,2,2,2,2,8,128]{6,5,4,3,2,1,0:T(8,128)}), f32[8,2,2,2,2,8,128]{6,5,4,3,2,1,0:T(8,128)S(1)}, u32[]{:S(2)}, u32[]{:S(2)}) async-start(f32[8,2,2,2,2,8,128]{6,5,4,3,2,1,0:T(8,128)} %shard_map.40), calls=%async_computation.4 | async-start | bytes 1048576 | tf_op jit(solution)/shard_map/all_to_all | solution.py:507
  125.1 14.0 %shard_map.41.tile_hbm.f_hbm = f32[4,256,256]{2,1,0:T(8,128)S(1)} custom-call(s32[3]{0:T(128)S(1)} %copy-done.3, s32[16,8]{1,0:T(8,128)S(1)} %bitcast.10, f32[4,8,6,8,128]{4,3,2,1,0:T(8,128)S(1)} %all-to-all-done.3.d_ref), custom_call_target="tpu_custom_call" | custom-call | flops 15000000512 | bytes 1000000 | tf_op jit(solution)/shard_map/pallas_call | solution.py:263
  139.1 2.4 %all-to-all-done.4.own_hbm = f32[8,2,2,2,2,8,128]{6,5,4,3,2,1,0:T(8,128)S(1)} async-done(((f32[8,2,2,2,2,8,128]{6,5,4,3,2,1,0:T(8,128)}), f32[8,2,2,2,2,8,128]{6,5,4,3,2,1,0:T(8,128)S(1)}, u32[]{:S(2)}, u32[]{:S(2)}) %all-to-all-start.4) | async-done | bytes 524320 | tf_op jit(solution)/shard_map/all_to_all | solution.py:507
  141.5 1.6 broadcast_in_dim.5
  143.1 4.5 %all-to-all-start.5 = ((f32[4,8,16,8,128]{4,3,2,1,0:T(8,128)}), f32[4,8,16,8,128]{4,3,2,1,0:T(8,128)}, u32[]{:S(2)}, u32[]{:S(2)}) async-start(f32[4,8,16,8,128]{4,3,2,1,0:T(8,128)} %broadcast_in_dim.5), calls=%async_computation.5 | async-start | bytes 4194304 | tf_op jit(solution)/shard_map/all_to_all | solution.py:513
  147.5 4.2 %collective-permute-start.2 = (f32[8,2,2,2,2,8,128]{6,5,4,3,2,1,0:T(8,128)S(1)}, f32[8,2,2,2,2,8,128]{6,5,4,3,2,1,0:T(8,128)S(1)}, u32[]{:S(2)}, u32[]{:S(2)}) collective-permute-start(f32[8,2,2,2,2,8,128]{6,5,4,3,2,1,0:T(8,128)S(1)} %all-to-all-done.4.own_hbm), channel_id=1, source_target_pairs={{0,32},{32,0},{64,96},{96,64},{128,160},{160,128},{192,224},{224,1... | collective-permute-start | bytes 1572872 | tf_op jit(solution)/shard_map/ppermute | solution.py:511
  153.0 12.2 %shard_map.42.g_hbm = f32[2,256,256]{2,1,0:T(8,128)S(1)} custom-call(f32[4,256,256]{2,1,0:T(8,128)S(1)} %copy-done.5), custom_call_target="tpu_custom_call" | custom-call | flops 15000000512 | bytes 1000000 | tf_op jit(solution)/shard_map/pallas_call | solution.py:282
  166.1 5.9 %all-to-all-done.5.rows_hbm = f32[4,8,16,8,128]{4,3,2,1,0:T(8,128)} async-done(((f32[4,8,16,8,128]{4,3,2,1,0:T(8,128)}), f32[4,8,16,8,128]{4,3,2,1,0:T(8,128)}, u32[]{:S(2)}, u32[]{:S(2)}) %all-to-all-start.5) | async-done | bytes 2097184 | tf_op jit(solution)/shard_map/all_to_all | solution.py:513
  174.2 8.2 %shard_map.43 = f32[4096,128]{1,0:T(8,128)} custom-call(s32[3]{0:T(128)S(1)} %copy-done.3, s32[16,8]{1,0:T(8,128)S(1)} %bitcast.11, s32[4,2]{1,0:T(4,128)S(1)} %copy.16.prec, f32[8,2,2,2,2,8,128]{6,5,4,3,2,1,0:T(8,128)S(1)} %all-to-all-done.4.own_hbm, f32[8,2,2,2,2,8,128]{6,5,4,3,2,1,0:T(8,128)S(1)} %collective-permute-done.2.other_hbm, ...), custom_call_target="tpu_custom_call" | custom-call | flops 10000000000 | bytes 10000000 | tf_op jit(solution)/shard_map/pallas_call | solution.py:455
  (36 shorter events, 8.7 us)
Async XLA Ops:
  1.5 30.8 %copy-start.2 = (s32[3]{0:T(128)}, s32[3]{0:T(128)S(1)}, u32[]{:S(2)}) copy-start(s32[3]{0:T(128)S(1)} %pad_add_fusion.scal) | copy-start | bytes 40
  1.5 1.6 copy-start
  32.3 30.6 %all-to-all-start.1 = ((f32[32,8,8,128]{3,2,1,0:T(8,128)}), f32[32,8,8,128]{3,2,1,0:T(8,128)S(1)}, u32[]{:S(2)}, u32[]{:S(2)}) async-start(f32[32,8,8,128]{3,2,1,0:T(8,128)} %get-tuple-element.16), calls=%async_computation.1 | async-start | bytes 2097152 | tf_op jit(solution)/shard_map/all_to_all | solution.py:494
  62.9 1.0 copy-start.9
  66.3 28.5 %copy-start.13 = (f32[2,2,2,8,128]{4,3,2,1,0:T(8,128)S(1)}, f32[2,2,2,8,128]{4,3,2,1,0:T(8,128)}, u32[]{:S(2)}) copy-start(f32[2,2,2,8,128]{4,3,2,1,0:T(8,128)} %get-tuple-element.18) | copy-start | bytes 98308
  66.3 36.3 %copy-start.12 = (f32[2,2,2,8,128]{4,3,2,1,0:T(8,128)S(1)}, f32[2,2,2,8,128]{4,3,2,1,0:T(8,128)}, u32[]{:S(2)}) copy-start(f32[2,2,2,8,128]{4,3,2,1,0:T(8,128)} %get-tuple-element.19) | copy-start | bytes 98308
  89.6 35.4 %copy-start.3 = (s32[3]{0:T(128)S(1)}, s32[3]{0:T(128)}, u32[]{:S(2)}) copy-start(s32[3]{0:T(128)} %copy-done.2) | copy-start | bytes 40
  90.6 24.3 %all-to-all-start.3 = ((f32[4,8,6,8,128]{4,3,2,1,0:T(8,128)}), f32[4,8,6,8,128]{4,3,2,1,0:T(8,128)S(1)}, u32[]{:S(2)}, u32[]{:S(2)}) async-start(f32[4,8,6,8,128]{4,3,2,1,0:T(8,128)} %broadcast_in_dim.4), calls=%async_computation.3 | async-start | bytes 1572864 | tf_op jit(solution)/shard_map/all_to_all | solution.py:503
  94.8 12.2 %collective-permute-start = (f32[2,2,2,8,128]{4,3,2,1,0:T(8,128)S(1)}, f32[2,2,2,8,128]{4,3,2,1,0:T(8,128)S(1)}, u32[]{:S(2)}, u32[]{:S(2)}) collective-permute-start(f32[2,2,2,8,128]{4,3,2,1,0:T(8,128)S(1)} %copy-done.13), channel_id=1, source_target_pairs={{0,0},{1,32},{2,64},{3,96},{4,128},{5,160},{6,192},{7,224},{8,256}... | collective-permute-start | bytes 98312 | tf_op jit(solution)/shard_map/ppermute | solution.py:499
  102.6 10.0 %collective-permute-start.1 = (f32[2,2,2,8,128]{4,3,2,1,0:T(8,128)S(1)}, f32[2,2,2,8,128]{4,3,2,1,0:T(8,128)S(1)}, u32[]{:S(2)}, u32[]{:S(2)}) collective-permute-start(f32[2,2,2,8,128]{4,3,2,1,0:T(8,128)S(1)} %copy-done.12), channel_id=1, source_target_pairs={{0,16},{1,48},{2,80},{3,112},{4,144},{5,176},{6,208},{7,240},{8,27... | collective-permute-start | bytes 98312 | tf_op jit(solution)/shard_map/ppermute | solution.py:500
  107.0 5.6 %copy-start.10 = (f32[2,2,2,8,128]{4,3,2,1,0:T(8,128)}, f32[2,2,2,8,128]{4,3,2,1,0:T(8,128)S(1)}, u32[]{:S(2)}) copy-start(f32[2,2,2,8,128]{4,3,2,1,0:T(8,128)S(1)} %collective-permute-done.first_ref) | copy-start | bytes 98308
  112.6 0.6 copy-start.11
  114.9 26.6 %all-to-all-start.4 = ((f32[8,2,2,2,2,8,128]{6,5,4,3,2,1,0:T(8,128)}), f32[8,2,2,2,2,8,128]{6,5,4,3,2,1,0:T(8,128)S(1)}, u32[]{:S(2)}, u32[]{:S(2)}) async-start(f32[8,2,2,2,2,8,128]{6,5,4,3,2,1,0:T(8,128)} %shard_map.40), calls=%async_computation.4 | async-start | bytes 1048576 | tf_op jit(solution)/shard_map/all_to_all | solution.py:507
  139.1 4.0 %copy-start.4 = (f32[4,256,256]{2,1,0:T(8,128)}, f32[4,256,256]{2,1,0:T(8,128)S(1)}, u32[]{:S(2)}) copy-start(f32[4,256,256]{2,1,0:T(8,128)S(1)} %shard_map.41.tile_hbm.f_hbm) | copy-start | bytes 3145732
  143.1 28.9 %all-to-all-start.5 = ((f32[4,8,16,8,128]{4,3,2,1,0:T(8,128)}), f32[4,8,16,8,128]{4,3,2,1,0:T(8,128)}, u32[]{:S(2)}, u32[]{:S(2)}) async-start(f32[4,8,16,8,128]{4,3,2,1,0:T(8,128)} %broadcast_in_dim.5), calls=%async_computation.5 | async-start | bytes 4194304 | tf_op jit(solution)/shard_map/all_to_all | solution.py:513
  147.5 24.4 %copy-start.1 = (f32[4,1,256,2,1,256]{5,4,3,2,1,0:T(1,128)S(1)}, f32[4,1,256,2,1,256]{5,4,3,2,1,0:T(1,128)}, u32[]{:S(2)}) copy-start(f32[4,1,256,2,1,256]{5,4,3,2,1,0:T(1,128)} %param.3) | copy-start | bytes 6291460
  147.5 18.5 %collective-permute-start.2 = (f32[8,2,2,2,2,8,128]{6,5,4,3,2,1,0:T(8,128)S(1)}, f32[8,2,2,2,2,8,128]{6,5,4,3,2,1,0:T(8,128)S(1)}, u32[]{:S(2)}, u32[]{:S(2)}) collective-permute-start(f32[8,2,2,2,2,8,128]{6,5,4,3,2,1,0:T(8,128)S(1)} %all-to-all-done.4.own_hbm), channel_id=1, source_target_pairs={{0,32},{32,0},{64,96},{96,64},{128,160},{160,128},{192,224},{224,1... | collective-permute-start | bytes 1572872 | tf_op jit(solution)/shard_map/ppermute | solution.py:511
  151.8 1.2 copy-start.5
  165.3 0.8 copy-start.7
  171.9 1.2 copy-start.6
  173.2 1.0 copy-start.8

commit v6 on v5

--- a/solution.py
+++ b/solution.py
@@ -147,17 +147,16 @@
 def cols_kernel(scal, first_ref, second_ref, out_ref):
     low = scal[2] < N_ROW
     first, second = first_ref[...], second_ref[...]
-    for y in range(8):
-        out_ref[y, 0] = jnp.where(low, first, second)
-        out_ref[y, 1] = jnp.where(low, second, first)
-
-
-def col_copies(scal, first, second):
+    out_ref[0] = jnp.where(low, first, second)
+    out_ref[1] = jnp.where(low, second, first)
+
+
+def order_cols(scal, first, second):
     return pl.pallas_call(
         cols_kernel,
         in_specs=[SMEM, VMEM, VMEM],
         out_specs=VMEM,
-        out_shape=jax.ShapeDtypeStruct((8, 2) + first.shape, f32),
+        out_shape=jax.ShapeDtypeStruct((2,) + first.shape, f32),
     )(scal, first, second)
 
 
@@ -236,61 +235,7 @@
     out_ref[1, HALF:, HALF:] = v1
 
 
-FACTOR_SCRATCH = [
-    pltpu.VMEM((B, B), f32),
-    pltpu.VMEM((2, HALF, HALF), f32),
-    pltpu.VMEM((2, HALF, HALF), f32),
-]
-
-
-def first_kernel(scal, lev, d_ref, out_ref, d_rows, s_ref, u_ref, v_ref):
-    below = scal[0] + 1
-    for x in range(4):
-        for z in range(8):
-            d_rows[4 * z + x] = d_ref[x, z]
-
-    def tile(n):
-        return jnp.concatenate([d_rows[:, 2 * n + h].reshape(B, HALF) for h in range(2)], axis=1)
-
-    s_ref[...] = tile(0)
-    factor_tile(out_ref, s_ref, u_ref, v_ref)
-    solved = by_level(dot_nt(tile(1), out_ref[1]), lev[below % N_ROW, below // N_ROW])
-    out_ref[2] = solved
-    out_ref[3] = tile(2) - dot_nt(solved, solved)
-
-
-def factor_first(scal, lev, diags):
-    return pl.pallas_call(
-        first_kernel,
-        in_specs=[SMEM, SMEM, VMEM],
-        out_specs=VMEM,
-        out_shape=jax.ShapeDtypeStruct((4, B, B), f32),
-        scratch_shapes=[pltpu.VMEM((N_COL, 6, 8, HALF), f32)] + FACTOR_SCRATCH,
-        compiler_params=pltpu.CompilerParams(vmem_limit_bytes=8 << 20),
-        cost_estimate=pl.CostEstimate(flops=15 * 10**9, bytes_accessed=10**6, transcendentals=0),
-    )(scal, lev, diags)
-
-
-def second_kernel(tile_hbm, out_ref, s_ref, u_ref, v_ref, sem):
-    fetch = pltpu.make_async_copy(tile_hbm.at[3], s_ref, sem)
-    fetch.start()
-    fetch.wait()
-    factor_tile(out_ref, s_ref, u_ref, v_ref)
-
-
-def factor_second(tiles):
-    return pl.pallas_call(
-        second_kernel,
-        in_specs=[HBM],
-        out_specs=VMEM,
-        out_shape=jax.ShapeDtypeStruct((2, B, B), f32),
-        scratch_shapes=FACTOR_SCRATCH + [pltpu.SemaphoreType.DMA(())],
-        compiler_params=pltpu.CompilerParams(vmem_limit_bytes=8 << 20),
-        cost_estimate=pl.CostEstimate(flops=15 * 10**9, bytes_accessed=10**6, transcendentals=0),
-    )(tiles)
-
-
-def update_kernel(
+def final_kernel(
     r0,
     c0,
     scal,
@@ -298,19 +243,22 @@
     prec,
     own_hbm,
     other_hbm,
-    f_hbm,
-    g_hbm,
+    line_hbm,
     mat_hbm,
-    rows_hbm,
     out_hbm,
     own_ref,
     other_ref,
+    d_ref,
+    rows_ref,
+    mat_ref,
+    out_ref,
+    panel,
+    d_rows,
     f_ref,
     g_ref,
-    mat_ref,
-    rows_ref,
-    out_ref,
-    panel,
+    s_ref,
+    u_ref,
+    v_ref,
     sems,
     out_sems,
 ):
@@ -318,12 +266,12 @@
     core = p % 2
     rows = 4 - r0
     tiles = rows + 2 - c0
+    split = 4 * rows
     pairs = (
+        (line_hbm.at[:, :, split : split + 6], d_ref),
         (own_hbm, own_ref),
         (other_hbm, other_ref),
-        (rows_hbm, rows_ref),
-        (f_hbm, f_ref),
-        (g_hbm, g_ref),
+        (line_hbm.at[:, :, 0:split], rows_ref),
         (mat_hbm, mat_ref),
     )
     fetches = [pltpu.make_async_copy(a, b, sems.at[n]) for n, (a, b) in enumerate(pairs)]
@@ -337,7 +285,30 @@
     def level_of(t, i):
         return lev[i % N_ROW, 4 * t + i // N_ROW]
 
-    for fetch in fetches[:3]:
+    fetches[0].wait()
+    for x in range(4):
+        for z in range(8):
+            d_rows[4 * z + x] = d_ref[x, z]
+
+    def diag_tile(n):
+        return jnp.concatenate([d_rows[:, 2 * n + h].reshape(B, HALF) for h in range(2)], axis=1)
+
+    s_ref[...] = diag_tile(0)
+
+    def factor(t, _):
+        factor_tile(f_ref.at[t], s_ref, u_ref, v_ref)
+
+        @pl.when(t == 0)
+        def _():
+            solved = by_level(dot_nt(diag_tile(1), f_ref[0, 1]), level_of(0, k + 1))
+            g_ref[...] = solved
+            s_ref[...] = diag_tile(2) - dot_nt(solved, solved)
+
+        return 0
+
+    lax.fori_loop(0, 2, factor, 0)
+
+    for fetch in fetches[1:]:
         fetch.wait()
     for t in range(2):
         for h in range(2):
@@ -354,31 +325,28 @@
                     for z in range(8):
                         at = 8 * (4 * z + x)
                         panel[t, r, at : at + 8, lanes] = rows_ref[x, z, 2 * rows * t + 2 * r + h]
-    fetches[3].wait()
-    fetches[4].wait()
 
     def solve(n, _):
         i = jnp.where(n < rows, (n + r0) * N_ROW + p, (n - rows + c0) * N_COL + q)
 
         @pl.when(i > k)
         def _():
-            panel[0, n] = by_level(dot_nt(panel[0, n], f_ref[1]), level_of(0, i))
+            panel[0, n] = by_level(dot_nt(panel[0, n], f_ref[0, 1]), level_of(0, i))
             level = level_of(1, i)
 
             @pl.when((i > k + 1) & (level == 2))
             def _():
-                raw = panel[1, n] - dot_nt(panel[0, n], f_ref[2])
-                panel[1, n] = dot_nt(raw, g_ref[1])
+                raw = panel[1, n] - dot_nt(panel[0, n], g_ref[...])
+                panel[1, n] = dot_nt(raw, f_ref[1, 1])
 
             @pl.when((i > k + 1) & (level == 1))
             def _():
-                raw = rounded(panel[1, n] - dot_narrow(panel[0, n], f_ref[2]))
-                panel[1, n] = rounded(dot_nt(raw, g_ref[1]))
+                raw = rounded(panel[1, n] - dot_narrow(panel[0, n], g_ref[...]))
+                panel[1, n] = rounded(dot_nt(raw, f_ref[1, 1]))
 
         return 0
 
     lax.fori_loop(0, tiles, solve, 0)
-    fetches[5].wait()
 
     def trail(n, _):
         r, c = n // 2, n % 2
@@ -433,11 +401,11 @@
 
         @pl.when(diagonal & (j == k))
         def _():
-            put(f_ref[0])
+            put(f_ref[0, 0])
 
         @pl.when(diagonal & (j == k + 1))
         def _():
-            put(g_ref[0])
+            put(f_ref[1, 0])
 
         @pl.when(c == 1)
         def _():
@@ -450,23 +418,33 @@
         store(r).wait()
 
 
-def update(r0, c0, scal, lev, prec, *operands):
-    mat = operands[4]
+def final(r0, c0, scal, lev, prec, own, other, line, mat):
+    rows = 4 - r0
     return pl.pallas_call(
-        functools.partial(update_kernel, r0, c0),
-        in_specs=[SMEM, SMEM, SMEM] + [HBM] * 6,
+        functools.partial(final_kernel, r0, c0),
+        in_specs=[SMEM, SMEM, SMEM] + [HBM] * 4,
         out_specs=HBM,
         out_shape=jax.ShapeDtypeStruct(mat.shape, f32),
-        scratch_shapes=[pltpu.VMEM(x.shape, f32) for x in operands]
-        + [
+        scratch_shapes=[
+            pltpu.VMEM(own.shape, f32),
+            pltpu.VMEM(other.shape, f32),
+            pltpu.VMEM((4, 8, 6, 8, HALF), f32),
+            pltpu.VMEM((4, 8, 4 * rows, 8, HALF), f32),
             pltpu.VMEM(mat.shape, f32),
-            pltpu.VMEM((2, 6 - r0 - c0, B, B), f32),
-            pltpu.SemaphoreType.DMA((6,)),
+            pltpu.VMEM(mat.shape, f32),
+            pltpu.VMEM((2, rows + 2 - c0, B, B), f32),
+            pltpu.VMEM((N_COL, 6, 8, HALF), f32),
+            pltpu.VMEM((2, 2, B, B), f32),
+            pltpu.VMEM((B, B), f32),
+            pltpu.VMEM((B, B), f32),
+            pltpu.VMEM((2, HALF, HALF), f32),
+            pltpu.VMEM((2, HALF, HALF), f32),
+            pltpu.SemaphoreType.DMA((5,)),
             pltpu.SemaphoreType.DMA((4,)),
         ],
-        compiler_params=pltpu.CompilerParams(vmem_limit_bytes=20 << 20),
-        cost_estimate=pl.CostEstimate(flops=10**10, bytes_accessed=10**7, transcendentals=0),
-    )(scal, lev, prec, *operands)
+        compiler_params=pltpu.CompilerParams(vmem_limit_bytes=24 << 20),
+        cost_estimate=pl.CostEstimate(flops=4 * 10**10, bytes_accessed=10**7, transcendentals=0),
+    )(scal, lev, prec, own, other, line, mat)
 
 
 def cross_pairs(odd):
@@ -486,7 +464,6 @@
     z_groups = [[4 * z + x for z in range(8)] for x in range(4)]
     x_groups = [[4 * z + x for x in range(4)] for z in range(8)]
     y_groups = [[2 * y + c for y in range(8)] for c in range(2)]
-    split = 16 - 4 * r0
 
     sent_diag, sent_bulk = pack(r0, scal, prec, mat)
     got_diag = lax.all_to_all(sent_diag, "col", 0, 0)
@@ -498,23 +475,13 @@
     line = lax.all_to_all(line, "col", 0, 0, axis_index_groups=z_groups)
     first = lax.ppermute(even, both, cross_pairs(False))
     second = lax.ppermute(odd, both, cross_pairs(True))
-
-    diag_line = jnp.broadcast_to(line[None, :, split:], (4, 8, 6, 8, HALF))
-    diags = lax.all_to_all(diag_line, "col", 0, 0, axis_index_groups=x_groups)
-    copies = col_copies(scal, first, second)
-    diags, copies = lax.optimization_barrier((diags, copies))
-
-    own_cols = lax.all_to_all(copies, "row", 0, 0, axis_index_groups=y_groups)
-    factors = factor_first(scal, lev, diags)
-    own_cols, factors, line = lax.optimization_barrier((own_cols, factors, line))
-
-    other_cols = lax.ppermute(own_cols, "row", [(i, i ^ 1) for i in range(N_ROW)])
-    bulk_line = jnp.broadcast_to(line[None, :, :split], (4, 8, split, 8, HALF))
-    row_tiles = lax.all_to_all(bulk_line, "col", 0, 0, axis_index_groups=x_groups)
-    seconds = factor_second(factors)
-    return update(
-        r0, c0, scal, lev, prec, own_cols, other_cols, factors, seconds, mat, row_tiles
-    )
+    line, first, second = lax.optimization_barrier((line, first, second))
+
+    copies = jnp.broadcast_to(line[None], (4,) + line.shape)
+    line = lax.all_to_all(copies, "col", 0, 0, axis_index_groups=x_groups)
+    own = lax.all_gather(order_cols(scal, first, second), "row", axis_index_groups=y_groups)
+    other = lax.ppermute(own, "row", [(i, i ^ 1) for i in range(N_ROW)])
+    return final(r0, c0, scal, lev, prec, own, other, line, mat)
 
 
 def per_device(matrix, precision, first_col):

time: 184 us -> 176 us (0.957)
  starting transfers between devices: 37.8 us -> 32.2 us
  waiting for transfers between devices: 17.3 us -> 22.8 us
  local copies, waits for them, and re-layouts: 11 us -> 6.89 us
  blocking collectives: 72.4 us -> 70.5 us
    all_to_all x1 -> x0, blocking collectives: 23.3 us -> none  [two_steps(): line = lax.all_to_all(line, 'col', 0, 0, axis_index_groups=z_groups)]
    all_gather x0 -> x1, blocking collectives: none -> 21.5 us  [two_steps(): lax.all_gather(order_cols(scal, first, second), 'row', axis_index_groups=...]
    all_to_all x3 -> x2, starting transfers between devices: 18.8 us -> 8.43 us  [the longest x1 4.75 us: two_steps(): line = lax.all_to_all(line, 'col', 0, 0, axis_index_groups=z_groups)]
    ppermute x1, waiting for transfers between devices: 5.64 us -> 15.8 us  [two_steps(): second = lax.ppermute(odd, both, cross_pairs(True))]
    ppermute x1, starting transfers between devices: 1.92 us -> 7.19 us  [two_steps(): second = lax.ppermute(odd, both, cross_pairs(True))]
    all_to_all x3 -> x2, waiting for transfers between devices: 8.26 us -> 4.43 us  [the longest x1 4.43 us: two_steps(): line = lax.all_to_all(copies, 'col', 0, 0, axis_index_groups=x_groups)]
    unnamed x28 -> x14, local copies, waits for them, and re-layouts: 7.48 us -> 4.17 us
    ppermute x1, starting transfers between devices: 7.82 us -> 5.49 us  [two_steps(): first = lax.ppermute(even, both, cross_pairs(False))]
  transfers between devices with their start and end apart: 7 -> 6, of which waited for: 5 -> 4; matrix products, arithmetic and copies ran while one was open for 1% -> 1% of each run, Pallas kernels for 16% -> 2%
where the time goes in v6:
time: 176 us; the launch traced here: 175 us
  blocking collectives  70.5 us (40%)
  Pallas kernels  40.7 us (23%)
  starting transfers between devices  32.2 us (18%)
  waiting for transfers between devices  22.8 us (13%)
  local copies, waits for them, and re-layouts  6.89 us (4%)
    pallas_call x1, Pallas kernels, final(): pl.pallas_call(functools.partial(final_kernel, r0, c0), in_specs=[SMEM, S...  33.1 us
    all_to_all x1, blocking collectives, two_steps(): got_diag = lax.all_to_all(sent_diag, 'col', 0, 0)  27.4 us
    all_gather x1, blocking collectives, two_steps(): seen = lax.all_gather(diag_parts(scal, got_diag), 'row')  21.7 us
    all_gather x1, blocking collectives, two_steps(): lax.all_gather(order_cols(scal, first, second), 'row', axis_index_groups=...  21.5 us
    ppermute x1, waiting for transfers between devices, two_steps(): second = lax.ppermute(odd, both, cross_pairs(True))  15.8 us
    ppermute x1, starting transfers between devices, two_steps(): second = lax.ppermute(odd, both, cross_pairs(True))  7.19 us
    ppermute x1, starting transfers between devices, two_steps(): other = lax.ppermute(own, 'row', [(i, i ^ 1) for i in range(N_ROW)])  6.06 us
    ppermute x1, starting transfers between devices, two_steps(): first = lax.ppermute(even, both, cross_pairs(False))  5.49 us
  transfers between devices with their start and end apart: 6, of which 4 were waited for; matrix products, arithmetic and copies ran while one was open for 1% of the time, Pallas kernels for 2%

profile of v6, /device:TPU:1, one launch (start us, length us, event | category | flops | bytes accessed | tf_op | source)
XLA Modules:
  0.0 174.8 jit_solution(5653832994999676098)
XLA Ops:
  0.7 0.8 copy.14.prec
  1.5 1.6 copy-done
  3.1 1.8 %shard_map.37 = (f32[32,3,8,128]{3,2,1,0:T(8,128)S(1)}, f32[32,8,8,128]{3,2,1,0:T(8,128)}) custom-call(s32[3]{0:T(128)S(1)} %pad_add_fusion.scal, s32[4,2]{1,0:T(4,128)S(1)} %copy.14.prec, f32[4096,128]{1,0:T(8,128)S(1)} %bitcast.9), custom_call_target="tpu_custom_call" | custom-call | tf_op jit(solution)/shard_map/pallas_call | solution.py:72
  4.9 27.4 %all_to_all.20.first_ref.second_ref = f32[32,3,8,128]{3,2,1,0:T(8,128)} all-to-all(f32[32,3,8,128]{3,2,1,0:T(8,128)S(1)} %get-tuple-element.13), channel_id=1, replica_groups=mesh['row'=16,'col'=32] {'col'}, dimensions={0} | all-to-all | bytes 786432 | tf_op jit(solution)/shard_map/all_to_all | solution.py:469
  32.3 5.0 %all-to-all-start.1 = ((f32[32,8,8,128]{3,2,1,0:T(8,128)}), f32[32,8,8,128]{3,2,1,0:T(8,128)S(1)}, u32[]{:S(2)}, u32[]{:S(2)}) async-start(f32[32,8,8,128]{3,2,1,0:T(8,128)} %get-tuple-element.14), calls=%async_computation.1 | async-start | bytes 2097152 | tf_op jit(solution)/shard_map/all_to_all | solution.py:471
  37.3 2.0 %shard_map.38 = f32[5,8,128]{2,1,0:T(8,128)} custom-call(s32[3]{0:T(128)} %copy-done.2, f32[32,3,8,128]{3,2,1,0:T(8,128)} %all_to_all.20.first_ref.second_ref, f32[32,3,8,128]{3,2,1,0:T(8,128)} %all_to_all.20.first_ref.second_ref), custom_call_target="tpu_custom_call" | custom-call | tf_op jit(solution)/shard_map/pallas_call | solution.py:94
  39.3 21.7 %all-gather = f32[80,8,128]{2,1,0:T(8,128)} all-gather(f32[5,8,128]{2,1,0:T(8,128)} %shard_map.38), channel_id=2, replica_groups=mesh['row'=16,'col'=32] {'row'}, dimensions={0}, use_global_device_ids=true | all-gather | bytes 348160 | tf_op jit(solution)/shard_map/all_gather | solution.py:470
  61.0 2.0 %all-to-all-done.1.first_ref.second_ref = f32[32,8,8,128]{3,2,1,0:T(8,128)S(1)} async-done(((f32[32,8,8,128]{3,2,1,0:T(8,128)}), f32[32,8,8,128]{3,2,1,0:T(8,128)S(1)}, u32[]{:S(2)}, u32[]{:S(2)}) %all-to-all-start.1) | async-done | bytes 1048608 | tf_op jit(solution)/shard_map/all_to_all | solution.py:471
  62.9 1.0 copy-done.4
  63.9 2.4 %shard_map.39 = (f32[8,22,8,128]{3,2,1,0:T(8,128)}, f32[2,2,2,8,128]{4,3,2,1,0:T(8,128)}, f32[2,2,2,8,128]{4,3,2,1,0:T(8,128)}) custom-call(s32[3]{0:T(128)} %copy-done.2, f32[32,8,8,128]{3,2,1,0:T(8,128)} %copy-done.4, f32[32,8,8,128]{3,2,1,0:T(8,128)} %copy-done.4, f32[16,5,8,128]{3,2,1,0:T(8,128)} %bitcast.14, f32[16,5,8,128]{3,2,1,0:T(8,128)} %bitcast.15), custom_call_target="tpu_custom_call" | custom-call | tf_op jit(solution)/shard_map/pallas_call | solution.py:130
  66.3 4.8 %all-to-all-start.2 = ((f32[8,22,8,128]{3,2,1,0:T(8,128)}), f32[8,22,8,128]{3,2,1,0:T(8,128)S(1)}, u32[]{:S(2)}, u32[]{:S(2)}) async-start(f32[8,22,8,128]{3,2,1,0:T(8,128)} %get-tuple-element.15), calls=%async_computation.2 | async-start | bytes 1441792 | tf_op jit(solution)/shard_map/all_to_all | solution.py:475
  71.0 5.5 %collective-permute-start = (f32[2,2,2,8,128]{4,3,2,1,0:T(8,128)}, f32[2,2,2,8,128]{4,3,2,1,0:T(8,128)S(1)}, u32[]{:S(2)}, u32[]{:S(2)}) collective-permute-start(f32[2,2,2,8,128]{4,3,2,1,0:T(8,128)} %get-tuple-element.16), channel_id=1, source_target_pairs={{0,0},{1,32},{2,64},{3,96},{4,128},{5,160},{6,192},{7,224},{8,256}... | collective-permute-start | bytes 98312 | tf_op jit(solution)/shard_map/ppermute | solution.py:476
  76.5 7.2 %collective-permute-start.1 = (f32[2,2,2,8,128]{4,3,2,1,0:T(8,128)}, f32[2,2,2,8,128]{4,3,2,1,0:T(8,128)S(1)}, u32[]{:S(2)}, u32[]{:S(2)}) collective-permute-start(f32[2,2,2,8,128]{4,3,2,1,0:T(8,128)} %get-tuple-element.17), channel_id=1, source_target_pairs={{0,16},{1,48},{2,80},{3,112},{4,144},{5,176},{6,208},{7,240},{8,27... | collective-permute-start | bytes 98312 | tf_op jit(solution)/shard_map/ppermute | solution.py:477
  83.8 15.8 %collective-permute-done.1.second_ref = f32[2,2,2,8,128]{4,3,2,1,0:T(8,128)S(1)} collective-permute-done((f32[2,2,2,8,128]{4,3,2,1,0:T(8,128)}, f32[2,2,2,8,128]{4,3,2,1,0:T(8,128)S(1)}, u32[]{:S(2)}, u32[]{:S(2)}) %collective-permute-start.1) | collective-permute-done | bytes 32800 | tf_op jit(solution)/shard_map/ppermute | solution.py:477
  99.6 1.8 %broadcast_in_dim.2 = f32[4,8,22,8,128]{4,3,2,1,0:T(8,128)} broadcast(f32[8,22,8,128]{3,2,1,0:T(8,128)S(1)} %all-to-all-done.2), dimensions={1,2,3,4} | broadcast | bytes 3604480 | tf_op jit(solution)/shard_map/broadcast_in_dim | solution.py:480
  101.4 3.7 %all-to-all-start.3 = ((f32[4,8,22,8,128]{4,3,2,1,0:T(8,128)}), f32[4,8,22,8,128]{4,3,2,1,0:T(8,128)S(1)}, u32[]{:S(2)}, u32[]{:S(2)}) async-start(f32[4,8,22,8,128]{4,3,2,1,0:T(8,128)} %broadcast_in_dim.2), calls=%async_computation.3 | async-start | bytes 5767168 | tf_op jit(solution)/shard_map/all_to_all | solution.py:481
  105.1 1.4 shard_map.40
  106.5 21.5 %all-gather.1 = f32[16,2,2,2,8,128]{5,4,3,2,1,0:T(8,128)S(1)} all-gather(f32[2,2,2,2,8,128]{5,4,3,2,1,0:T(8,128)} %shard_map.40), channel_id=3, replica_groups={{0,64,128,192,256,320,384,448},{32,96,160,224,288,352,416,480},{1,65,12..., dimensions={0}, use_global_device_ids=true | all-gather | bytes 589824 | tf_op jit(solution)/shard_map/all_gather | solution.py:482
  128.0 6.1 %collective-permute-start.2 = (f32[8,2,2,2,2,8,128]{6,5,4,3,2,1,0:T(8,128)S(1)}, f32[8,2,2,2,2,8,128]{6,5,4,3,2,1,0:T(8,128)}, u32[]{:S(2)}, u32[]{:S(2)}) collective-permute-start(f32[8,2,2,2,2,8,128]{6,5,4,3,2,1,0:T(8,128)S(1)} %bitcast.11), channel_id=1, source_target_pairs={{0,32},{32,0},{64,96},{96,64},{128,160},{160,128},{192,224},{224,1... | collective-permute-start | bytes 1572872 | tf_op jit(solution)/shard_map/ppermute | solution.py:483
  134.0 0.8 slice_convert_fusion
  135.0 0.6 collective-permute-done.2.other_hbm
  135.7 4.4 %all-to-all-done.3.line_hbm = f32[4,8,22,8,128]{4,3,2,1,0:T(8,128)S(1)} async-done(((f32[4,8,22,8,128]{4,3,2,1,0:T(8,128)}), f32[4,8,22,8,128]{4,3,2,1,0:T(8,128)S(1)}, u32[]{:S(2)}, u32[]{:S(2)}) %all-to-all-start.3) | async-done | bytes 2883616 | tf_op jit(solution)/shard_map/all_to_all | solution.py:481
  140.1 1.6 copy-done.1
  141.7 33.1 %shard_map.41 = f32[4096,128]{1,0:T(8,128)} custom-call(s32[3]{0:T(128)S(1)} %copy-done.3, s32[16,8]{1,0:T(8,128)S(1)} %bitcast.13, s32[4,2]{1,0:T(4,128)S(1)} %copy.14.prec, f32[8,2,2,2,2,8,128]{6,5,4,3,2,1,0:T(8,128)S(1)} %bitcast.12, f32[8,2,2,2,2,8,128]{6,5,4,3,2,1,0:T(8,128)} %collective-permute-done.2.other_hbm, ...), custom_call_target="tpu_custom_call" | custom-call | flops 40000000000 | bytes 10000000 | tf_op jit(solution)/shard_map/pallas_call | solution.py:423
  (15 shorter events, 0.3 us)
Async XLA Ops:
  1.5 35.8 %copy-start.2 = (s32[3]{0:T(128)}, s32[3]{0:T(128)S(1)}, u32[]{:S(2)}) copy-start(s32[3]{0:T(128)S(1)} %pad_add_fusion.scal) | copy-start | bytes 40
  1.5 1.6 copy-start
  32.3 30.6 %all-to-all-start.1 = ((f32[32,8,8,128]{3,2,1,0:T(8,128)}), f32[32,8,8,128]{3,2,1,0:T(8,128)S(1)}, u32[]{:S(2)}, u32[]{:S(2)}) async-start(f32[32,8,8,128]{3,2,1,0:T(8,128)} %get-tuple-element.14), calls=%async_computation.1 | async-start | bytes 2097152 | tf_op jit(solution)/shard_map/all_to_all | solution.py:471
  62.9 1.0 copy-start.4
  66.3 33.3 %all-to-all-start.2 = ((f32[8,22,8,128]{3,2,1,0:T(8,128)}), f32[8,22,8,128]{3,2,1,0:T(8,128)S(1)}, u32[]{:S(2)}, u32[]{:S(2)}) async-start(f32[8,22,8,128]{3,2,1,0:T(8,128)} %get-tuple-element.15), calls=%async_computation.2 | async-start | bytes 1441792 | tf_op jit(solution)/shard_map/all_to_all | solution.py:475
  71.0 12.7 %collective-permute-start = (f32[2,2,2,8,128]{4,3,2,1,0:T(8,128)}, f32[2,2,2,8,128]{4,3,2,1,0:T(8,128)S(1)}, u32[]{:S(2)}, u32[]{:S(2)}) collective-permute-start(f32[2,2,2,8,128]{4,3,2,1,0:T(8,128)} %get-tuple-element.16), channel_id=1, source_target_pairs={{0,0},{1,32},{2,64},{3,96},{4,128},{5,160},{6,192},{7,224},{8,256}... | collective-permute-start | bytes 98312 | tf_op jit(solution)/shard_map/ppermute | solution.py:476
  76.5 23.0 %collective-permute-start.1 = (f32[2,2,2,8,128]{4,3,2,1,0:T(8,128)}, f32[2,2,2,8,128]{4,3,2,1,0:T(8,128)S(1)}, u32[]{:S(2)}, u32[]{:S(2)}) collective-permute-start(f32[2,2,2,8,128]{4,3,2,1,0:T(8,128)} %get-tuple-element.17), channel_id=1, source_target_pairs={{0,16},{1,48},{2,80},{3,112},{4,144},{5,176},{6,208},{7,240},{8,27... | collective-permute-start | bytes 98312 | tf_op jit(solution)/shard_map/ppermute | solution.py:477
  83.8 17.6 %copy-start.5 = (f32[2,2,2,8,128]{4,3,2,1,0:T(8,128)}, f32[2,2,2,8,128]{4,3,2,1,0:T(8,128)S(1)}, u32[]{:S(2)}) copy-start(f32[2,2,2,8,128]{4,3,2,1,0:T(8,128)S(1)} %collective-permute-done.first_ref) | copy-start | bytes 98308
  99.6 1.8 %copy-start.6 = (f32[2,2,2,8,128]{4,3,2,1,0:T(8,128)}, f32[2,2,2,8,128]{4,3,2,1,0:T(8,128)S(1)}, u32[]{:S(2)}) copy-start(f32[2,2,2,8,128]{4,3,2,1,0:T(8,128)S(1)} %collective-permute-done.1.second_ref) | copy-start | bytes 98308
  101.4 38.7 %copy-start.3 = (s32[3]{0:T(128)S(1)}, s32[3]{0:T(128)}, u32[]{:S(2)}) copy-start(s32[3]{0:T(128)} %copy-done.2) | copy-start | bytes 40
  101.4 38.7 %all-to-all-start.3 = ((f32[4,8,22,8,128]{4,3,2,1,0:T(8,128)}), f32[4,8,22,8,128]{4,3,2,1,0:T(8,128)S(1)}, u32[]{:S(2)}, u32[]{:S(2)}) async-start(f32[4,8,22,8,128]{4,3,2,1,0:T(8,128)} %broadcast_in_dim.2), calls=%async_computation.3 | async-start | bytes 5767168 | tf_op jit(solution)/shard_map/all_to_all | solution.py:481
  128.0 7.7 %collective-permute-start.2 = (f32[8,2,2,2,2,8,128]{6,5,4,3,2,1,0:T(8,128)S(1)}, f32[8,2,2,2,2,8,128]{6,5,4,3,2,1,0:T(8,128)}, u32[]{:S(2)}, u32[]{:S(2)}) collective-permute-start(f32[8,2,2,2,2,8,128]{6,5,4,3,2,1,0:T(8,128)S(1)} %bitcast.11), channel_id=1, source_target_pairs={{0,32},{32,0},{64,96},{96,64},{128,160},{160,128},{192,224},{224,1... | collective-permute-start | bytes 1572872 | tf_op jit(solution)/shard_map/ppermute | solution.py:483
  140.1 1.6 copy-start.1

commit v7 on v6

--- a/solution.py
+++ b/solution.py
@@ -161,7 +161,7 @@
 
 
 def factor_half(block):
-    groups = HALF // 8
+    groups, half = HALF // 8, HALF // 16
     sub = lax.broadcasted_iota(jnp.int32, (8, HALF), 0)
     lane = lax.broadcasted_iota(jnp.int32, (8, HALF), 1)
     up = [block[8 * g : 8 * g + 8, :] for g in range(groups)]
@@ -174,35 +174,71 @@
     def column(x, c):
         return jnp.broadcast_to(x[:, c : c + 1], (8, HALF))
 
+    def pick(values):
+        out = values[7]
+        for i in range(6, -1, -1):
+            out = jnp.where(sub == i, values[i], out)
+        return out
+
+    for start in (0, half):
+        end = start + half
+        ahead = None
+        for b in range(start, end):
+            here = ahead or [column(up[b], 8 * b + l) for l in range(8)]
+            more = b + 1 < end
+            if more:
+                below = [column(up[b + 1], 8 * b + l) for l in range(8)]
+                ahead = [column(up[b + 1], 8 * (b + 1) + l) for l in range(8)]
+            pivots = [[row(here[l], i) for l in range(i + 1)] for i in range(8)]
+            wide = [row(up[b], i) for i in range(8)]
+            wide_inv = [row(inv[b], i) for i in range(8)]
+            for j in range(8):
+                recip = 1.0 / pivots[j][j]
+                for i in range(j + 1, 8):
+                    mult = pivots[i][j] * recip
+                    for l in range(j + 1, i + 1):
+                        pivots[i][l] = pivots[i][l] - mult * pivots[l][j]
+                    wide[i] = wide[i] - mult * wide[j]
+                    wide_inv[i] = wide_inv[i] - mult * wide_inv[j]
+                if more:
+                    mult = below[j] * recip
+                    for l in range(8):
+                        ahead[l] = ahead[l] - mult * row(below[j], l)
+                    for l in range(j + 1, 8):
+                        below[l] = below[l] - mult * pivots[l][j]
+                    up[b + 1] = up[b + 1] - mult * wide[j]
+                    inv[b + 1] = inv[b + 1] - mult * wide_inv[j]
+            scale = lax.rsqrt(pick([pivots[i][i] for i in range(8)]))
+            rows = pick(wide) * scale
+            irows = pick(wide_inv) * scale
+            upper.append(rows)
+            lower_inv.append(irows)
+            if b + 2 < end:
+                row_each = [row(rows, j) for j in range(8)]
+                irow_each = [row(irows, j) for j in range(8)]
+                flipped = rows.T
+                for g in range(b + 2, end):
+                    part = flipped[8 * g : 8 * g + 8, :]
+                    for j in range(8):
+                        mult = column(part, j)
+                        up[g] = up[g] - mult * row_each[j]
+                        inv[g] = inv[g] - mult * irow_each[j]
+        if end < groups:
+            left = jnp.concatenate(upper, 0)
+            both = jnp.concatenate([left, jnp.concatenate(lower_inv, 0)], 1)
+            product = lax.dot_general(
+                left[:, 8 * end :],
+                both,
+                (((0,), (0,)), ((), ())),
+                precision=HIGHEST,
+                preferred_element_type=f32,
+            )
+            for g in range(end, groups):
+                at = 8 * (g - end)
+                up[g] = up[g] - product[at : at + 8, :HALF]
+                inv[g] = inv[g] - product[at : at + 8, HALF:]
     for b in range(groups):
-        rows, irows = up[b], inv[b]
-        cols = [column(rows, 8 * b + j) for j in range(8)]
-        diag = jnp.zeros((8, HALF), f32)
-        for j in range(8):
-            pivot = row(cols[j], j)
-            recip = 1.0 / pivot
-            diag = jnp.where(sub == j, pivot, diag)
-            if j < 7:
-                mult = jnp.where(sub > j, cols[j] * recip, 0.0)
-                for l in range(j + 1, 8):
-                    cols[l] = cols[l] - mult * row(cols[l], j)
-                rows = rows - mult * row(rows, j)
-                irows = irows - mult * row(irows, j)
-        scale = lax.rsqrt(diag)
-        rows = rows * scale
-        irows = irows * scale
-        upper.append(jnp.where(lane >= sub + 8 * b, rows, 0.0))
-        lower_inv.append(irows)
-        if b + 1 < groups:
-            row_each = [row(rows, j) for j in range(8)]
-            irow_each = [row(irows, j) for j in range(8)]
-            flipped = rows.T
-            for g in range(b + 1, groups):
-                part = flipped[8 * g : 8 * g + 8, :]
-                for j in range(8):
-                    m = column(part, j)
-                    up[g] = up[g] - m * row_each[j]
-                    inv[g] = inv[g] - m * irow_each[j]
+        upper[b] = jnp.where(lane >= sub + 8 * b, upper[b], 0.0)
     return jnp.concatenate(upper, 0), jnp.concatenate(lower_inv, 0)
 
 
@@ -235,57 +271,11 @@
     out_ref[1, HALF:, HALF:] = v1
 
 
-def final_kernel(
-    r0,
-    c0,
-    scal,
-    lev,
-    prec,
-    own_hbm,
-    other_hbm,
-    line_hbm,
-    mat_hbm,
-    out_hbm,
-    own_ref,
-    other_ref,
-    d_ref,
-    rows_ref,
-    mat_ref,
-    out_ref,
-    panel,
-    d_rows,
-    f_ref,
-    g_ref,
-    s_ref,
-    u_ref,
-    v_ref,
-    sems,
-    out_sems,
-):
-    k, p, q = scal[0], scal[1], scal[2]
-    core = p % 2
-    rows = 4 - r0
-    tiles = rows + 2 - c0
-    split = 4 * rows
-    pairs = (
-        (line_hbm.at[:, :, split : split + 6], d_ref),
-        (own_hbm, own_ref),
-        (other_hbm, other_ref),
-        (line_hbm.at[:, :, 0:split], rows_ref),
-        (mat_hbm, mat_ref),
-    )
-    fetches = [pltpu.make_async_copy(a, b, sems.at[n]) for n, (a, b) in enumerate(pairs)]
-    for fetch in fetches:
-        fetch.start()
-
-    def store(r):
-        at = pl.ds(pl.multiple_of(r * 1024, 1024), 1024)
-        return pltpu.make_async_copy(out_ref.at[at], out_hbm.at[at], out_sems.at[r])
-
-    def level_of(t, i):
-        return lev[i % N_ROW, 4 * t + i // N_ROW]
-
-    fetches[0].wait()
+def level_of(lev, t, i):
+    return lev[i % N_ROW, 4 * t + i // N_ROW]
+
+
+def factor_both(scal, lev, d_ref, d_rows, f_ref, g_ref, s_ref, u_ref, v_ref):
     for x in range(4):
         for z in range(8):
             d_rows[4 * z + x] = d_ref[x, z]
@@ -300,7 +290,7 @@
 
         @pl.when(t == 0)
         def _():
-            solved = by_level(dot_nt(diag_tile(1), f_ref[0, 1]), level_of(0, k + 1))
+            solved = by_level(dot_nt(diag_tile(1), f_ref[0, 1]), level_of(lev, 0, scal[0] + 1))
             g_ref[...] = solved
             s_ref[...] = diag_tile(2) - dot_nt(solved, solved)
 
@@ -308,31 +298,26 @@
 
     lax.fori_loop(0, 2, factor, 0)
 
-    for fetch in fetches[1:]:
-        fetch.wait()
+
+def place_rows(rows, rows_ref, panel):
     for t in range(2):
         for h in range(2):
             lanes = slice(h * HALF, (h + 1) * HALF)
-            for c in range(2 - c0):
-                for part in range(2):
-                    for y in range(8):
-                        at = 8 * (16 * part + 2 * y)
-                        for ref, side in ((own_ref, core), (other_ref, 1 - core)):
-                            to = pl.ds(pl.multiple_of(at + 8 * side, 8), 8)
-                            panel[t, rows + c, to, lanes] = ref[y, part, t, c, h]
             for r in range(rows):
                 for x in range(4):
                     for z in range(8):
                         at = 8 * (4 * z + x)
                         panel[t, r, at : at + 8, lanes] = rows_ref[x, z, 2 * rows * t + 2 * r + h]
 
+
+def solve_tiles(first, count, index_of, k, lev, panel, f_ref, g_ref):
     def solve(n, _):
-        i = jnp.where(n < rows, (n + r0) * N_ROW + p, (n - rows + c0) * N_COL + q)
+        i = index_of(n)
 
         @pl.when(i > k)
         def _():
-            panel[0, n] = by_level(dot_nt(panel[0, n], f_ref[0, 1]), level_of(0, i))
-            level = level_of(1, i)
+            panel[0, n] = by_level(dot_nt(panel[0, n], f_ref[0, 1]), level_of(lev, 0, i))
+            level = level_of(lev, 1, i)
 
             @pl.when((i > k + 1) & (level == 2))
             def _():
@@ -346,7 +331,11 @@
 
         return 0
 
-    lax.fori_loop(0, tiles, solve, 0)
+    lax.fori_loop(first, first + count, solve, 0)
+
+
+def trail_tiles(r0, c0, scal, prec, panel, f_ref, mat_ref, out_ref, store):
+    k, p, q = scal[0], scal[1], scal[2]
 
     def trail(n, _):
         r, c = n // 2, n % 2
@@ -355,7 +344,7 @@
         level = prec[r, c]
         active = (i >= j) & (j > k)
         row_at = jnp.maximum(r - r0, 0)
-        col_at = rows + jnp.maximum(c - c0, 0)
+        col_at = 4 - r0 + jnp.maximum(c - c0, 0)
         halves = [pl.ds(r * 1024 + c * 2 + h, B, stride=4) for h in range(2)]
 
         def put(value):
@@ -370,22 +359,23 @@
         diagonal = (i == j) & ((j == k) | (j == k + 1))
         plain = jnp.logical_not(own_first | own_second | diagonal)
 
-        @pl.when(plain & (level == 2))
+        @pl.when(plain & (level == 2) & jnp.logical_not(active))
         def _():
             put(get())
 
-            @pl.when(active)
-            def _():
-                put(get() - dot_nt(panel[0, row_at], panel[0, col_at]) - dot_nt(panel[1, row_at], panel[1, col_at]))
-
-        @pl.when(plain & (level == 1))
+        @pl.when(plain & (level == 2) & active)
+        def _():
+            first = dot_nt(panel[0, row_at], panel[0, col_at])
+            put(get() - first - dot_nt(panel[1, row_at], panel[1, col_at]))
+
+        @pl.when(plain & (level == 1) & jnp.logical_not(active))
         def _():
             put(rounded(get()))
 
-            @pl.when(active)
-            def _():
-                once = rounded(rounded(get()) - dot_narrow(panel[0, row_at], panel[0, col_at]))
-                put(rounded(once - dot_narrow(panel[1, row_at], panel[1, col_at])))
+        @pl.when(plain & (level == 1) & active)
+        def _():
+            once = rounded(rounded(get()) - dot_narrow(panel[0, row_at], panel[0, col_at]))
+            put(rounded(once - dot_narrow(panel[1, row_at], panel[1, col_at])))
 
         @pl.when(plain & (level == 0))
         def _():
@@ -399,13 +389,9 @@
         def _():
             put(panel[1, row_at])
 
-        @pl.when(diagonal & (j == k))
-        def _():
-            put(f_ref[0, 0])
-
-        @pl.when(diagonal & (j == k + 1))
-        def _():
-            put(f_ref[1, 0])
+        @pl.when(diagonal)
+        def _():
+            put(f_ref[j - k, 0])
 
         @pl.when(c == 1)
         def _():
@@ -418,33 +404,95 @@
         store(r).wait()
 
 
-def final(r0, c0, scal, lev, prec, own, other, line, mat):
+def store_to(out_ref, out_hbm, out_sems):
+    def store(r):
+        at = pl.ds(pl.multiple_of(r * 1024, 1024), 1024)
+        return pltpu.make_async_copy(out_ref.at[at], out_hbm.at[at], out_sems.at[r])
+
+    return store
+
+
+def copies_in(pairs, sems):
+    copies = [pltpu.make_async_copy(a, b, sems.at[n]) for n, (a, b) in enumerate(pairs)]
+    for copy in copies:
+        copy.start()
+    return copies
+
+
+FACTOR_SCRATCH = [
+    pltpu.VMEM((N_COL, 6, 8, HALF), f32),
+    pltpu.VMEM((2, 2, B, B), f32),
+    pltpu.VMEM((B, B), f32),
+    pltpu.VMEM((B, B), f32),
+    pltpu.VMEM((2, HALF, HALF), f32),
+    pltpu.VMEM((2, HALF, HALF), f32),
+]
+
+
+def final_kernel(r0, c0, n_cols, scal, lev, prec, *refs):
+    col_hbm, (line_hbm, mat_hbm, out_hbm) = refs[:n_cols], refs[n_cols : n_cols + 3]
+    refs = refs[n_cols + 3 :]
+    col_refs, (d_ref, rows_ref, mat_ref, out_ref, panel) = refs[:n_cols], refs[n_cols : n_cols + 5]
+    d_rows, f_ref, g_ref, s_ref, u_ref, v_ref, sems, out_sems = refs[n_cols + 5 :]
+    k, p, q = scal[0], scal[1], scal[2]
+    core = p % 2
+    rows = 4 - r0
+    split = 4 * rows
+    pairs = [(line_hbm.at[:, :, split : split + 6], d_ref)]
+    pairs += zip(col_hbm, col_refs)
+    pairs += [(line_hbm.at[:, :, 0:split], rows_ref), (mat_hbm, mat_ref)]
+    fetches = copies_in(pairs, sems)
+    fetches[0].wait()
+    factor_both(scal, lev, d_ref, d_rows, f_ref, g_ref, s_ref, u_ref, v_ref)
+    for fetch in fetches[1:]:
+        fetch.wait()
+    place_rows(rows, rows_ref, panel)
+    for t in range(2):
+        for h in range(2):
+            lanes = slice(h * HALF, (h + 1) * HALF)
+            for c in range(2 - c0):
+                for part in range(2):
+                    if n_cols == 1:
+                        at = slice(part * HALF, (part + 1) * HALF)
+                        tile_half = col_refs[0][:, part, t, c, h].reshape(HALF, HALF)
+                        panel[t, rows + c, at, lanes] = tile_half
+                        continue
+                    for y in range(8):
+                        at = 8 * (16 * part + 2 * y)
+                        for ref, side in zip(col_refs, (core, 1 - core)):
+                            to = pl.ds(pl.multiple_of(at + 8 * side, 8), 8)
+                            panel[t, rows + c, to, lanes] = ref[y, part, t, c, h]
+
+    def index_of(n):
+        return jnp.where(n < rows, (n + r0) * N_ROW + p, (n - rows + c0) * N_COL + q)
+
+    solve_tiles(0, rows + 2 - c0, index_of, k, lev, panel, f_ref, g_ref)
+    trail_tiles(
+        r0, c0, scal, prec, panel, f_ref, mat_ref, out_ref, store_to(out_ref, out_hbm, out_sems)
+    )
+
+
+def final(r0, c0, scal, lev, prec, cols, line, mat):
     rows = 4 - r0
     return pl.pallas_call(
-        functools.partial(final_kernel, r0, c0),
-        in_specs=[SMEM, SMEM, SMEM] + [HBM] * 4,
+        functools.partial(final_kernel, r0, c0, len(cols)),
+        in_specs=[SMEM, SMEM, SMEM] + [HBM] * (len(cols) + 2),
         out_specs=HBM,
         out_shape=jax.ShapeDtypeStruct(mat.shape, f32),
         scratch_shapes=[
-            pltpu.VMEM(own.shape, f32),
-            pltpu.VMEM(other.shape, f32),
+            *[pltpu.VMEM(x.shape, f32) for x in cols],
             pltpu.VMEM((4, 8, 6, 8, HALF), f32),
             pltpu.VMEM((4, 8, 4 * rows, 8, HALF), f32),
             pltpu.VMEM(mat.shape, f32),
             pltpu.VMEM(mat.shape, f32),
             pltpu.VMEM((2, rows + 2 - c0, B, B), f32),
-            pltpu.VMEM((N_COL, 6, 8, HALF), f32),
-            pltpu.VMEM((2, 2, B, B), f32),
-            pltpu.VMEM((B, B), f32),
-            pltpu.VMEM((B, B), f32),
-            pltpu.VMEM((2, HALF, HALF), f32),
-            pltpu.VMEM((2, HALF, HALF), f32),
+            *FACTOR_SCRATCH,
             pltpu.SemaphoreType.DMA((5,)),
             pltpu.SemaphoreType.DMA((4,)),
         ],
         compiler_params=pltpu.CompilerParams(vmem_limit_bytes=24 << 20),
         cost_estimate=pl.CostEstimate(flops=4 * 10**10, bytes_accessed=10**7, transcendentals=0),
-    )(scal, lev, prec, own, other, line, mat)
+    )(scal, lev, prec, *cols, line, mat)
 
 
 def cross_pairs(odd):
@@ -479,9 +527,14 @@
 
     copies = jnp.broadcast_to(line[None], (4,) + line.shape)
     line = lax.all_to_all(copies, "col", 0, 0, axis_index_groups=x_groups)
-    own = lax.all_gather(order_cols(scal, first, second), "row", axis_index_groups=y_groups)
-    other = lax.ppermute(own, "row", [(i, i ^ 1) for i in range(N_ROW)])
-    return final(r0, c0, scal, lev, prec, own, other, line, mat)
+    parts = order_cols(scal, first, second)
+    if c0 == 0:
+        own = lax.all_gather(parts, "row", axis_index_groups=y_groups)
+        other = lax.ppermute(own, "row", [(i, i ^ 1) for i in range(N_ROW)])
+        cols = (own, other)
+    else:
+        cols = (lax.all_gather(parts, "row"),)
+    return final(r0, c0, scal, lev, prec, cols, line, mat)
 
 
 def per_device(matrix, precision, first_col):
@@ -491,7 +544,8 @@
     scal = jnp.stack([k, p, q]).astype(jnp.int32)
     prec = precision.reshape(4, 2)
     mat = matrix.reshape(4096, HALF)
-    out = two_steps(0, 0, scal, prec, mat)
+    bands = [functools.partial(two_steps, r0, r0 // 2) for r0 in range(3)]
+    out = lax.switch(k // N_ROW, bands, scal, prec, mat)
     return out.reshape(matrix.shape)
 
 

time: 176 us -> 167 us (0.949)
  Pallas kernels: 40.7 us -> 33.8 us
  local copies, waits for them, and re-layouts: 6.89 us -> 4.98 us
    pallas_call x1, Pallas kernels: 33.1 us -> 25.5 us  [final(): pl.pallas_call(functools.partial(final_kernel, r0, c0, len(cols)), in_spe...]
    unnamed x14 -> x2, local copies, waits for them, and re-layouts: 4.17 us -> 1.31 us
where the time goes in v7:
time: 167 us; the launch traced here: 166 us
  blocking collectives  70.4 us (42%)
  Pallas kernels  33.8 us (20%)
  starting transfers between devices  32.3 us (19%)
  waiting for transfers between devices  22.9 us (14%)
  local copies, waits for them, and re-layouts  4.98 us (3%)
    all_to_all x1, blocking collectives, two_steps(): got_diag = lax.all_to_all(sent_diag, 'col', 0, 0)  27.4 us
    pallas_call x1, Pallas kernels, final(): pl.pallas_call(functools.partial(final_kernel, r0, c0, len(cols)), in_spe...  25.5 us
    all_gather x1, blocking collectives, two_steps(): seen = lax.all_gather(diag_parts(scal, got_diag), 'row')  21.7 us
    all_gather x1, blocking collectives, two_steps(): own = lax.all_gather(parts, 'row', axis_index_groups=y_groups)  21.3 us
    ppermute x1, waiting for transfers between devices, two_steps(): second = lax.ppermute(odd, both, cross_pairs(True))  15.7 us
    ppermute x1, starting transfers between devices, two_steps(): second = lax.ppermute(odd, both, cross_pairs(True))  7.19 us
    ppermute x1, starting transfers between devices, two_steps(): other = lax.ppermute(own, 'row', [(i, i ^ 1) for i in range(N_ROW)])  6.14 us
    ppermute x1, starting transfers between devices, two_steps(): first = lax.ppermute(even, both, cross_pairs(False))  5.61 us
  transfers between devices with their start and end apart: 6, of which 4 were waited for; matrix products, arithmetic and copies ran while one was open for 1% of the time, Pallas kernels for 2%

profile of v7, /device:TPU:1, one launch (start us, length us, event | category | flops | bytes accessed | tf_op | source)
XLA Modules:
  0.0 166.3 jit_solution(6534902310459382076)
XLA Ops:
  0.8 164.3 %conditional.1 = (f32[4,1,256,2,1,256]{5,4,3,2,1,0:T(1,128)S(1)}) conditional(s32[]{:T(128)} %clamp.3, (s32[4,1,2,1]{0,3,2,1:T(1,128)}, f32[4,1,256,2,1,256]{5,4,3,2,1,0:T(1,128)}, s32[3]{0:T(128)S(1)}) %tuple.20, (s32[4,1,2,1]{0,3,2,1:T(1,128)}, f32[4,1,256,2,1,256]{5,4,3,2,1,0:T(1,128)}, s32[3]{0:T(128)S(1)}) %tuple.20, ...), branch_computations={%region_0.1_spmd, %region_1.2_spmd, %region_2.3_spmd} | conditional | flops 40000000000 | bytes 36106228 | solution.py:548
  0.8 0.8 copy.51.prec
  1.5 2.8 %branch_0_fun.5 = (f32[32,3,8,128]{3,2,1,0:T(8,128)S(1)}, f32[32,8,8,128]{3,2,1,0:T(8,128)}) custom-call(s32[3]{0:T(128)S(1)} %get-tuple-element.34.scal, s32[4,2]{1,0:T(4,128)S(1)} %copy.51.prec, f32[4096,128]{1,0:T(8,128)} %bitcast.42), custom_call_target="tpu_custom_call" | custom-call | tf_op jit(solution)/shard_map/cond/branch_0_fun/pallas_call | solution.py:72
  4.4 27.4 %all_to_all.48.first_ref.second_ref = f32[32,3,8,128]{3,2,1,0:T(8,128)} all-to-all(f32[32,3,8,128]{3,2,1,0:T(8,128)S(1)} %get-tuple-element.37), channel_id=1, replica_groups=mesh['row'=16,'col'=32] {'col'}, dimensions={0} | all-to-all | bytes 786432 | tf_op jit(solution)/shard_map/cond/branch_0_fun/all_to_all | solution.py:517
  31.8 5.0 %all-to-all-start.1 = ((f32[32,8,8,128]{3,2,1,0:T(8,128)}), f32[32,8,8,128]{3,2,1,0:T(8,128)S(1)}, u32[]{:S(2)}, u32[]{:S(2)}) async-start(f32[32,8,8,128]{3,2,1,0:T(8,128)} %get-tuple-element.38), calls=%async_computation.1 | async-start | bytes 2097152 | tf_op jit(solution)/shard_map/cond/branch_0_fun/all_to_all | solution.py:519
  36.8 1.9 %branch_0_fun.6 = f32[5,8,128]{2,1,0:T(8,128)} custom-call(s32[3]{0:T(128)S(1)} %get-tuple-element.34.scal, f32[32,3,8,128]{3,2,1,0:T(8,128)} %all_to_all.48.first_ref.second_ref, f32[32,3,8,128]{3,2,1,0:T(8,128)} %all_to_all.48.first_ref.second_ref), custom_call_target="tpu_custom_call" | custom-call | tf_op jit(solution)/shard_map/cond/branch_0_fun/pallas_call | solution.py:94
  38.7 21.7 %all-gather = f32[80,8,128]{2,1,0:T(8,128)} all-gather(f32[5,8,128]{2,1,0:T(8,128)} %branch_0_fun.6), channel_id=2, replica_groups=mesh['row'=16,'col'=32] {'row'}, dimensions={0}, use_global_device_ids=true | all-gather | bytes 348160 | tf_op jit(solution)/shard_map/cond/branch_0_fun/all_gather | solution.py:518
  60.3 2.1 %all-to-all-done.1.first_ref.second_ref = f32[32,8,8,128]{3,2,1,0:T(8,128)S(1)} async-done(((f32[32,8,8,128]{3,2,1,0:T(8,128)}), f32[32,8,8,128]{3,2,1,0:T(8,128)S(1)}, u32[]{:S(2)}, u32[]{:S(2)}) %all-to-all-start.1) | async-done | bytes 1048608 | tf_op jit(solution)/shard_map/cond/branch_0_fun/all_to_all | solution.py:519
  62.4 1.0 copy-done
  63.4 2.2 %branch_0_fun.7 = (f32[8,22,8,128]{3,2,1,0:T(8,128)}, f32[2,2,2,8,128]{4,3,2,1,0:T(8,128)}, f32[2,2,2,8,128]{4,3,2,1,0:T(8,128)}) custom-call(s32[3]{0:T(128)S(1)} %get-tuple-element.34.scal, f32[32,8,8,128]{3,2,1,0:T(8,128)} %copy-done, f32[32,8,8,128]{3,2,1,0:T(8,128)} %copy-done, f32[16,5,8,128]{3,2,1,0:T(8,128)} %bitcast.48, f32[16,5,8,128]{3,2,1,0:T(8,128)} %bitcast.49), custom_call_target="tpu_custom_call" | custom-call | tf_op jit(solution)/shard_map/cond/branch_0_fun/pallas_call | solution.py:130
  65.6 4.6 %all-to-all-start.2 = ((f32[8,22,8,128]{3,2,1,0:T(8,128)}), f32[8,22,8,128]{3,2,1,0:T(8,128)S(1)}, u32[]{:S(2)}, u32[]{:S(2)}) async-start(f32[8,22,8,128]{3,2,1,0:T(8,128)} %get-tuple-element.39), calls=%async_computation.2 | async-start | bytes 1441792 | tf_op jit(solution)/shard_map/cond/branch_0_fun/all_to_all | solution.py:523
  70.3 5.6 %collective-permute-start = (f32[2,2,2,8,128]{4,3,2,1,0:T(8,128)}, f32[2,2,2,8,128]{4,3,2,1,0:T(8,128)S(1)}, u32[]{:S(2)}, u32[]{:S(2)}) collective-permute-start(f32[2,2,2,8,128]{4,3,2,1,0:T(8,128)} %get-tuple-element.40), channel_id=1, source_target_pairs={{0,0},{1,32},{2,64},{3,96},{4,128},{5,160},{6,192},{7,224},{8,256}... | collective-permute-start | bytes 98312 | tf_op jit(solution)/shard_map/cond/branch_0_fun/ppermute | solution.py:524
  75.9 7.2 %collective-permute-start.1 = (f32[2,2,2,8,128]{4,3,2,1,0:T(8,128)}, f32[2,2,2,8,128]{4,3,2,1,0:T(8,128)S(1)}, u32[]{:S(2)}, u32[]{:S(2)}) collective-permute-start(f32[2,2,2,8,128]{4,3,2,1,0:T(8,128)} %get-tuple-element.41), channel_id=1, source_target_pairs={{0,16},{1,48},{2,80},{3,112},{4,144},{5,176},{6,208},{7,240},{8,27... | collective-permute-start | bytes 98312 | tf_op jit(solution)/shard_map/cond/branch_0_fun/ppermute | solution.py:525
  83.1 15.7 %collective-permute-done.1.second_ref = f32[2,2,2,8,128]{4,3,2,1,0:T(8,128)S(1)} collective-permute-done((f32[2,2,2,8,128]{4,3,2,1,0:T(8,128)}, f32[2,2,2,8,128]{4,3,2,1,0:T(8,128)S(1)}, u32[]{:S(2)}, u32[]{:S(2)}) %collective-permute-start.1) | collective-permute-done | bytes 32800 | tf_op jit(solution)/shard_map/cond/branch_0_fun/ppermute | solution.py:525
  98.8 1.8 %broadcast_in_dim.2 = f32[4,8,22,8,128]{4,3,2,1,0:T(8,128)} broadcast(f32[8,22,8,128]{3,2,1,0:T(8,128)S(1)} %all-to-all-done.2), dimensions={1,2,3,4} | broadcast | bytes 3604480 | tf_op jit(solution)/shard_map/cond/branch_0_fun/broadcast_in_dim | solution.py:528
  100.6 3.7 %all-to-all-start.3 = ((f32[4,8,22,8,128]{4,3,2,1,0:T(8,128)}), f32[4,8,22,8,128]{4,3,2,1,0:T(8,128)S(1)}, u32[]{:S(2)}, u32[]{:S(2)}) async-start(f32[4,8,22,8,128]{4,3,2,1,0:T(8,128)} %broadcast_in_dim.2), calls=%async_computation.3 | async-start | bytes 5767168 | tf_op jit(solution)/shard_map/cond/branch_0_fun/all_to_all | solution.py:529
  104.2 1.4 branch_0_fun.8
  105.7 21.3 %all-gather.1 = f32[16,2,2,2,8,128]{5,4,3,2,1,0:T(8,128)S(1)} all-gather(f32[2,2,2,2,8,128]{5,4,3,2,1,0:T(8,128)} %branch_0_fun.8), channel_id=3, replica_groups={{0,64,128,192,256,320,384,448},{32,96,160,224,288,352,416,480},{1,65,12..., dimensions={0}, use_global_device_ids=true | all-gather | bytes 589824 | tf_op jit(solution)/shard_map/cond/branch_0_fun/all_gather | solution.py:532
  127.0 6.1 %collective-permute-start.2 = (f32[8,2,2,2,2,8,128]{6,5,4,3,2,1,0:T(8,128)S(1)}, f32[8,2,2,2,2,8,128]{6,5,4,3,2,1,0:T(8,128)}, u32[]{:S(2)}, u32[]{:S(2)}) collective-permute-start(f32[8,2,2,2,2,8,128]{6,5,4,3,2,1,0:T(8,128)S(1)} %bitcast.34), channel_id=1, source_target_pairs={{0,32},{32,0},{64,96},{96,64},{128,160},{160,128},{192,224},{224,1... | collective-permute-start | bytes 1572872 | tf_op jit(solution)/shard_map/cond/branch_0_fun/ppermute | solution.py:533
  133.2 0.8 slice_convert_fusion
  134.2 0.6 collective-permute-done.2.refs_1_
  134.8 4.5 %all-to-all-done.3.refs_2_ = f32[4,8,22,8,128]{4,3,2,1,0:T(8,128)S(1)} async-done(((f32[4,8,22,8,128]{4,3,2,1,0:T(8,128)}), f32[4,8,22,8,128]{4,3,2,1,0:T(8,128)S(1)}, u32[]{:S(2)}, u32[]{:S(2)}) %all-to-all-start.3) | async-done | bytes 2883616 | tf_op jit(solution)/shard_map/cond/branch_0_fun/all_to_all | solution.py:529
  139.3 25.5 %branch_0_fun.9 = f32[4096,128]{1,0:T(8,128)S(1)} custom-call(s32[3]{0:T(128)S(1)} %get-tuple-element.34.scal, s32[16,8]{1,0:T(8,128)S(1)} %bitcast.39, s32[4,2]{1,0:T(4,128)S(1)} %copy.51.prec, f32[8,2,2,2,2,8,128]{6,5,4,3,2,1,0:T(8,128)S(1)} %bitcast.35, f32[8,2,2,2,2,8,128]{6,5,4,3,2,1,0:T(8,128)} %collective-permute-done.2.refs_1_, ...), custom_call_target="tpu_custom_call" | custom-call | flops 40000000000 | bytes 10000000 | tf_op jit(solution)/shard_map/cond/branch_0_fun/pallas_call | solution.py:477
  165.0 1.3 copy-done.9
  (10 shorter events, 0.3 us)
Async XLA Ops:
  31.8 30.6 %all-to-all-start.1 = ((f32[32,8,8,128]{3,2,1,0:T(8,128)}), f32[32,8,8,128]{3,2,1,0:T(8,128)S(1)}, u32[]{:S(2)}, u32[]{:S(2)}) async-start(f32[32,8,8,128]{3,2,1,0:T(8,128)} %get-tuple-element.38), calls=%async_computation.1 | async-start | bytes 2097152 | tf_op jit(solution)/shard_map/cond/branch_0_fun/all_to_all | solution.py:519
  62.4 1.0 copy-start
  65.6 33.2 %all-to-all-start.2 = ((f32[8,22,8,128]{3,2,1,0:T(8,128)}), f32[8,22,8,128]{3,2,1,0:T(8,128)S(1)}, u32[]{:S(2)}, u32[]{:S(2)}) async-start(f32[8,22,8,128]{3,2,1,0:T(8,128)} %get-tuple-element.39), calls=%async_computation.2 | async-start | bytes 1441792 | tf_op jit(solution)/shard_map/cond/branch_0_fun/all_to_all | solution.py:523
  70.3 12.8 %collective-permute-start = (f32[2,2,2,8,128]{4,3,2,1,0:T(8,128)}, f32[2,2,2,8,128]{4,3,2,1,0:T(8,128)S(1)}, u32[]{:S(2)}, u32[]{:S(2)}) collective-permute-start(f32[2,2,2,8,128]{4,3,2,1,0:T(8,128)} %get-tuple-element.40), channel_id=1, source_target_pairs={{0,0},{1,32},{2,64},{3,96},{4,128},{5,160},{6,192},{7,224},{8,256}... | collective-permute-start | bytes 98312 | tf_op jit(solution)/shard_map/cond/branch_0_fun/ppermute | solution.py:524
  75.9 22.9 %collective-permute-start.1 = (f32[2,2,2,8,128]{4,3,2,1,0:T(8,128)}, f32[2,2,2,8,128]{4,3,2,1,0:T(8,128)S(1)}, u32[]{:S(2)}, u32[]{:S(2)}) collective-permute-start(f32[2,2,2,8,128]{4,3,2,1,0:T(8,128)} %get-tuple-element.41), channel_id=1, source_target_pairs={{0,16},{1,48},{2,80},{3,112},{4,144},{5,176},{6,208},{7,240},{8,27... | collective-permute-start | bytes 98312 | tf_op jit(solution)/shard_map/cond/branch_0_fun/ppermute | solution.py:525
  83.1 17.5 %copy-start.3 = (f32[2,2,2,8,128]{4,3,2,1,0:T(8,128)}, f32[2,2,2,8,128]{4,3,2,1,0:T(8,128)S(1)}, u32[]{:S(2)}) copy-start(f32[2,2,2,8,128]{4,3,2,1,0:T(8,128)S(1)} %collective-permute-done.first_ref) | copy-start | bytes 98308 | tf_op jit(solution)/shard_map/cond
  98.8 1.8 %copy-start.5 = (f32[2,2,2,8,128]{4,3,2,1,0:T(8,128)}, f32[2,2,2,8,128]{4,3,2,1,0:T(8,128)S(1)}, u32[]{:S(2)}) copy-start(f32[2,2,2,8,128]{4,3,2,1,0:T(8,128)S(1)} %collective-permute-done.1.second_ref) | copy-start | bytes 98308 | tf_op jit(solution)/shard_map/cond
  100.6 38.7 %all-to-all-start.3 = ((f32[4,8,22,8,128]{4,3,2,1,0:T(8,128)}), f32[4,8,22,8,128]{4,3,2,1,0:T(8,128)S(1)}, u32[]{:S(2)}, u32[]{:S(2)}) async-start(f32[4,8,22,8,128]{4,3,2,1,0:T(8,128)} %broadcast_in_dim.2), calls=%async_computation.3 | async-start | bytes 5767168 | tf_op jit(solution)/shard_map/cond/branch_0_fun/all_to_all | solution.py:529
  127.0 7.8 %collective-permute-start.2 = (f32[8,2,2,2,2,8,128]{6,5,4,3,2,1,0:T(8,128)S(1)}, f32[8,2,2,2,2,8,128]{6,5,4,3,2,1,0:T(8,128)}, u32[]{:S(2)}, u32[]{:S(2)}) collective-permute-start(f32[8,2,2,2,2,8,128]{6,5,4,3,2,1,0:T(8,128)S(1)} %bitcast.34), channel_id=1, source_target_pairs={{0,32},{32,0},{64,96},{96,64},{128,160},{160,128},{192,224},{224,1... | collective-permute-start | bytes 1572872 | tf_op jit(solution)/shard_map/cond/branch_0_fun/ppermute | solution.py:533
  165.0 1.3 copy-start.9
